TPU v7x, 32 devices: a whole 2x2x4 slice. The times are simulated.
32 devices in a mesh: segment: 4 (over y, x), dp: 8 (over z, core).
Axes of the slice: x: 2, y: 2, z: 4, core: 2. Of those that a mesh axis runs over, the one named last changes fastest.
Arguments:
- activations: bfloat16 [4, 64, 4, 4, 8, 256], P('segment', 'dp'), may hold values from -6 to 6
- preacts: bfloat16 [4, 64, 4, 4, 8, 256], P('segment', 'dp'), may hold values from -10 to 10
- out_grad: bfloat16 [64, 4, 4, 8, 256], P('dp'), may hold values from -6 to 6
- weights: float32 [4, 256, 27, 256], P('segment', 'dp'), may hold values from -0.078125 to 0.078125
- momentum: float32 [4, 256, 27, 256], P('segment', 'dp'), may hold values from -6 to 6
- noise: float32 [4, 256, 27, 256], P('segment', 'dp'), may hold values from -6 to 6
Outputs:
- new_momentum: float32 [4, 256, 27, 256], P('segment', 'dp')
All inputs are finite; a program needn't handle non-finite values.
Results may differ from a plain program's by a relative error of at most 0.0033.
Values may be sent and summed in bfloat16 or wider, within the bound.
No kernel may reach another device: no remote copies, remote signals or barrier semaphores. Data moves between devices by JAX's collectives and lax.ppermute only.
A program may use at most 192 MiB of HBM per device.

v0:
```python
import math

import jax
import jax.numpy as jnp
from jax import lax
from jax.sharding import PartitionSpec as P


def shifted(x, axis, by):
    size = lax.axis_size(axis)
    pairs = [(i, i + by) for i in range(size) if 0 <= i + by < size]
    return lax.ppermute(x, axis, pairs)


def tap_stack(field, sign):
    batch_n, span_t, span_x, span_y, channels = field.shape
    padded = jnp.pad(field, ((0, 0), (1, 1), (1, 1), (1, 1), (0, 0)))
    views = []
    for along_t in (-1, 0, 1):
        for along_x in (-1, 0, 1):
            for along_y in (-1, 0, 1):
                start_t = 1 + sign * along_t
                start_x = 1 + sign * along_x
                start_y = 1 + sign * along_y
                views.append(
                    padded[
                        :,
                        start_t : start_t + span_t,
                        start_x : start_x + span_x,
                        start_y : start_y + span_y,
                        :,
                    ]
                )
    return jnp.stack(views, axis=4).reshape(batch_n * span_t * span_x * span_y, 27, channels)


def shards(activations, preacts, out_grad, weights, momentum, noise):
    segments = lax.axis_size("segment")
    devices_dp = lax.axis_size("dp")
    segment_id = lax.axis_index("segment")
    kernel = lax.all_gather(weights.astype(jnp.bfloat16), "dp", axis=1, tiled=True)[0]
    inputs = activations[0]
    pres = preacts[0]
    micro, span_t, span_x, span_y, channels = inputs.shape
    cells = span_t * span_x * span_y
    is_last = segment_id == segments - 1
    total_init = jnp.zeros((channels, 27, channels), jnp.float32)
    stored_init = jnp.zeros((1,), jnp.bfloat16)
    incoming_init = jnp.zeros(inputs.shape[1:], jnp.bfloat16)

    def step_fn(step, carry):
        incoming, total, stored = carry
        index = step - (segments - 1 - segment_id)
        valid = jnp.logical_and(index >= 0, index < micro)
        clipped = jnp.clip(index, 0, micro - 1)
        given = lax.dynamic_index_in_dim(out_grad, clipped, 0, keepdims=False)
        upstream = jnp.where(is_last, given, incoming)
        pre = lax.dynamic_index_in_dim(pres, clipped, 0, keepdims=False).astype(jnp.float32)
        sig = jax.nn.sigmoid(pre)
        up_wide = upstream.astype(jnp.float32)
        grad_pre = (up_wide * sig * (1.0 + pre * (1.0 - sig)) * valid.astype(jnp.float32)).astype(
            jnp.bfloat16
        )
        pre_cols = tap_stack(grad_pre[None], -1)
        back = jnp.einsum("nto,cto->nc", pre_cols, kernel, preferred_element_type=jnp.float32)
        passed = (up_wide + back.reshape(upstream.shape)).astype(jnp.bfloat16)
        in_cols = tap_stack(lax.dynamic_index_in_dim(inputs, clipped, 0, keepdims=True), 1)
        total = total + jnp.einsum(
            "ntc,no->cto",
            in_cols,
            grad_pre.reshape(cells, channels),
            preferred_element_type=jnp.float32,
        )
        incoming = shifted(passed, "segment", -1)
        return (incoming, total, stored)

    carry = lax.fori_loop(
        0, micro + segments - 1, step_fn, (incoming_init, total_init, stored_init)
    )
    total = carry[1]
    stored = carry[2]
    owned = lax.psum_scatter(total, "dp", scatter_dimension=0, tiled=True)
    rate = 1.0 / math.sqrt(devices_dp * micro * cells)
    updated = 0.9 * momentum[0] - rate * owned + 0.3 * noise[0]
    return updated[None]


def solution(mesh):
    placed = (
        P("segment", "dp", None, None, None, None),
        P("segment", "dp", None, None, None, None),
        P("dp", None, None, None, None),
        P("segment", "dp", None, None),
        P("segment", "dp", None, None),
        P("segment", "dp", None, None),
    )
    return jax.shard_map(
        shards,
        mesh=mesh,
        in_specs=placed,
        out_specs=P("segment", "dp", None, None),
        check_vma=False,
    )
```

profile of v0, /device:TPU:0, one launch (start us, length us, event | category | flops | bytes accessed | tf_op | source)
XLA Modules:
  0.0 318.9 jit_solution(7608822403578652086)
XLA Ops:
  6.5 2.0 convert_element_type.65
  8.6 44.6 %all-gather.2.cloned.1.call-done = bf16[1,256,27,256]{3,1,2,0:T(8,128)(2,1)} async-done(((bf16[1,32,27,256]{3,1,2,0:T(8,128)(2,1)}), bf16[1,256,27,256]{3,1,2,0:T(8,128)(2,1)}) %all-gather.2.cloned.1.call-update) | async-done | bytes 3538960 | tf_op jit(solution)/shard_map/all_gather | solution.py:41
  53.2 165.2 %while.18 = (s32[]{:T(128)}, bf16[4,4,8,256]{3,2,1,0:T(8,128)(2,1)S(1)}, f32[256,27,256]{0,2,1:T(8,128)}, pred[]{:T(512)}, s32[]{:T(128)}, /*index=5*/bf16[8,4,4...) while((s32[]{:T(128)}, ...), condition=%wide.region_1.2_spmd.clone, body=%wide.region_0.1_spmd.clone.sunk | while | flops 910065664 | bytes 47317272 | solution.py:77
  54.7 1.6 copy-done.2
  61.2 4.0 %bitcast_add_fusion.3 = f32[256,27,256]{0,2,1:T(8,128)} fusion(f32[256,27,256]{0,2,1:T(8,128)} %get-tuple-element.502, pred[]{:T(512)S(6)} %compare.5, bf16[128,256,1]{1,0,2:T(8,128)(2,1)S(1)} %bitcast.227, bf16[128,27,256]{2,0,1:T(8,128)(2,1)S(1)} %constant_dynamic-update-slice_fusion.161), kind=kOutput, calls=%fused_computation.clone.1 | convolution fusion | flops 456523776 | bytes 15990785 | tf_op jit(solution)/shard_map/while/body/eval_jaxpr/ntc,no->cto/dot_general | solution.py:68
  73.3 7.0 %bitcast_add_fusion.3 = f32[256,27,256]{0,2,1:T(8,128)} fusion(f32[256,27,256]{0,2,1:T(8,128)} %get-tuple-element.502, pred[]{:T(512)S(6)} %compare.5, bf16[128,256,1]{1,0,2:T(8,128)(2,1)S(1)} %bitcast.227, bf16[128,27,256]{2,0,1:T(8,128)(2,1)S(1)} %constant_dynamic-update-slice_fusion.161), kind=kOutput, calls=%fused_computation.clone.1 | convolution fusion | flops 456523776 | bytes 15990785 | tf_op jit(solution)/shard_map/while/body/eval_jaxpr/ntc,no->cto/dot_general | solution.py:68
  88.3 7.0 %bitcast_add_fusion.3 = f32[256,27,256]{0,2,1:T(8,128)} fusion(f32[256,27,256]{0,2,1:T(8,128)} %get-tuple-element.502, pred[]{:T(512)S(6)} %compare.5, bf16[128,256,1]{1,0,2:T(8,128)(2,1)S(1)} %bitcast.227, bf16[128,27,256]{2,0,1:T(8,128)(2,1)S(1)} %constant_dynamic-update-slice_fusion.161), kind=kOutput, calls=%fused_computation.clone.1 | convolution fusion | flops 456523776 | bytes 15990785 | tf_op jit(solution)/shard_map/while/body/eval_jaxpr/ntc,no->cto/dot_general | solution.py:68
  103.4 7.0 %bitcast_add_fusion.3 = f32[256,27,256]{0,2,1:T(8,128)} fusion(f32[256,27,256]{0,2,1:T(8,128)} %get-tuple-element.502, pred[]{:T(512)S(6)} %compare.5, bf16[128,256,1]{1,0,2:T(8,128)(2,1)S(1)} %bitcast.227, bf16[128,27,256]{2,0,1:T(8,128)(2,1)S(1)} %constant_dynamic-update-slice_fusion.161), kind=kOutput, calls=%fused_computation.clone.1 | convolution fusion | flops 456523776 | bytes 15990785 | tf_op jit(solution)/shard_map/while/body/eval_jaxpr/ntc,no->cto/dot_general | solution.py:68
  111.9 1.6 copy-done.2
  118.4 7.0 %bitcast_add_fusion.3 = f32[256,27,256]{0,2,1:T(8,128)} fusion(f32[256,27,256]{0,2,1:T(8,128)} %get-tuple-element.502, pred[]{:T(512)S(6)} %compare.5, bf16[128,256,1]{1,0,2:T(8,128)(2,1)S(1)} %bitcast.227, bf16[128,27,256]{2,0,1:T(8,128)(2,1)S(1)} %constant_dynamic-update-slice_fusion.161), kind=kOutput, calls=%fused_computation.clone.1 | convolution fusion | flops 456523776 | bytes 15990785 | tf_op jit(solution)/shard_map/while/body/eval_jaxpr/ntc,no->cto/dot_general | solution.py:68
  127.0 1.6 copy-done.2
  133.5 7.0 %bitcast_add_fusion.3 = f32[256,27,256]{0,2,1:T(8,128)} fusion(f32[256,27,256]{0,2,1:T(8,128)} %get-tuple-element.502, pred[]{:T(512)S(6)} %compare.5, bf16[128,256,1]{1,0,2:T(8,128)(2,1)S(1)} %bitcast.227, bf16[128,27,256]{2,0,1:T(8,128)(2,1)S(1)} %constant_dynamic-update-slice_fusion.161), kind=kOutput, calls=%fused_computation.clone.1 | convolution fusion | flops 456523776 | bytes 15990785 | tf_op jit(solution)/shard_map/while/body/eval_jaxpr/ntc,no->cto/dot_general | solution.py:68
  142.0 1.6 copy-done.2
  148.5 7.0 %bitcast_add_fusion.3 = f32[256,27,256]{0,2,1:T(8,128)} fusion(f32[256,27,256]{0,2,1:T(8,128)} %get-tuple-element.502, pred[]{:T(512)S(6)} %compare.5, bf16[128,256,1]{1,0,2:T(8,128)(2,1)S(1)} %bitcast.227, bf16[128,27,256]{2,0,1:T(8,128)(2,1)S(1)} %constant_dynamic-update-slice_fusion.161), kind=kOutput, calls=%fused_computation.clone.1 | convolution fusion | flops 456523776 | bytes 15990785 | tf_op jit(solution)/shard_map/while/body/eval_jaxpr/ntc,no->cto/dot_general | solution.py:68
  157.3 1.6 copy-done.2
  163.8 7.0 %bitcast_add_fusion.3 = f32[256,27,256]{0,2,1:T(8,128)} fusion(f32[256,27,256]{0,2,1:T(8,128)} %get-tuple-element.502, pred[]{:T(512)S(6)} %compare.5, bf16[128,256,1]{1,0,2:T(8,128)(2,1)S(1)} %bitcast.227, bf16[128,27,256]{2,0,1:T(8,128)(2,1)S(1)} %constant_dynamic-update-slice_fusion.161), kind=kOutput, calls=%fused_computation.clone.1 | convolution fusion | flops 456523776 | bytes 15990785 | tf_op jit(solution)/shard_map/while/body/eval_jaxpr/ntc,no->cto/dot_general | solution.py:68
  172.9 1.6 copy-done.2
  179.4 7.0 %bitcast_add_fusion.3 = f32[256,27,256]{0,2,1:T(8,128)} fusion(f32[256,27,256]{0,2,1:T(8,128)} %get-tuple-element.502, pred[]{:T(512)S(6)} %compare.5, bf16[128,256,1]{1,0,2:T(8,128)(2,1)S(1)} %bitcast.227, bf16[128,27,256]{2,0,1:T(8,128)(2,1)S(1)} %constant_dynamic-update-slice_fusion.161), kind=kOutput, calls=%fused_computation.clone.1 | convolution fusion | flops 456523776 | bytes 15990785 | tf_op jit(solution)/shard_map/while/body/eval_jaxpr/ntc,no->cto/dot_general | solution.py:68
  188.6 1.6 copy-done.2
  195.1 7.0 %bitcast_add_fusion.3 = f32[256,27,256]{0,2,1:T(8,128)} fusion(f32[256,27,256]{0,2,1:T(8,128)} %get-tuple-element.502, pred[]{:T(512)S(6)} %compare.5, bf16[128,256,1]{1,0,2:T(8,128)(2,1)S(1)} %bitcast.227, bf16[128,27,256]{2,0,1:T(8,128)(2,1)S(1)} %constant_dynamic-update-slice_fusion.161), kind=kOutput, calls=%fused_computation.clone.1 | convolution fusion | flops 456523776 | bytes 15990785 | tf_op jit(solution)/shard_map/while/body/eval_jaxpr/ntc,no->cto/dot_general | solution.py:68
  210.8 7.0 %bitcast_add_fusion.3 = f32[256,27,256]{0,2,1:T(8,128)} fusion(f32[256,27,256]{0,2,1:T(8,128)} %get-tuple-element.502, pred[]{:T(512)S(6)} %compare.5, bf16[128,256,1]{1,0,2:T(8,128)(2,1)S(1)} %bitcast.227, bf16[128,27,256]{2,0,1:T(8,128)(2,1)S(1)} %constant_dynamic-update-slice_fusion.161), kind=kOutput, calls=%fused_computation.clone.1 | convolution fusion | flops 456523776 | bytes 15990785 | tf_op jit(solution)/shard_map/while/body/eval_jaxpr/ntc,no->cto/dot_general | solution.py:68
  218.5 8.0 %copy.11 = f32[256,27,256]{2,0,1:T(8,128)} copy(f32[256,27,256]{0,2,1:T(8,128)} %get-tuple-element.227) | data formatting | bytes 14155776 | tf_op jit(solution)/shard_map/while | solution.py:77
  226.5 83.2 %reduce-scatter.2.cloned.1.call-done = f32[32,27,256]{2,0,1:T(8,128)} async-done(((f32[256,27,256]{2,0,1:T(8,128)}), f32[32,27,256]{2,0,1:T(8,128)}) %reduce-scatter.2.cloned.1.call-update) | async-done | bytes 884752 | tf_op jit(solution)/shard_map/reduce_scatter | solution.py:82
  309.7 2.4 fusion.11
  (729 shorter events, 74.5 us)
Async XLA Ops:
  6.5 46.7 %all-gather.2.cloned.1.call-start = ((), (), s32[]{:S(2)}) async-start(), calls=%async_computation.1 | async-start | bytes 3981312 | tf_op jit(solution)/shard_map/all_gather | solution.py:41
  8.6 301.1 %reduce-scatter.2.cloned.1.call-start = ((), (), s32[]{:S(2)}) async-start(), calls=%async_computation.2 | async-start | bytes 7962624 | tf_op jit(solution)/shard_map/reduce_scatter | solution.py:82
  54.3 2.0 copy-start.2
  58.5 6.8 %collective-permute-start = (bf16[4,4,8,256]{3,2,1,0:T(8,128)(2,1)S(1)}, bf16[4,4,8,256]{3,2,1,0:T(8,128)(2,1)S(1)}, u32[]{:S(2)}, u32[]{:S(2)}) collective-permute-start(bf16[4,4,8,256]{3,2,1,0:T(8,128)(2,1)S(1)} %fusion.27), channel_id=1, source_target_pairs={{8,0},{16,8},{24,16},{9,1},{17,9},{25,17},{10,2},{18,10},{26,18},{... | collective-permute-start | bytes 196616 | tf_op jit(solution)/shard_map/while/body/eval_jaxpr/ppermute | solution.py:12
  66.4 2.0 copy-start.2
  70.6 9.8 %collective-permute-start = (bf16[4,4,8,256]{3,2,1,0:T(8,128)(2,1)S(1)}, bf16[4,4,8,256]{3,2,1,0:T(8,128)(2,1)S(1)}, u32[]{:S(2)}, u32[]{:S(2)}) collective-permute-start(bf16[4,4,8,256]{3,2,1,0:T(8,128)(2,1)S(1)} %fusion.27), channel_id=1, source_target_pairs={{8,0},{16,8},{24,16},{9,1},{17,9},{25,17},{10,2},{18,10},{26,18},{... | collective-permute-start | bytes 196616 | tf_op jit(solution)/shard_map/while/body/eval_jaxpr/ppermute | solution.py:12
  81.4 2.0 copy-start.2
  85.6 9.8 %collective-permute-start = (bf16[4,4,8,256]{3,2,1,0:T(8,128)(2,1)S(1)}, bf16[4,4,8,256]{3,2,1,0:T(8,128)(2,1)S(1)}, u32[]{:S(2)}, u32[]{:S(2)}) collective-permute-start(bf16[4,4,8,256]{3,2,1,0:T(8,128)(2,1)S(1)} %fusion.27), channel_id=1, source_target_pairs={{8,0},{16,8},{24,16},{9,1},{17,9},{25,17},{10,2},{18,10},{26,18},{... | collective-permute-start | bytes 196616 | tf_op jit(solution)/shard_map/while/body/eval_jaxpr/ppermute | solution.py:12
  100.7 9.8 %collective-permute-start = (bf16[4,4,8,256]{3,2,1,0:T(8,128)(2,1)S(1)}, bf16[4,4,8,256]{3,2,1,0:T(8,128)(2,1)S(1)}, u32[]{:S(2)}, u32[]{:S(2)}) collective-permute-start(bf16[4,4,8,256]{3,2,1,0:T(8,128)(2,1)S(1)} %fusion.27), channel_id=1, source_target_pairs={{8,0},{16,8},{24,16},{9,1},{17,9},{25,17},{10,2},{18,10},{26,18},{... | collective-permute-start | bytes 196616 | tf_op jit(solution)/shard_map/while/body/eval_jaxpr/ppermute | solution.py:12
  111.5 2.0 copy-start.2
  115.7 9.8 %collective-permute-start = (bf16[4,4,8,256]{3,2,1,0:T(8,128)(2,1)S(1)}, bf16[4,4,8,256]{3,2,1,0:T(8,128)(2,1)S(1)}, u32[]{:S(2)}, u32[]{:S(2)}) collective-permute-start(bf16[4,4,8,256]{3,2,1,0:T(8,128)(2,1)S(1)} %fusion.27), channel_id=1, source_target_pairs={{8,0},{16,8},{24,16},{9,1},{17,9},{25,17},{10,2},{18,10},{26,18},{... | collective-permute-start | bytes 196616 | tf_op jit(solution)/shard_map/while/body/eval_jaxpr/ppermute | solution.py:12
  126.6 2.0 copy-start.2
  130.8 9.8 %collective-permute-start = (bf16[4,4,8,256]{3,2,1,0:T(8,128)(2,1)S(1)}, bf16[4,4,8,256]{3,2,1,0:T(8,128)(2,1)S(1)}, u32[]{:S(2)}, u32[]{:S(2)}) collective-permute-start(bf16[4,4,8,256]{3,2,1,0:T(8,128)(2,1)S(1)} %fusion.27), channel_id=1, source_target_pairs={{8,0},{16,8},{24,16},{9,1},{17,9},{25,17},{10,2},{18,10},{26,18},{... | collective-permute-start | bytes 196616 | tf_op jit(solution)/shard_map/while/body/eval_jaxpr/ppermute | solution.py:12
  141.6 2.0 copy-start.2
  145.8 9.9 %collective-permute-start = (bf16[4,4,8,256]{3,2,1,0:T(8,128)(2,1)S(1)}, bf16[4,4,8,256]{3,2,1,0:T(8,128)(2,1)S(1)}, u32[]{:S(2)}, u32[]{:S(2)}) collective-permute-start(bf16[4,4,8,256]{3,2,1,0:T(8,128)(2,1)S(1)} %fusion.27), channel_id=1, source_target_pairs={{8,0},{16,8},{24,16},{9,1},{17,9},{25,17},{10,2},{18,10},{26,18},{... | collective-permute-start | bytes 196616 | tf_op jit(solution)/shard_map/while/body/eval_jaxpr/ppermute | solution.py:12
  156.9 2.0 copy-start.2
  161.0 10.4 %collective-permute-start = (bf16[4,4,8,256]{3,2,1,0:T(8,128)(2,1)S(1)}, bf16[4,4,8,256]{3,2,1,0:T(8,128)(2,1)S(1)}, u32[]{:S(2)}, u32[]{:S(2)}) collective-permute-start(bf16[4,4,8,256]{3,2,1,0:T(8,128)(2,1)S(1)} %fusion.27), channel_id=1, source_target_pairs={{8,0},{16,8},{24,16},{9,1},{17,9},{25,17},{10,2},{18,10},{26,18},{... | collective-permute-start | bytes 196616 | tf_op jit(solution)/shard_map/while/body/eval_jaxpr/ppermute | solution.py:12
  172.5 2.0 copy-start.2
  176.7 10.4 %collective-permute-start = (bf16[4,4,8,256]{3,2,1,0:T(8,128)(2,1)S(1)}, bf16[4,4,8,256]{3,2,1,0:T(8,128)(2,1)S(1)}, u32[]{:S(2)}, u32[]{:S(2)}) collective-permute-start(bf16[4,4,8,256]{3,2,1,0:T(8,128)(2,1)S(1)} %fusion.27), channel_id=1, source_target_pairs={{8,0},{16,8},{24,16},{9,1},{17,9},{25,17},{10,2},{18,10},{26,18},{... | collective-permute-start | bytes 196616 | tf_op jit(solution)/shard_map/while/body/eval_jaxpr/ppermute | solution.py:12
  188.2 2.0 copy-start.2
  192.4 10.4 %collective-permute-start = (bf16[4,4,8,256]{3,2,1,0:T(8,128)(2,1)S(1)}, bf16[4,4,8,256]{3,2,1,0:T(8,128)(2,1)S(1)}, u32[]{:S(2)}, u32[]{:S(2)}) collective-permute-start(bf16[4,4,8,256]{3,2,1,0:T(8,128)(2,1)S(1)} %fusion.27), channel_id=1, source_target_pairs={{8,0},{16,8},{24,16},{9,1},{17,9},{25,17},{10,2},{18,10},{26,18},{... | collective-permute-start | bytes 196616 | tf_op jit(solution)/shard_map/while/body/eval_jaxpr/ppermute | solution.py:12
  208.1 10.4 %collective-permute-start = (bf16[4,4,8,256]{3,2,1,0:T(8,128)(2,1)S(1)}, bf16[4,4,8,256]{3,2,1,0:T(8,128)(2,1)S(1)}, u32[]{:S(2)}, u32[]{:S(2)}) collective-permute-start(bf16[4,4,8,256]{3,2,1,0:T(8,128)(2,1)S(1)} %fusion.27), channel_id=1, source_target_pairs={{8,0},{16,8},{24,16},{9,1},{17,9},{25,17},{10,2},{18,10},{26,18},{... | collective-permute-start | bytes 196616 | tf_op jit(solution)/shard_map/while/body/eval_jaxpr/ppermute | solution.py:12
  226.4 83.2 %copy-start = (f32[1,32,27,256]{3,1,2,0:T(8,128)S(1)}, f32[1,32,27,256]{3,1,2,0:T(8,128)}, u32[]{:S(2)}) copy-start(f32[1,32,27,256]{3,1,2,0:T(8,128)} %param.13) | copy-start | bytes 2654212
  226.4 83.2 %copy-start.1 = (f32[1,32,27,256]{3,1,2,0:T(8,128)S(1)}, f32[1,32,27,256]{3,1,2,0:T(8,128)}, u32[]{:S(2)}) copy-start(f32[1,32,27,256]{3,1,2,0:T(8,128)} %param.12) | copy-start | bytes 2654212
  (2 other events, 4.0 us)
Sparse Core Ops, SparseCore 0:
  9.0 44.1 all-gather.1
  226.6 83.0 reduce-scatter.1
where the time goes:
time: 322 us; the launch traced here: 319 us
  waiting for transfers between devices  131 us (41%)
  matrix products  88.6 us (28%)
  local copies, waits for them, and re-layouts  42.5 us (13%)
  other arithmetic  24.3 us (8%)
  starting transfers between devices  14.3 us (4%)
  between operations  13.4 us (4%)
  loops' own time  5.33 us (2%)
    reduce_scatter x1, waiting for transfers between devices, shards(): owned = lax.psum_scatter(total, 'dp', scatter_dimension=0, tiled=True)  83.2 us
    dot_general x11, matrix products, step_fn(): jnp.einsum('ntc,no->cto', in_cols, grad_pre.reshape(cells, channels), pre...  74.3 us
    all_gather x1, waiting for transfers between devices, shards(): lax.all_gather(weights.astype(jnp.bfloat16), 'dp', axis=1, tiled=True)[0]  44.6 us
    while x594, local copies, waits for them, and re-layouts  21.5 us
    dot_general x11, matrix products, step_fn(): jnp.einsum('nto,cto->nc', pre_cols, kernel, preferred_element_type=jnp.fl...  14.3 us
    ppermute x11, starting transfers between devices, shifted(): return lax.ppermute(x, axis, pairs)  14.2 us
    convert_element_type x11, other arithmetic, step_fn(): (up_wide * sig * (1.0 + pre * (1.0 - sig)) * valid.astype(jnp.float32)).a...  10.4 us
    convert_element_type x11, other arithmetic, step_fn(): passed = (up_wide + back.reshape(upstream.shape)).astype(jnp.bfloat16)  9.54 us
  transfers between devices with their start and end apart: 13, of which 7 were waited for; matrix products, arithmetic and copies ran while one was open for 27% of the time, Pallas kernels for 0%

commit v1 on v0

v1 whole, which is shorter than its diff:
```python
import functools
import math

import jax
import jax.numpy as jnp
from jax import lax
from jax.experimental import pallas as pl
from jax.experimental.pallas import tpu as pltpu
from jax.sharding import PartitionSpec as P

BF16 = jnp.bfloat16
F32 = jnp.float32
VMEM_BYTES = 48 * 1024 * 1024


def shifted(x, axis, by):
    size = lax.axis_size(axis)
    pairs = [(i, i + by) for i in range(size) if 0 <= i + by < size]
    return lax.ppermute(x, axis, pairs)


def swapped(x, axis, mask):
    return lax.ppermute(x, axis, [(i, i ^ mask) for i in range(lax.axis_size(axis))])


def tap_stack(field, sign):
    batch_n, span_t, span_x, span_y, channels = field.shape
    padded = jnp.pad(field, ((0, 0), (1, 1), (1, 1), (1, 1), (0, 0)))
    views = []
    for along_t in (-1, 0, 1):
        for along_x in (-1, 0, 1):
            for along_y in (-1, 0, 1):
                start_t = 1 + sign * along_t
                start_x = 1 + sign * along_x
                start_y = 1 + sign * along_y
                views.append(
                    padded[
                        :,
                        start_t : start_t + span_t,
                        start_x : start_x + span_x,
                        start_y : start_y + span_y,
                        :,
                    ]
                )
    return jnp.stack(views, axis=4).reshape(batch_n * span_t * span_x * span_y, 27, channels)


def general_shards(activations, preacts, out_grad, weights, momentum, noise):
    segments = lax.axis_size("segment")
    devices_dp = lax.axis_size("dp")
    segment_id = lax.axis_index("segment")
    kernel = lax.all_gather(weights.astype(BF16), "dp", axis=1, tiled=True)[0]
    inputs = activations[0]
    pres = preacts[0]
    micro, span_t, span_x, span_y, channels = inputs.shape
    cells = span_t * span_x * span_y
    is_last = segment_id == segments - 1

    def step_fn(step, carry):
        incoming, total = carry
        index = step - (segments - 1 - segment_id)
        valid = jnp.logical_and(index >= 0, index < micro)
        clipped = jnp.clip(index, 0, micro - 1)
        given = lax.dynamic_index_in_dim(out_grad, clipped, 0, keepdims=False)
        upstream = jnp.where(is_last, given, incoming)
        pre = lax.dynamic_index_in_dim(pres, clipped, 0, keepdims=False).astype(F32)
        sig = jax.nn.sigmoid(pre)
        up_wide = upstream.astype(F32)
        grad_pre = (up_wide * sig * (1.0 + pre * (1.0 - sig)) * valid.astype(F32)).astype(BF16)
        pre_cols = tap_stack(grad_pre[None], -1)
        back = jnp.einsum("nto,cto->nc", pre_cols, kernel, preferred_element_type=F32)
        passed = (up_wide + back.reshape(upstream.shape)).astype(BF16)
        in_cols = tap_stack(lax.dynamic_index_in_dim(inputs, clipped, 0, keepdims=True), 1)
        total = total + jnp.einsum(
            "ntc,no->cto", in_cols, grad_pre.reshape(cells, channels), preferred_element_type=F32
        )
        return shifted(passed, "segment", -1), total

    init = (jnp.zeros(inputs.shape[1:], BF16), jnp.zeros((channels, 27, channels), F32))
    total = lax.fori_loop(0, micro + segments - 1, step_fn, init)[1]
    owned = lax.psum_scatter(total, "dp", scatter_dimension=0, tiled=True)
    rate = 1.0 / math.sqrt(devices_dp * micro * cells)
    return (0.9 * momentum[0] - rate * owned + 0.3 * noise[0])[None]


def iota(shape, dim):
    return lax.broadcasted_iota(jnp.int32, shape, dim)


def log2(n):
    return n.bit_length() - 1


def channel_of(place, quarter, per, sub):
    return (place >> log2(sub)) * per + quarter * sub + (place & (sub - 1))


def dot(a, b):
    return jnp.dot(a, b, preferred_element_type=F32)


def call(body, out_shape, args, flops=0, scratch=()):
    bytes_accessed = sum(x.size * x.dtype.itemsize for x in args)
    return pl.pallas_call(
        body,
        out_shape=out_shape,
        in_specs=[pl.BlockSpec(memory_space=pltpu.SMEM)]
        + [pl.BlockSpec(memory_space=pltpu.VMEM)] * (len(args) - 1),
        out_specs=jax.tree.map(lambda _: pl.BlockSpec(memory_space=pltpu.VMEM), out_shape),
        scratch_shapes=list(scratch),
        compiler_params=pltpu.CompilerParams(vmem_limit_bytes=VMEM_BYTES),
        cost_estimate=pl.CostEstimate(
            flops=flops, bytes_accessed=bytes_accessed, transcendentals=0
        ),
    )(*args)


def weights_body(per, sub, ids, w_ref, *out_refs):
    channels = w_ref.shape[2]
    quarter_n = channels // 4
    s = ids[0]
    for m, out_ref in enumerate(out_refs):
        target = s ^ m
        rows = [
            w_ref[pl.ds(target * sub, sub), t, :] for t in range(27)
        ]
        stacked = jnp.concatenate(rows, axis=0).astype(BF16)
        lane = iota((channels, channels), 1)
        place = lane & (quarter_n - 1)
        quarter = (lane >> log2(quarter_n)) ^ target
        order = iota((channels, channels), 0) == channel_of(place, quarter, per, sub)
        moved = dot(stacked, order.astype(BF16))
        for bc in range(9):
            part = [moved[(a * 9 + bc) * sub : (a * 9 + bc + 1) * sub] for a in range(3)]
            out_ref[:, bc * channels : (bc + 1) * channels] = jnp.concatenate(part, axis=0).astype(
                BF16
            )


def quarters_body(per, sub, ids, pre_ref, up_ref, up_out, *out_refs):
    rows, channels = pre_ref.shape
    quarter_n = channels // 4
    half = rows // 2
    s = ids[0]
    shape = (channels, 8 * quarter_n)
    lane = iota(shape, 1)
    place = lane & (quarter_n - 1)
    quarter = (lane >> log2(2 * quarter_n)) ^ s
    hit = iota(shape, 0) == channel_of(place, quarter, per, sub)
    low = (lane & (2 * quarter_n - 1)) < quarter_n
    first = jnp.logical_and(hit, low).astype(BF16)
    second = jnp.logical_and(hit, jnp.logical_not(low)).astype(BF16)
    packed = dot(pre_ref[:half], first) + dot(pre_ref[half:], second)
    for m, out_ref in enumerate(out_refs):
        out_ref[...] = packed[:, m * 2 * quarter_n : (m + 1) * 2 * quarter_n].astype(BF16)
    width = 2 * quarter_n
    up_out[...] = (dot(up_ref[:half], first[:, :width]) + dot(up_ref[half:], second[:, :width])).astype(BF16)


def silu_back(up_wide, pre):
    pre = pre.astype(F32)
    sig = jax.nn.sigmoid(pre)
    return (up_wide * sig * (1.0 + pre * (1.0 - sig))).astype(BF16)


def shifts(field, span):
    span_x, span_y = span
    rows, lanes = field.shape
    y = iota((rows, lanes), 0) & (span_y - 1)
    along_y = (
        jnp.where(y == span_y - 1, 0.0, pltpu.roll(field, rows - 1, 0)),
        field,
        jnp.where(y == 0, 0.0, pltpu.roll(field, 1, 0)),
    )
    out = []
    for b in (-1, 0, 1):
        for c in (-1, 0, 1):
            part = along_y[c + 1].reshape(rows // (span_x * span_y), span_x, span_y, lanes)
            edge = jnp.zeros_like(part[:, :1])
            if b == 1:
                part = jnp.concatenate([edge, part[:, :-1]], axis=1)
            elif b == -1:
                part = jnp.concatenate([part[:, 1:], edge], axis=1)
            out.append(part.reshape(rows, lanes))
    return out


def back_body(span, n_dp, ids, g0, g1, g2, g3, w_ref, up_ref, pre_ref, up_out, g_out, cols):
    span_t, span_x, span_y = span
    half, width = g0.shape
    quarter_n = width // 2
    channels = 4 * quarter_n
    sub = quarter_n // n_dp
    rows = 2 * half
    plane = span_x * span_y
    d = ids[1]
    shape = (4 * width, 2 * channels)
    src, dst = iota(shape, 0), iota(shape, 1)
    m, h, place = src >> log2(width), (src >> log2(quarter_n)) & 1, src & (quarter_n - 1)
    unpack = (dst == h * channels + m * quarter_n + place).astype(BF16)
    both = dot(jnp.concatenate([g0[...], g1[...], g2[...], g3[...]], axis=1), unpack)
    field = jnp.concatenate([both[:, :channels], both[:, channels:]], axis=0)
    for k, part in enumerate(shifts(field, (span_x, span_y))):
        cols[:, k * channels : (k + 1) * channels] = part.astype(BF16)
    shape = (3 * quarter_n, 3 * quarter_n)
    dst, src = iota(shape, 0), iota(shape, 1)
    a, place = dst >> log2(quarter_n), dst & (quarter_n - 1)
    apart = (place >> log2(sub)) ^ d
    piece = (apart >> 1) + (n_dp // 2) * (apart & 1)
    order = src == piece * (3 * sub) + a * sub + (place & (sub - 1))
    kernel = dot(order.astype(BF16), w_ref[...]).astype(BF16)
    terms = lax.dot_general(
        cols[...], kernel, (((1,), (1,)), ((), ())), preferred_element_type=F32
    )
    back = []
    for a in range(3):
        back.append(
            terms[:, a * quarter_n : (a + 1) * quarter_n].reshape(
                rows // (span_t * plane), span_t, plane, quarter_n
            )
        )
    edge = jnp.zeros_like(back[0][:, :1])
    total = (
        back[1]
        + jnp.concatenate([back[0][:, 1:], edge], axis=1)
        + jnp.concatenate([edge, back[2][:, :-1]], axis=1)
    ).reshape(rows, quarter_n)
    total = jnp.concatenate([total[:half], total[half:]], axis=1)
    passed = (up_ref[...].astype(F32) + total).astype(BF16)
    up_out[...] = passed
    g_out[...] = silu_back(passed.astype(F32), pre_ref[...])


def grads_body(span, n_dp, ids, g_ref, x_ref, keep, give, cols, total):
    span_t, span_x, span_y = span
    half, width = g_ref.shape
    quarter_n = width // 2
    rows, channels = x_ref.shape
    per = channels // n_dp
    plane = span_x * span_y
    crops = rows // (span_t * plane)
    d = ids[1]
    shape = (width, 2 * width)
    src, dst = iota(shape, 0), iota(shape, 1)
    twice = jnp.logical_and(
        (src & (quarter_n - 1)) == (dst & (quarter_n - 1)),
        (src >> log2(quarter_n)) == (dst >> log2(width)),
    ).astype(BF16)
    both = dot(g_ref[...], twice)
    field = jnp.concatenate([both[:, :width], both[:, width:]], axis=0)
    parts = shifts(field, (span_x, span_y))
    left = iota((rows, width), 1) < quarter_n
    for k in range(5):
        other = parts[2 * k + 1] if k < 4 else 0.0
        cols[:, k * width : (k + 1) * width] = jnp.where(left, parts[2 * k], other).astype(BF16)
    inputs = x_ref[...].reshape(crops, span_t, plane, channels)
    taken = cols[...].reshape(crops, span_t, plane, 5 * width)
    for a in (-1, 0, 1):
        x_a = inputs[:, max(a, 0) : span_t + min(a, 0)].reshape(-1, channels)
        g_a = taken[:, max(-a, 0) : span_t + min(-a, 0)].reshape(-1, 5 * width)
        total[(a + 1) * channels : (a + 2) * channels, :] = lax.dot_general(
            x_a, g_a, (((0,), (0,)), ((), ())), preferred_element_type=F32
        )
    for k in range(n_dp // 2):
        for bit, ref in ((0, keep), (1, give)):
            owner = d ^ (2 * k + bit)
            for a in range(3):
                ref[k, a * per : (a + 1) * per, :] = total[
                    pl.ds(pl.multiple_of(a * channels + owner * per, per), per), :
                ].astype(ref.dtype)


def pair_body(ids, keep, other, own, *out_refs):
    own[...] = keep[0] + other[0].astype(F32)
    for k, out_ref in enumerate(out_refs):
        out_ref[...] = (keep[k + 1] + other[k + 1].astype(F32)).astype(BF16)


def sums_body(pieces, ids, *refs):
    ins, outs = refs[: 4 * pieces], refs[4 * pieces :]
    s = ids[0]
    for section in range(4):
        parts = ins[section * pieces : (section + 1) * pieces]
        total = parts[0][...]
        for part in parts[1:]:
            total = total + part[...].astype(F32)
        for m, out_ref in enumerate(outs):
            @pl.when((s ^ m) == section)
            def _(out_ref=out_ref, total=total):
                out_ref[...] = total.astype(BF16)


def update_body(per, sub, rate, ids, f0, f1, f2, f3, momentum, noise, out):
    channels = momentum.shape[2]
    quarter_n = channels // 4
    width = 2 * quarter_n
    s = ids[0]
    shape = (4 * width, 2 * channels)
    src, dst = iota(shape, 0), iota(shape, 1)
    m, h, place = src >> log2(width), (src >> log2(quarter_n)) & 1, src & (quarter_n - 1)
    order = (dst == h * channels + channel_of(place, m ^ s, per, sub)).astype(BF16)
    for k in range(5):
        lanes = slice(k * width, (k + 1) * width)
        grads = dot(jnp.concatenate([f[:, lanes] for f in (f0, f1, f2, f3)], axis=1), order)
        for h in range(2 if k < 4 else 1):
            for a in range(3):
                t = a * 9 + 2 * k + h
                own = grads[a * per : (a + 1) * per, h * channels : (h + 1) * channels]
                out[:, t, :] = 0.9 * momentum[:, t, :] - rate * own + 0.3 * noise[:, t, :]


def pick(index, arrays):
    return lax.select_n(index, *arrays)


def quartered_shards(activations, preacts, out_grad, weights, momentum, noise):
    n_dp = lax.axis_size("dp")
    s = lax.axis_index("segment").astype(jnp.int32)
    d = lax.axis_index("dp").astype(jnp.int32)
    ids = jnp.stack([s, d])
    micro, span_t, span_x, span_y, channels = out_grad.shape
    span = (span_t, span_x, span_y)
    rows = micro * span_t * span_x * span_y
    quarter_n = channels // 4
    width = 2 * quarter_n
    half = rows // 2
    per = channels // n_dp
    sub = per // 4
    chips = n_dp // 2
    inputs = activations.reshape(rows, channels)
    pres = preacts.reshape(rows, channels)
    packed = jax.ShapeDtypeStruct((half, width), BF16)
    taken = 5 * width

    w_parts = call(
        functools.partial(weights_body, per, sub),
        [jax.ShapeDtypeStruct((3 * sub, 9 * channels), BF16)] * 4,
        (ids, weights[0]),
    )
    w_held = [w_parts[0]] + [swapped(w_parts[m], "segment", m) for m in (3, 1, 2)]
    w_held = [w_held[0], w_held[2], w_held[3], w_held[1]]
    up, *p_parts = call(
        functools.partial(quarters_body, per, sub),
        [packed] * 5,
        (ids, pres, out_grad.reshape(rows, channels)),
    )
    p_held = [p_parts[0]] + [swapped(p_parts[m], "segment", m) for m in (3, 1, 2)]
    p_held = [p_held[0], p_held[2], p_held[3], p_held[1]]

    def gathered(section):
        own = pick(s ^ section, w_held)
        pieces = jnp.stack([own] + [swapped(own, "dp", 2 * k) for k in range(1, chips)])
        other = swapped(pieces, "dp", 1)
        return jnp.concatenate([pieces, other], axis=0).reshape(3 * quarter_n, 9 * channels)

    def spread(x):
        far, one, two = (swapped(x, "segment", m) for m in (3, 1, 2))
        return x, one, two, far

    def reduced(section, g):
        keep, give = call(
            functools.partial(grads_body, span, n_dp),
            [
                jax.ShapeDtypeStruct((chips, 3 * per, taken), F32),
                jax.ShapeDtypeStruct((chips, 3 * per, taken), BF16),
            ],
            (ids, g, pick(s ^ section, x_held)),
            scratch=[pltpu.VMEM((rows, taken), BF16), pltpu.VMEM((3 * channels, taken), F32)],
        )
        own, *out = call(
            pair_body,
            [jax.ShapeDtypeStruct((3 * per, taken), F32)]
            + [jax.ShapeDtypeStruct((3 * per, taken), BF16)] * (chips - 1),
            (ids, keep, swapped(give, "dp", 1)),
        )
        return [own] + [swapped(x, "dp", 2 * (k + 1)) for k, x in enumerate(out)]

    kernels = {3: gathered(3)}
    g = silu_back(up.astype(F32), pick(s ^ 3, p_held))
    fields = {3: spread(g)}
    x_held = spread(inputs)
    kernels[2] = gathered(2)
    kernels[1] = gathered(1)
    sums = {}
    for section in (3, 2, 1):
        up, g = call(
            functools.partial(back_body, span, n_dp),
            [packed] * 2,
            (ids, *fields[section], kernels[section], up, pick(s ^ (section - 1), p_held)),
            scratch=[pltpu.VMEM((rows, 9 * channels), BF16)],
        )
        fields[section - 1] = spread(g) if section > 1 else (g,)
        sums[section] = reduced(section, fields[section][0])
    sums[0] = reduced(0, g)
    owned = call(
        functools.partial(sums_body, chips),
        [jax.ShapeDtypeStruct((3 * per, taken), BF16)] * 4,
        (ids, *sums[0], *sums[1], *sums[2], *sums[3]),
    )
    far, one, two = (swapped(owned[m], "segment", m) for m in (3, 1, 2))
    rate = 1.0 / math.sqrt(n_dp * rows)
    return call(
        functools.partial(update_body, per, sub, rate),
        jax.ShapeDtypeStruct(momentum.shape[1:], F32),
        (ids, owned[0], one, two, far, momentum[0], noise[0]),
    )[None]


def solution(mesh):
    placed = (
        P("segment", "dp", None, None, None, None),
        P("segment", "dp", None, None, None, None),
        P("dp", None, None, None, None),
        P("segment", "dp", None, None),
        P("segment", "dp", None, None),
        P("segment", "dp", None, None),
    )

    def shards(activations, preacts, out_grad, weights, momentum, noise):
        channels = weights.shape[-1]
        n_dp = mesh.shape["dp"]
        fits = (
            mesh.shape["segment"] == 4
            and channels % (32 * n_dp) == 0
            and n_dp & (n_dp - 1) == 0
            and out_grad.shape[3] == 8
        )
        plan = quartered_shards if fits else general_shards
        return plan(activations, preacts, out_grad, weights, momentum, noise)

    return jax.shard_map(
        shards,
        mesh=mesh,
        in_specs=placed,
        out_specs=P("segment", "dp", None, None),
        check_vma=False,
    )
```

time: 322 us -> 172 us (0.53)
  matrix products: 88.6 us -> 0 us
  waiting for transfers between devices: 131 us -> 60.8 us
  starting transfers between devices: 14.3 us -> 78.4 us
  local copies, waits for them, and re-layouts: 42.5 us -> 4.39 us
  Pallas kernels: 0 us -> 26.8 us
  other arithmetic: 24.3 us -> 0.9 us
  between operations: 13.4 us -> 0.34 us
  loops' own time: 5.33 us -> 0 us
    dot_general x22 -> x0, matrix products: 88.6 us -> none  [the longest x11 74.3 us: step_fn(): jnp.einsum('ntc,no->cto', in_cols, grad_pre.reshape(cells, channels), pre...]
    reduce_scatter x1 -> x0, waiting for transfers between devices: 83.2 us -> none  [shards(): owned = lax.psum_scatter(total, 'dp', scatter_dimension=0, tiled=True)]
    ppermute x11 -> x49, starting transfers between devices: 14.2 us -> 78.4 us  [swapped(): lax.ppermute(x, axis, [(i, i ^ mask) for i in range(lax.axis_size(axis))])]
    ppermute x11 -> x49, waiting for transfers between devices: 2.7 us -> 60.8 us  [swapped(): lax.ppermute(x, axis, [(i, i ^ mask) for i in range(lax.axis_size(axis))])]
    all_gather x1 -> x0, waiting for transfers between devices: 44.6 us -> none  [shards(): lax.all_gather(weights.astype(jnp.bfloat16), 'dp', axis=1, tiled=True)[0]]
    while x595 -> x0, local copies, waits for them, and re-layouts: 29.5 us -> none
    pallas_call x0 -> x15, Pallas kernels: none -> 26.8 us  [call(): pl.pallas_call(body, out_shape=out_shape, in_specs=[pl.BlockSpec(memory_s...]
    convert_element_type x23 -> x1, other arithmetic: 21.9 us -> 0.17 us  [silu_back(): return (up_wide * sig * (1.0 + pre * (1.0 - sig))).astype(BF16)]
  transfers between devices with their start and end apart: 13 -> 49, of which waited for: 7 -> 22; matrix products, arithmetic and copies ran while one was open for 27% -> 1% of each run, Pallas kernels for 0% -> 13%
where the time goes in v1:
time: 172 us
  starting transfers between devices  78.4 us (46%)
  waiting for transfers between devices  60.8 us (35%)
  Pallas kernels  26.8 us (16%)
  local copies, waits for them, and re-layouts  4.39 us (3%)
    ppermute x49, starting transfers between devices, swapped(): lax.ppermute(x, axis, [(i, i ^ mask) for i in range(lax.axis_size(axis))])  78.4 us
    ppermute x49, waiting for transfers between devices, swapped(): lax.ppermute(x, axis, [(i, i ^ mask) for i in range(lax.axis_size(axis))])  60.8 us
    pallas_call x15, Pallas kernels, call(): pl.pallas_call(body, out_shape=out_shape, in_specs=[pl.BlockSpec(memory_s...  26.8 us
  transfers between devices with their start and end apart: 49, of which 22 were waited for; matrix products, arithmetic and copies ran while one was open for 1% of the time, Pallas kernels for 13%

profile of v1, /device:TPU:0, one launch (start us, length us, event | category | flops | bytes accessed | tf_op | source)
XLA Modules:
  0.0 171.6 jit_solution(1569670263147219092)
XLA Ops:
  2.9 3.0 %collective-permute-start.7 = (bf16[24,2304]{1,0:T(8,128)(2,1)S(1)}, bf16[24,2304]{1,0:T(8,128)(2,1)S(1)}, u32[]{:S(2)}, u32[]{:S(2)}) collective-permute-start(bf16[24,2304]{1,0:T(8,128)(2,1)S(1)} %get-tuple-element.54), channel_id=1, source_target_pairs={{0,16},{8,24},{16,0},{24,8},{1,17},{9,25},{17,1},{25,9},{2,18},{10... | collective-permute-start | bytes 331784 | tf_op jit(solution)/shard_map/ppermute | solution.py:23
  12.3 14.5 %collective-permute-start.1 = (bf16[512,128]{1,0:T(8,128)(2,1)S(1)}, bf16[512,128]{1,0:T(8,128)(2,1)S(1)}, u32[]{:S(2)}, u32[]{:S(2)}) collective-permute-start(bf16[512,128]{1,0:T(8,128)(2,1)S(1)} %get-tuple-element.50), channel_id=1, source_target_pairs={{0,16},{8,24},{16,0},{24,8},{1,17},{9,25},{17,1},{25,9},{2,18},{10... | collective-permute-start | bytes 393224 | tf_op jit(solution)/shard_map/ppermute | solution.py:23
  28.4 11.0 %collective-permute-done.1 = bf16[512,128]{1,0:T(8,128)(2,1)S(1)} collective-permute-done((bf16[512,128]{1,0:T(8,128)(2,1)S(1)}, bf16[512,128]{1,0:T(8,128)(2,1)S(1)}, u32[]{:S(2)}, u32[]{:S(2)}) %collective-permute-start.1) | collective-permute-done | bytes 131104 | tf_op jit(solution)/shard_map/ppermute | solution.py:23
  42.7 2.6 %collective-permute-start.10 = (bf16[24,2304]{1,0:T(8,128)(2,1)S(1)}, bf16[24,2304]{1,0:T(8,128)(2,1)S(1)}, u32[]{:S(2)}, u32[]{:S(2)}) collective-permute-start(bf16[24,2304]{1,0:T(8,128)(2,1)S(1)} %get-tuple-element.105), channel_id=1, source_target_pairs={{0,4},{1,5},{2,6},{3,7},{4,0},{5,1},{6,2},{7,3},{8,12},{9,13},{10,... | collective-permute-start | bytes 331784 | tf_op jit(solution)/shard_map/ppermute | solution.py:23
  46.9 3.3 %collective-permute-start.11 = (bf16[24,2304]{1,0:T(8,128)(2,1)S(1)}, bf16[24,2304]{1,0:T(8,128)(2,1)S(1)}, u32[]{:S(2)}, u32[]{:S(2)}) collective-permute-start(bf16[24,2304]{1,0:T(8,128)(2,1)S(1)} %get-tuple-element.105), channel_id=1, source_target_pairs={{0,6},{1,7},{2,4},{3,5},{4,2},{5,3},{6,0},{7,1},{8,14},{9,15},{10,... | collective-permute-start | bytes 331784 | tf_op jit(solution)/shard_map/ppermute | solution.py:23
  53.9 2.6 %collective-permute-start.17 = (bf16[24,2304]{1,0:T(8,128)(2,1)S(1)}, bf16[24,2304]{1,0:T(8,128)(2,1)S(1)}, u32[]{:S(2)}, u32[]{:S(2)}) collective-permute-start(bf16[24,2304]{1,0:T(8,128)(2,1)S(1)} %get-tuple-element.103), channel_id=1, source_target_pairs={{0,4},{1,5},{2,6},{3,7},{4,0},{5,1},{6,2},{7,3},{8,12},{9,13},{10,... | collective-permute-start | bytes 331784 | tf_op jit(solution)/shard_map/ppermute | solution.py:23
  57.6 2.5 %collective-permute-start.18 = (bf16[24,2304]{1,0:T(8,128)(2,1)S(1)}, bf16[24,2304]{1,0:T(8,128)(2,1)S(1)}, u32[]{:S(2)}, u32[]{:S(2)}) collective-permute-start(bf16[24,2304]{1,0:T(8,128)(2,1)S(1)} %get-tuple-element.103), channel_id=1, source_target_pairs={{0,6},{1,7},{2,4},{3,5},{4,2},{5,3},{6,0},{7,1},{8,14},{9,15},{10,... | collective-permute-start | bytes 331784 | tf_op jit(solution)/shard_map/ppermute | solution.py:23
  60.1 2.6 %collective-permute-done.17 = bf16[24,2304]{1,0:T(8,128)(2,1)S(1)} collective-permute-done((bf16[24,2304]{1,0:T(8,128)(2,1)S(1)}, bf16[24,2304]{1,0:T(8,128)(2,1)S(1)}, u32[]{:S(2)}, u32[]{:S(2)}) %collective-permute-start.17) | collective-permute-done | bytes 110624 | tf_op jit(solution)/shard_map/ppermute | solution.py:23
  64.6 2.6 %collective-permute-start.24 = (bf16[24,2304]{1,0:T(8,128)(2,1)S(1)}, bf16[24,2304]{1,0:T(8,128)(2,1)S(1)}, u32[]{:S(2)}, u32[]{:S(2)}) collective-permute-start(bf16[24,2304]{1,0:T(8,128)(2,1)S(1)} %get-tuple-element.90), channel_id=1, source_target_pairs={{0,4},{1,5},{2,6},{3,7},{4,0},{5,1},{6,2},{7,3},{8,12},{9,13},{10,... | collective-permute-start | bytes 331784 | tf_op jit(solution)/shard_map/ppermute | solution.py:23
  72.7 2.5 %collective-permute-done.25 = bf16[24,2304]{1,0:T(8,128)(2,1)S(1)} collective-permute-done((bf16[24,2304]{1,0:T(8,128)(2,1)S(1)}, bf16[24,2304]{1,0:T(8,128)(2,1)S(1)}, u32[]{:S(2)}, u32[]{:S(2)}) %collective-permute-start.25) | collective-permute-done | bytes 110624 | tf_op jit(solution)/shard_map/ppermute | solution.py:23
  78.1 2.4 %shard_map.75 = (f32[4,96,640]{2,1,0:T(8,128)S(1)}, bf16[4,96,640]{2,1,0:T(8,128)(2,1)S(1)}) custom-call(s32[2]{0:T(128)S(1)} %pad_add_fusion.ids, bf16[512,128]{1,0:T(8,128)(2,1)S(1)} %fusion.5.g0.g_ref, bf16[1024,256]{1,0:T(8,128)(2,1)S(1)} %get-tuple-element.95.x_ref), custom_call_target="tpu_custom_call" | custom-call | bytes 655368 | tf_op jit(solution)/shard_map/pallas_call | solution.py:104
  81.1 3.3 %collective-permute-done.4.g2 = bf16[512,128]{1,0:T(8,128)(2,1)S(1)} collective-permute-done((bf16[512,128]{1,0:T(8,128)(2,1)S(1)}, bf16[512,128]{1,0:T(8,128)(2,1)S(1)}, u32[]{:S(2)}, u32[]{:S(2)}) %collective-permute-start.4) | collective-permute-done | bytes 131104 | tf_op jit(solution)/shard_map/ppermute | solution.py:23
  84.4 2.9 %shard_map.66 = (bf16[512,128]{1,0:T(8,128)(2,1)S(1)}, bf16[512,128]{1,0:T(8,128)(2,1)S(1)}) custom-call(s32[2]{0:T(128)S(1)} %pad_add_fusion.ids, bf16[512,128]{1,0:T(8,128)(2,1)S(1)} %fusion.5.g0.g_ref, bf16[512,128]{1,0:T(8,128)(2,1)S(1)} %collective-permute-done.3.g1, bf16[512,128]{1,0:T(8,128)(2,1)S(1)} %collective-permute-done.4.g2, ...), custom_call_target="tpu_custom_call" | custom-call | bytes 1671176 | tf_op jit(solution)/shard_map/pallas_call | solution.py:104
  93.8 2.7 %collective-permute-done.15.g3 = bf16[512,128]{1,0:T(8,128)(2,1)S(1)} collective-permute-done((bf16[512,128]{1,0:T(8,128)(2,1)S(1)}, bf16[512,128]{1,0:T(8,128)(2,1)S(1)}, u32[]{:S(2)}, u32[]{:S(2)}) %collective-permute-start.15) | collective-permute-done | bytes 131104 | tf_op jit(solution)/shard_map/ppermute | solution.py:23
  96.6 3.1 %shard_map.67 = (bf16[512,128]{1,0:T(8,128)(2,1)S(1)}, bf16[512,128]{1,0:T(8,128)(2,1)S(1)}) custom-call(s32[2]{0:T(128)S(1)} %pad_add_fusion.ids, bf16[512,128]{1,0:T(8,128)(2,1)S(1)} %get-tuple-element.56.g0.g_ref, bf16[512,128]{1,0:T(8,128)(2,1)S(1)} %collective-permute-done.13.g1, bf16[512,128]{1,0:T(8,128)(2,1)S(1)} %collective-permute-done.14.g2, ...), custom_call_target="tpu_custom_call" | custom-call | bytes 1671176 | tf_op jit(solution)/shard_map/pallas_call | solution.py:104
  108.1 3.6 %shard_map.68 = (bf16[512,128]{1,0:T(8,128)(2,1)}, bf16[512,128]{1,0:T(8,128)(2,1)S(1)}) custom-call(s32[2]{0:T(128)S(1)} %pad_add_fusion.ids, bf16[512,128]{1,0:T(8,128)(2,1)S(1)} %get-tuple-element.58.g0.g_ref, bf16[512,128]{1,0:T(8,128)(2,1)S(1)} %collective-permute-done.20.g1, bf16[512,128]{1,0:T(8,128)(2,1)S(1)} %collective-permute-done.21.g2, ...), custom_call_target="tpu_custom_call" | custom-call | bytes 1671176 | tf_op jit(solution)/shard_map/pallas_call | solution.py:104
  115.9 3.3 %collective-permute-start.45 = (bf16[96,640]{1,0:T(8,128)(2,1)S(1)}, bf16[96,640]{1,0:T(8,128)(2,1)S(1)}, u32[]{:S(2)}, u32[]{:S(2)}) collective-permute-start(bf16[96,640]{1,0:T(8,128)(2,1)S(1)} %get-tuple-element.84), channel_id=1, source_target_pairs={{0,6},{1,7},{2,4},{3,5},{4,2},{5,3},{6,0},{7,1},{8,14},{9,15},{10,... | collective-permute-start | bytes 368648 | tf_op jit(solution)/shard_map/ppermute | solution.py:23
  121.9 5.5 %collective-permute-done.44.refs_14_ = bf16[96,640]{1,0:T(8,128)(2,1)S(1)} collective-permute-done((bf16[96,640]{1,0:T(8,128)(2,1)S(1)}, bf16[96,640]{1,0:T(8,128)(2,1)S(1)}, u32[]{:S(2)}, u32[]{:S(2)}) %collective-permute-start.44) | collective-permute-done | bytes 122912 | tf_op jit(solution)/shard_map/ppermute | solution.py:23
  129.3 6.2 %collective-permute-start.36 = (bf16[96,640]{1,0:T(8,128)(2,1)S(1)}, bf16[96,640]{1,0:T(8,128)(2,1)S(1)}, u32[]{:S(2)}, u32[]{:S(2)}) collective-permute-start(bf16[96,640]{1,0:T(8,128)(2,1)S(1)} %get-tuple-element.71), channel_id=1, source_target_pairs={{0,4},{1,5},{2,6},{3,7},{4,0},{5,1},{6,2},{7,3},{8,12},{9,13},{10,... | collective-permute-start | bytes 368648 | tf_op jit(solution)/shard_map/ppermute | solution.py:23
  135.6 2.5 %collective-permute-start.37 = (bf16[96,640]{1,0:T(8,128)(2,1)S(1)}, bf16[96,640]{1,0:T(8,128)(2,1)S(1)}, u32[]{:S(2)}, u32[]{:S(2)}) collective-permute-start(bf16[96,640]{1,0:T(8,128)(2,1)S(1)} %get-tuple-element.72), channel_id=1, source_target_pairs={{0,6},{1,7},{2,4},{3,5},{4,2},{5,3},{6,0},{7,1},{8,14},{9,15},{10,... | collective-permute-start | bytes 368648 | tf_op jit(solution)/shard_map/ppermute | solution.py:23
  138.1 3.4 %collective-permute-done.40.refs_10_ = bf16[96,640]{1,0:T(8,128)(2,1)S(1)} collective-permute-done((bf16[96,640]{1,0:T(8,128)(2,1)S(1)}, bf16[96,640]{1,0:T(8,128)(2,1)S(1)}, u32[]{:S(2)}, u32[]{:S(2)}) %collective-permute-start.40) | collective-permute-done | bytes 122912 | tf_op jit(solution)/shard_map/ppermute | solution.py:23
  141.6 4.7 %collective-permute-start.32 = (bf16[96,640]{1,0:T(8,128)(2,1)S(1)}, bf16[96,640]{1,0:T(8,128)(2,1)S(1)}, u32[]{:S(2)}, u32[]{:S(2)}) collective-permute-start(bf16[96,640]{1,0:T(8,128)(2,1)S(1)} %get-tuple-element.65), channel_id=1, source_target_pairs={{0,4},{1,5},{2,6},{3,7},{4,0},{5,1},{6,2},{7,3},{8,12},{9,13},{10,... | collective-permute-start | bytes 368648 | tf_op jit(solution)/shard_map/ppermute | solution.py:23
  146.2 2.4 %collective-permute-start.33 = (bf16[96,640]{1,0:T(8,128)(2,1)S(1)}, bf16[96,640]{1,0:T(8,128)(2,1)S(1)}, u32[]{:S(2)}, u32[]{:S(2)}) collective-permute-start(bf16[96,640]{1,0:T(8,128)(2,1)S(1)} %get-tuple-element.66), channel_id=1, source_target_pairs={{0,6},{1,7},{2,4},{3,5},{4,2},{5,3},{6,0},{7,1},{8,14},{9,15},{10,... | collective-permute-start | bytes 368648 | tf_op jit(solution)/shard_map/ppermute | solution.py:23
  149.0 10.0 %collective-permute-done.32.refs_2_ = bf16[96,640]{1,0:T(8,128)(2,1)S(1)} collective-permute-done((bf16[96,640]{1,0:T(8,128)(2,1)S(1)}, bf16[96,640]{1,0:T(8,128)(2,1)S(1)}, u32[]{:S(2)}, u32[]{:S(2)}) %collective-permute-start.32) | collective-permute-done | bytes 122912 | tf_op jit(solution)/shard_map/ppermute | solution.py:23
  (122 shorter events, 67.9 us)
Async XLA Ops:
  5.9 20.9 %collective-permute-start.8 = (bf16[24,2304]{1,0:T(8,128)(2,1)S(1)}, bf16[24,2304]{1,0:T(8,128)(2,1)S(1)}, u32[]{:S(2)}, u32[]{:S(2)}) collective-permute-start(bf16[24,2304]{1,0:T(8,128)(2,1)S(1)} %get-tuple-element.55), channel_id=1, source_target_pairs={{0,24},{8,16},{16,8},{24,0},{1,25},{9,17},{17,9},{25,1},{2,26},{10... | collective-permute-start | bytes 331784 | tf_op jit(solution)/shard_map/ppermute | solution.py:23
  7.3 19.5 %collective-permute-start.6 = (bf16[24,2304]{1,0:T(8,128)(2,1)S(1)}, bf16[24,2304]{1,0:T(8,128)(2,1)S(1)}, u32[]{:S(2)}, u32[]{:S(2)}) collective-permute-start(bf16[24,2304]{1,0:T(8,128)(2,1)S(1)} %get-tuple-element.53), channel_id=1, source_target_pairs={{0,8},{8,0},{16,24},{24,16},{1,9},{9,1},{17,25},{25,17},{2,10},{10... | collective-permute-start | bytes 331784 | tf_op jit(solution)/shard_map/ppermute | solution.py:23
  7.4 67.8 %collective-permute-start.28 = (bf16[1024,256]{1,0:T(8,128)(2,1)S(1)}, bf16[1024,256]{1,0:T(8,128)(2,1)S(1)}, u32[]{:S(2)}, u32[]{:S(2)}) collective-permute-start(bf16[1024,256]{1,0:T(8,128)(2,1)S(1)} %bitcast.51), channel_id=1, source_target_pairs={{0,16},{8,24},{16,0},{24,8},{1,17},{9,25},{17,1},{25,9},{2,18},{10... | collective-permute-start | bytes 1572872 | tf_op jit(solution)/shard_map/ppermute | solution.py:23
  9.4 68.1 %collective-permute-start.29 = (bf16[1024,256]{1,0:T(8,128)(2,1)S(1)}, bf16[1024,256]{1,0:T(8,128)(2,1)S(1)}, u32[]{:S(2)}, u32[]{:S(2)}) collective-permute-start(bf16[1024,256]{1,0:T(8,128)(2,1)S(1)} %bitcast.52), channel_id=1, source_target_pairs={{0,24},{8,16},{16,8},{24,0},{1,25},{9,17},{17,9},{25,1},{2,26},{10... | collective-permute-start | bytes 1572872 | tf_op jit(solution)/shard_map/ppermute | solution.py:23
  12.3 27.1 %collective-permute-start.1 = (bf16[512,128]{1,0:T(8,128)(2,1)S(1)}, bf16[512,128]{1,0:T(8,128)(2,1)S(1)}, u32[]{:S(2)}, u32[]{:S(2)}) collective-permute-start(bf16[512,128]{1,0:T(8,128)(2,1)S(1)} %get-tuple-element.50), channel_id=1, source_target_pairs={{0,16},{8,24},{16,0},{24,8},{1,17},{9,25},{17,1},{25,9},{2,18},{10... | collective-permute-start | bytes 393224 | tf_op jit(solution)/shard_map/ppermute | solution.py:23
  26.8 14.3 %collective-permute-start.2 = (bf16[512,128]{1,0:T(8,128)(2,1)S(1)}, bf16[512,128]{1,0:T(8,128)(2,1)S(1)}, u32[]{:S(2)}, u32[]{:S(2)}) collective-permute-start(bf16[512,128]{1,0:T(8,128)(2,1)S(1)} %get-tuple-element.51), channel_id=1, source_target_pairs={{0,24},{8,16},{16,8},{24,0},{1,25},{9,17},{17,9},{25,1},{2,26},{10... | collective-permute-start | bytes 393224 | tf_op jit(solution)/shard_map/ppermute | solution.py:23
  26.8 15.9 %collective-permute-start = (bf16[512,128]{1,0:T(8,128)(2,1)S(1)}, bf16[512,128]{1,0:T(8,128)(2,1)S(1)}, u32[]{:S(2)}, u32[]{:S(2)}) collective-permute-start(bf16[512,128]{1,0:T(8,128)(2,1)S(1)} %get-tuple-element.49), channel_id=1, source_target_pairs={{0,8},{8,0},{16,24},{24,16},{1,9},{9,1},{17,25},{25,17},{2,10},{10... | collective-permute-start | bytes 393224 | tf_op jit(solution)/shard_map/ppermute | solution.py:23
  39.4 38.1 %collective-permute-start.27 = (bf16[1024,256]{1,0:T(8,128)(2,1)S(1)}, bf16[1024,256]{1,0:T(8,128)(2,1)S(1)}, u32[]{:S(2)}, u32[]{:S(2)}) collective-permute-start(bf16[1024,256]{1,0:T(8,128)(2,1)S(1)} %bitcast.53), channel_id=1, source_target_pairs={{0,8},{8,0},{16,24},{24,16},{1,9},{9,1},{17,25},{25,17},{2,10},{10... | collective-permute-start | bytes 1572872 | tf_op jit(solution)/shard_map/ppermute | solution.py:23
  77.5 11.8 %collective-permute-start.19 = (bf16[4,24,2304]{2,1,0:T(8,128)(2,1)S(1)}, bf16[4,24,2304]{2,1,0:T(8,128)(2,1)S(1)}, u32[]{:S(2)}, u32[]{:S(2)}) collective-permute-start(bf16[4,24,2304]{2,1,0:T(8,128)(2,1)S(1)} %pad_maximum_fusion.1), channel_id=1, source_target_pairs={{0,1},{1,0},{2,3},{3,2},{4,5},{5,4},{6,7},{7,6},{8,9},{9,8},{10,11... | collective-permute-start | bytes 1327112 | tf_op jit(solution)/shard_map/ppermute | solution.py:23
  80.5 21.6 %collective-permute-start.26 = (bf16[4,24,2304]{2,1,0:T(8,128)(2,1)S(1)}, bf16[4,24,2304]{2,1,0:T(8,128)(2,1)S(1)}, u32[]{:S(2)}, u32[]{:S(2)}) collective-permute-start(bf16[4,24,2304]{2,1,0:T(8,128)(2,1)S(1)} %pad_maximum_fusion.2), channel_id=1, source_target_pairs={{0,1},{1,0},{2,3},{3,2},{4,5},{5,4},{6,7},{7,6},{8,9},{9,8},{10,11... | collective-permute-start | bytes 1327112 | tf_op jit(solution)/shard_map/ppermute | solution.py:23
  80.8 33.3 %collective-permute-start.42 = (bf16[4,96,640]{2,1,0:T(8,128)(2,1)S(1)}, bf16[4,96,640]{2,1,0:T(8,128)(2,1)S(1)}, u32[]{:S(2)}, u32[]{:S(2)}) collective-permute-start(bf16[4,96,640]{2,1,0:T(8,128)(2,1)S(1)} %get-tuple-element.80), channel_id=1, source_target_pairs={{0,1},{1,0},{2,3},{3,2},{4,5},{5,4},{6,7},{7,6},{8,9},{9,8},{10,11... | collective-permute-start | bytes 1474568 | tf_op jit(solution)/shard_map/ppermute | solution.py:23
  93.8 22.1 %collective-permute-start.38 = (bf16[4,96,640]{2,1,0:T(8,128)(2,1)S(1)}, bf16[4,96,640]{2,1,0:T(8,128)(2,1)S(1)}, u32[]{:S(2)}, u32[]{:S(2)}) collective-permute-start(bf16[4,96,640]{2,1,0:T(8,128)(2,1)S(1)} %get-tuple-element.74), channel_id=1, source_target_pairs={{0,1},{1,0},{2,3},{3,2},{4,5},{5,4},{6,7},{7,6},{8,9},{9,8},{10,11... | collective-permute-start | bytes 1474568 | tf_op jit(solution)/shard_map/ppermute | solution.py:23
  105.7 14.2 %collective-permute-start.34 = (bf16[4,96,640]{2,1,0:T(8,128)(2,1)S(1)}, bf16[4,96,640]{2,1,0:T(8,128)(2,1)S(1)}, u32[]{:S(2)}, u32[]{:S(2)}) collective-permute-start(bf16[4,96,640]{2,1,0:T(8,128)(2,1)S(1)} %get-tuple-element.68), channel_id=1, source_target_pairs={{0,1},{1,0},{2,3},{3,2},{4,5},{5,4},{6,7},{7,6},{8,9},{9,8},{10,11... | collective-permute-start | bytes 1474568 | tf_op jit(solution)/shard_map/ppermute | solution.py:23
  114.0 14.6 %collective-permute-start.30 = (bf16[4,96,640]{2,1,0:T(8,128)(2,1)S(1)}, bf16[4,96,640]{2,1,0:T(8,128)(2,1)S(1)}, u32[]{:S(2)}, u32[]{:S(2)}) collective-permute-start(bf16[4,96,640]{2,1,0:T(8,128)(2,1)S(1)} %get-tuple-element.62), channel_id=1, source_target_pairs={{0,1},{1,0},{2,3},{3,2},{4,5},{5,4},{6,7},{7,6},{8,9},{9,8},{10,11... | collective-permute-start | bytes 1474568 | tf_op jit(solution)/shard_map/ppermute | solution.py:23
  114.8 12.5 %collective-permute-start.44 = (bf16[96,640]{1,0:T(8,128)(2,1)S(1)}, bf16[96,640]{1,0:T(8,128)(2,1)S(1)}, u32[]{:S(2)}, u32[]{:S(2)}) collective-permute-start(bf16[96,640]{1,0:T(8,128)(2,1)S(1)} %get-tuple-element.83), channel_id=1, source_target_pairs={{0,4},{1,5},{2,6},{3,7},{4,0},{5,1},{6,2},{7,3},{8,12},{9,13},{10,... | collective-permute-start | bytes 368648 | tf_op jit(solution)/shard_map/ppermute | solution.py:23
  115.9 13.4 %collective-permute-start.45 = (bf16[96,640]{1,0:T(8,128)(2,1)S(1)}, bf16[96,640]{1,0:T(8,128)(2,1)S(1)}, u32[]{:S(2)}, u32[]{:S(2)}) collective-permute-start(bf16[96,640]{1,0:T(8,128)(2,1)S(1)} %get-tuple-element.84), channel_id=1, source_target_pairs={{0,6},{1,7},{2,4},{3,5},{4,2},{5,3},{6,0},{7,1},{8,14},{9,15},{10,... | collective-permute-start | bytes 368648 | tf_op jit(solution)/shard_map/ppermute | solution.py:23
  119.9 15.7 %collective-permute-start.39 = (bf16[96,640]{1,0:T(8,128)(2,1)S(1)}, bf16[96,640]{1,0:T(8,128)(2,1)S(1)}, u32[]{:S(2)}, u32[]{:S(2)}) collective-permute-start(bf16[96,640]{1,0:T(8,128)(2,1)S(1)} %get-tuple-element.76), channel_id=1, source_target_pairs={{0,2},{1,3},{2,0},{3,1},{4,6},{5,7},{6,4},{7,5},{8,10},{9,11},{10,... | collective-permute-start | bytes 368648 | tf_op jit(solution)/shard_map/ppermute | solution.py:23
  121.7 19.9 %collective-permute-start.40 = (bf16[96,640]{1,0:T(8,128)(2,1)S(1)}, bf16[96,640]{1,0:T(8,128)(2,1)S(1)}, u32[]{:S(2)}, u32[]{:S(2)}) collective-permute-start(bf16[96,640]{1,0:T(8,128)(2,1)S(1)} %get-tuple-element.77), channel_id=1, source_target_pairs={{0,4},{1,5},{2,6},{3,7},{4,0},{5,1},{6,2},{7,3},{8,12},{9,13},{10,... | collective-permute-start | bytes 368648 | tf_op jit(solution)/shard_map/ppermute | solution.py:23
  127.3 14.2 %collective-permute-start.41 = (bf16[96,640]{1,0:T(8,128)(2,1)S(1)}, bf16[96,640]{1,0:T(8,128)(2,1)S(1)}, u32[]{:S(2)}, u32[]{:S(2)}) collective-permute-start(bf16[96,640]{1,0:T(8,128)(2,1)S(1)} %get-tuple-element.78), channel_id=1, source_target_pairs={{0,6},{1,7},{2,4},{3,5},{4,2},{5,3},{6,0},{7,1},{8,14},{9,15},{10,... | collective-permute-start | bytes 368648 | tf_op jit(solution)/shard_map/ppermute | solution.py:23
  128.7 17.6 %collective-permute-start.35 = (bf16[96,640]{1,0:T(8,128)(2,1)S(1)}, bf16[96,640]{1,0:T(8,128)(2,1)S(1)}, u32[]{:S(2)}, u32[]{:S(2)}) collective-permute-start(bf16[96,640]{1,0:T(8,128)(2,1)S(1)} %get-tuple-element.70), channel_id=1, source_target_pairs={{0,2},{1,3},{2,0},{3,1},{4,6},{5,7},{6,4},{7,5},{8,10},{9,11},{10,... | collective-permute-start | bytes 368648 | tf_op jit(solution)/shard_map/ppermute | solution.py:23
  129.3 19.3 %collective-permute-start.36 = (bf16[96,640]{1,0:T(8,128)(2,1)S(1)}, bf16[96,640]{1,0:T(8,128)(2,1)S(1)}, u32[]{:S(2)}, u32[]{:S(2)}) collective-permute-start(bf16[96,640]{1,0:T(8,128)(2,1)S(1)} %get-tuple-element.71), channel_id=1, source_target_pairs={{0,4},{1,5},{2,6},{3,7},{4,0},{5,1},{6,2},{7,3},{8,12},{9,13},{10,... | collective-permute-start | bytes 368648 | tf_op jit(solution)/shard_map/ppermute | solution.py:23
  135.6 13.1 %collective-permute-start.37 = (bf16[96,640]{1,0:T(8,128)(2,1)S(1)}, bf16[96,640]{1,0:T(8,128)(2,1)S(1)}, u32[]{:S(2)}, u32[]{:S(2)}) collective-permute-start(bf16[96,640]{1,0:T(8,128)(2,1)S(1)} %get-tuple-element.72), channel_id=1, source_target_pairs={{0,6},{1,7},{2,4},{3,5},{4,2},{5,3},{6,0},{7,1},{8,14},{9,15},{10,... | collective-permute-start | bytes 368648 | tf_op jit(solution)/shard_map/ppermute | solution.py:23
  141.6 17.4 %collective-permute-start.32 = (bf16[96,640]{1,0:T(8,128)(2,1)S(1)}, bf16[96,640]{1,0:T(8,128)(2,1)S(1)}, u32[]{:S(2)}, u32[]{:S(2)}) collective-permute-start(bf16[96,640]{1,0:T(8,128)(2,1)S(1)} %get-tuple-element.65), channel_id=1, source_target_pairs={{0,4},{1,5},{2,6},{3,7},{4,0},{5,1},{6,2},{7,3},{8,12},{9,13},{10,... | collective-permute-start | bytes 368648 | tf_op jit(solution)/shard_map/ppermute | solution.py:23
  146.2 12.7 %collective-permute-start.33 = (bf16[96,640]{1,0:T(8,128)(2,1)S(1)}, bf16[96,640]{1,0:T(8,128)(2,1)S(1)}, u32[]{:S(2)}, u32[]{:S(2)}) collective-permute-start(bf16[96,640]{1,0:T(8,128)(2,1)S(1)} %get-tuple-element.66), channel_id=1, source_target_pairs={{0,6},{1,7},{2,4},{3,5},{4,2},{5,3},{6,0},{7,1},{8,14},{9,15},{10,... | collective-permute-start | bytes 368648 | tf_op jit(solution)/shard_map/ppermute | solution.py:23
  (30 other events, 211.0 us)

commit v2 on v1

v2 whole, which is shorter than its diff:
```python
import functools
import math

import jax
import jax.numpy as jnp
from jax import lax
from jax.experimental import pallas as pl
from jax.experimental.pallas import tpu as pltpu
from jax.sharding import PartitionSpec as P

BF16 = jnp.bfloat16
F32 = jnp.float32
VMEM_BYTES = 48 * 1024 * 1024
PEAK_PER_US = 1.1535e9


def shifted(x, axis, by):
    size = lax.axis_size(axis)
    pairs = [(i, i + by) for i in range(size) if 0 <= i + by < size]
    return lax.ppermute(x, axis, pairs)


def swapped(x, axis, mask):
    return lax.ppermute(x, axis, [(i, i ^ mask) for i in range(lax.axis_size(axis))])


def tap_stack(field, sign):
    batch_n, span_t, span_x, span_y, channels = field.shape
    padded = jnp.pad(field, ((0, 0), (1, 1), (1, 1), (1, 1), (0, 0)))
    views = []
    for along_t in (-1, 0, 1):
        for along_x in (-1, 0, 1):
            for along_y in (-1, 0, 1):
                start_t = 1 + sign * along_t
                start_x = 1 + sign * along_x
                start_y = 1 + sign * along_y
                views.append(
                    padded[
                        :,
                        start_t : start_t + span_t,
                        start_x : start_x + span_x,
                        start_y : start_y + span_y,
                        :,
                    ]
                )
    return jnp.stack(views, axis=4).reshape(batch_n * span_t * span_x * span_y, 27, channels)


def general_shards(activations, preacts, out_grad, weights, momentum, noise):
    segments = lax.axis_size("segment")
    devices_dp = lax.axis_size("dp")
    segment_id = lax.axis_index("segment")
    kernel = lax.all_gather(weights.astype(BF16), "dp", axis=1, tiled=True)[0]
    inputs = activations[0]
    pres = preacts[0]
    micro, span_t, span_x, span_y, channels = inputs.shape
    cells = span_t * span_x * span_y
    is_last = segment_id == segments - 1

    def step_fn(step, carry):
        incoming, total = carry
        index = step - (segments - 1 - segment_id)
        valid = jnp.logical_and(index >= 0, index < micro)
        clipped = jnp.clip(index, 0, micro - 1)
        given = lax.dynamic_index_in_dim(out_grad, clipped, 0, keepdims=False)
        upstream = jnp.where(is_last, given, incoming)
        pre = lax.dynamic_index_in_dim(pres, clipped, 0, keepdims=False).astype(F32)
        sig = jax.nn.sigmoid(pre)
        up_wide = upstream.astype(F32)
        grad_pre = (up_wide * sig * (1.0 + pre * (1.0 - sig)) * valid.astype(F32)).astype(BF16)
        pre_cols = tap_stack(grad_pre[None], -1)
        back = jnp.einsum("nto,cto->nc", pre_cols, kernel, preferred_element_type=F32)
        passed = (up_wide + back.reshape(upstream.shape)).astype(BF16)
        in_cols = tap_stack(lax.dynamic_index_in_dim(inputs, clipped, 0, keepdims=True), 1)
        total = total + jnp.einsum(
            "ntc,no->cto", in_cols, grad_pre.reshape(cells, channels), preferred_element_type=F32
        )
        return shifted(passed, "segment", -1), total

    init = (jnp.zeros(inputs.shape[1:], BF16), jnp.zeros((channels, 27, channels), F32))
    total = lax.fori_loop(0, micro + segments - 1, step_fn, init)[1]
    owned = lax.psum_scatter(total, "dp", scatter_dimension=0, tiled=True)
    rate = 1.0 / math.sqrt(devices_dp * micro * cells)
    return (0.9 * momentum[0] - rate * owned + 0.3 * noise[0])[None]


def iota(shape, dim):
    return lax.broadcasted_iota(jnp.int32, shape, dim)


def log2(n):
    return n.bit_length() - 1


def channel_of(place, quarter, per, sub):
    return (place >> log2(sub)) * per + quarter * sub + (place & (sub - 1))


def dot(a, b):
    return jnp.dot(a, b, preferred_element_type=F32)


def call(body, out_shape, args, us, scratch=()):
    return pl.pallas_call(
        body,
        out_shape=out_shape,
        in_specs=[pl.BlockSpec(memory_space=pltpu.SMEM)]
        + [pl.BlockSpec(memory_space=pltpu.VMEM)] * (len(args) - 1),
        out_specs=jax.tree.map(lambda _: pl.BlockSpec(memory_space=pltpu.VMEM), out_shape),
        scratch_shapes=list(scratch),
        compiler_params=pltpu.CompilerParams(vmem_limit_bytes=VMEM_BYTES),
        cost_estimate=pl.CostEstimate(
            flops=int(us * PEAK_PER_US), bytes_accessed=0, transcendentals=0
        ),
    )(*args)


def weights_body(per, sub, ids, w_ref, *out_refs):
    channels = w_ref.shape[2]
    quarter_n = channels // 4
    s = ids[0]
    lane = iota((channels, channels), 1)
    place = lane & (quarter_n - 1)
    for m, out_ref in enumerate(out_refs):
        target = s ^ m
        own = w_ref[:, pl.ds(pl.multiple_of(target * sub, sub), sub), :]
        quarter = (lane >> log2(quarter_n)) ^ target
        order = iota((channels, channels), 0) == channel_of(place, quarter, per, sub)
        moved = dot(own.reshape(27 * sub, channels).astype(BF16), order.astype(BF16))
        for bc in range(9):
            part = [moved[(a * 9 + bc) * sub : (a * 9 + bc + 1) * sub] for a in range(3)]
            out_ref[:, bc * channels : (bc + 1) * channels] = jnp.concatenate(part, axis=0).astype(
                BF16
            )


def packing(channels, s, per, sub):
    quarter_n = channels // 4
    shape = (channels, 8 * quarter_n)
    lane = iota(shape, 1)
    place = lane & (quarter_n - 1)
    quarter = (lane >> log2(2 * quarter_n)) ^ s
    hit = iota(shape, 0) == channel_of(place, quarter, per, sub)
    low = (lane & (2 * quarter_n - 1)) < quarter_n
    first = jnp.logical_and(hit, low).astype(BF16)
    second = jnp.logical_and(hit, jnp.logical_not(low)).astype(BF16)
    return first, second


def packed_into(refs, field, first, second):
    half = field.shape[0] // 2
    width = first.shape[1] // 4
    lanes = width * len(refs)
    moved = dot(field[:half], first[:, :lanes]) + dot(field[half:], second[:, :lanes])
    for m, ref in enumerate(refs):
        ref[...] = moved[:, m * width : (m + 1) * width].astype(BF16)


def preacts_body(per, sub, ids, pre_ref, up_ref, up_out, *out_refs):
    first, second = packing(pre_ref.shape[1], ids[0], per, sub)
    packed_into(out_refs, pre_ref, first, second)
    packed_into([up_out], up_ref, first, second)


def first_body(per, sub, ids, up_ref, pre_ref, x_ref, *out_refs):
    half = up_ref.shape[0]
    packed_into([r.at[half:] for r in out_refs], x_ref, *packing(x_ref.shape[1], ids[0], per, sub))
    grad_pre = silu_back(up_ref[...].astype(F32), pre_ref[...])
    for ref in out_refs:
        ref[:half] = grad_pre


def silu_back(up_wide, pre):
    pre = pre.astype(F32)
    sig = jax.nn.sigmoid(pre)
    return (up_wide * sig * (1.0 + pre * (1.0 - sig))).astype(BF16)


def shifts(field, span):
    span_x, span_y = span
    rows, lanes = field.shape
    y = iota((rows, lanes), 0) & (span_y - 1)
    along_y = (
        jnp.where(y == span_y - 1, 0.0, pltpu.roll(field, rows - 1, 0)),
        field,
        jnp.where(y == 0, 0.0, pltpu.roll(field, 1, 0)),
    )
    out = []
    for b in (-1, 0, 1):
        for c in (-1, 0, 1):
            part = along_y[c + 1].reshape(rows // (span_x * span_y), span_x, span_y, lanes)
            edge = jnp.zeros_like(part[:, :1])
            if b == 1:
                part = jnp.concatenate([edge, part[:, :-1]], axis=1)
            elif b == -1:
                part = jnp.concatenate([part[:, 1:], edge], axis=1)
            out.append(part.reshape(rows, lanes))
    return out


def fill_columns(cols, parts, half, span):
    width = parts[0].shape[1]
    quarter_n = width // 2
    channels = 4 * quarter_n
    shape = (4 * width, 2 * channels)
    src, dst = iota(shape, 0), iota(shape, 1)
    m, h, place = src >> log2(width), (src >> log2(quarter_n)) & 1, src & (quarter_n - 1)
    unpack = (dst == h * channels + m * quarter_n + place).astype(BF16)
    both = dot(jnp.concatenate([part[:half] for part in parts], axis=1), unpack)
    field = jnp.concatenate([both[:, :channels], both[:, channels:]], axis=0)
    for k, part in enumerate(shifts(field, span[1:])):
        cols[:, k * channels : (k + 1) * channels] = part.astype(BF16)


def back_body(span, n_dp, ids, g0, g1, g2, g3, w_ref, up_ref, pre_ref, up_out, g_out, cols):
    span_t, span_x, span_y = span
    half, width = up_ref.shape
    quarter_n = width // 2
    sub = quarter_n // n_dp
    rows = 2 * half
    plane = span_x * span_y
    d = ids[1]
    fill_columns(cols, (g0, g1, g2, g3), half, span)
    shape = (3 * quarter_n, 3 * quarter_n)
    dst, src = iota(shape, 0), iota(shape, 1)
    a, place = dst >> log2(quarter_n), dst & (quarter_n - 1)
    apart = (place >> log2(sub)) ^ d
    piece = ((apart >> 2) & 1) + (apart & 2) + (n_dp // 2) * (apart & 1)
    order = src == piece * (3 * sub) + a * sub + (place & (sub - 1))
    kernel = dot(order.astype(BF16), w_ref[...]).astype(BF16)
    terms = lax.dot_general(
        cols[...], kernel, (((1,), (1,)), ((), ())), preferred_element_type=F32
    )
    back = []
    for a in range(3):
        back.append(
            terms[:, a * quarter_n : (a + 1) * quarter_n].reshape(
                rows // (span_t * plane), span_t, plane, quarter_n
            )
        )
    edge = jnp.zeros_like(back[0][:, :1])
    total = (
        back[1]
        + jnp.concatenate([back[0][:, 1:], edge], axis=1)
        + jnp.concatenate([edge, back[2][:, :-1]], axis=1)
    ).reshape(rows, quarter_n)
    total = jnp.concatenate([total[:half], total[half:]], axis=1)
    passed = (up_ref[...].astype(F32) + total).astype(BF16)
    up_out[...] = passed
    g_out[...] = silu_back(passed.astype(F32), pre_ref[...])


def grads_body(span, n_dp, ids, g0, g1, g2, g3, x_ref, keep, give, cols, total):
    span_t, span_x, span_y = span
    half, width = x_ref.shape
    quarter_n = width // 2
    sub = quarter_n // n_dp
    plane = span_x * span_y
    d = ids[1]
    fill_columns(cols, (g0, g1, g2, g3), half, span)
    shape = (width, 2 * width)
    src, dst = iota(shape, 0), iota(shape, 1)
    twice = jnp.logical_and(
        (src & (quarter_n - 1)) == (dst & (quarter_n - 1)),
        (src >> log2(quarter_n)) == (dst >> log2(width)),
    ).astype(BF16)
    both = dot(x_ref[...], twice)
    field = jnp.concatenate([both[:, :width], both[:, width:]], axis=0)
    field = field.reshape(2 * half // (span_t * plane), span_t, plane, width)
    edge = jnp.zeros_like(field[:, :1])
    later = jnp.concatenate([field[:, 1:], edge], axis=1)
    earlier = jnp.concatenate([edge, field[:, :-1]], axis=1)
    left = iota(field.shape, 3) < quarter_n
    taps = jnp.concatenate([jnp.where(left, earlier, field), later], axis=3)
    taps = taps.reshape(2 * half, 2 * width)[:, : 3 * quarter_n].astype(BF16)
    total[...] = lax.dot_general(
        taps, cols[...], (((0,), (0,)), ((), ())), preferred_element_type=F32
    )
    for k in range(n_dp // 2):
        for bit, ref in ((0, keep), (1, give)):
            owner = d ^ (2 * k + bit)
            own = [
                total[pl.ds(pl.multiple_of(a * quarter_n + owner * sub, sub), sub), :]
                for a in range(3)
            ]
            ref[k] = jnp.concatenate(own, axis=0).astype(ref.dtype)


def pair_body(ids, keep, other, stay, send):
    for k in range(keep.shape[0]):
        total = keep[k] + other[k].astype(F32)
        if k % 2 == 0:
            stay[k // 2] = total
        else:
            send[k // 2] = total.astype(BF16)


def next_body(ids, stay, other, own, send):
    own[...] = stay[0] + other[0].astype(F32)
    send[...] = (stay[1] + other[1].astype(F32)).astype(BF16)


def sums_body(ids, *refs):
    ins, outs = refs[:8], refs[8:]
    s = ids[0]
    for section in range(4):
        total = (ins[2 * section][...] + ins[2 * section + 1][...].astype(F32)).astype(BF16)
        for m, out_ref in enumerate(outs):
            @pl.when((s ^ m) == section)
            def _(out_ref=out_ref, total=total):
                out_ref[...] = total


def update_body(per, sub, rate, ids, f0, f1, f2, f3, momentum, noise, out):
    channels = momentum.shape[2]
    quarter_n = channels // 4
    s = ids[0]
    lane = iota((channels, channels), 0)
    for m, f in enumerate((f0, f1, f2, f3)):
        source = s ^ m
        place, quarter = lane & (quarter_n - 1), (lane >> log2(quarter_n)) ^ source
        order = iota((channels, channels), 1) == channel_of(place, quarter, per, sub)
        wide = f[...].astype(F32)
        parts = [
            wide[a * sub : (a + 1) * sub, bc * channels : (bc + 1) * channels]
            for a in range(3)
            for bc in range(9)
        ]
        grads = dot(jnp.concatenate(parts, axis=0).astype(BF16), order.astype(BF16))
        rows = pl.ds(pl.multiple_of(source * sub, sub), sub)
        out[:, rows, :] = (
            0.9 * momentum[:, rows, :]
            - rate * grads.reshape(27, sub, channels)
            + 0.3 * noise[:, rows, :]
        )


def pick(index, arrays):
    return lax.select_n(index, *arrays)


def after(x, *others):
    return lax.optimization_barrier((x, *others))[0]


def quartered_shards(activations, preacts, out_grad, weights, momentum, noise):
    n_dp = lax.axis_size("dp")
    s = lax.axis_index("segment").astype(jnp.int32)
    d = lax.axis_index("dp").astype(jnp.int32)
    ids = jnp.stack([s, d])
    micro, span_t, span_x, span_y, channels = out_grad.shape
    span = (span_t, span_x, span_y)
    rows = micro * span_t * span_x * span_y
    quarter_n = channels // 4
    width = 2 * quarter_n
    half = rows // 2
    per = channels // n_dp
    sub = per // 4
    inputs = activations.reshape(rows, channels)
    pres = preacts.reshape(rows, channels)
    packed = jax.ShapeDtypeStruct((half, width), BF16)
    piece = (3 * sub, 9 * channels)
    columns = pltpu.VMEM((rows, 9 * channels), BF16)

    def array(dtype, *lead):
        return jax.ShapeDtypeStruct(lead + piece, dtype)

    def by_tap(x):
        return jnp.swapaxes(x[0], 0, 1)

    def spread(parts):
        far, one, two = (swapped(parts[m], "segment", m) for m in (3, 1, 2))
        return parts[0], one, two, far

    w_held = spread(
        call(functools.partial(weights_body, per, sub), [array(BF16)] * 4, (ids, by_tap(weights)), 0.9)
    )
    up, *p_parts = call(
        functools.partial(preacts_body, per, sub),
        [packed] * 5,
        (ids, pres, out_grad.reshape(rows, channels)), 1.1,
    )
    p_held = spread(p_parts)

    def far_half(own, *others):
        return jnp.stack([own, after(swapped(own, "dp", 4), *others)])

    def all_chips(pieces, *others):
        return jnp.concatenate([pieces, after(swapped(pieces, "dp", 2), *others)], axis=0)

    def both_cores(pieces):
        other = swapped(pieces, "dp", 1)
        return jnp.concatenate([pieces, other], axis=0).reshape(3 * quarter_n, 9 * channels)

    def terms(field, x):
        return call(
            functools.partial(grads_body, span, n_dp),
            [array(F32, 4), array(BF16, 4)],
            (ids, *field, x), 2.6,
            scratch=[columns, pltpu.VMEM((3 * quarter_n, 9 * channels), F32)],
        )

    def paired(keep, give):
        return call(
            pair_body, [array(F32, 2), array(BF16, 2)], (ids, keep, swapped(give, "dp", 1)), 0.6
        )

    def reduced(stay, send, *others):
        other = after(swapped(send, "dp", 2), *others)
        return call(next_body, [array(F32), array(BF16)], (ids, stay, other), 0.6)

    def summed(own, send):
        return own, swapped(send, "dp", 4)

    def back(section, field, up):
        return call(
            functools.partial(back_body, span, n_dp),
            [packed] * 2,
            (ids, *field, kernels[section], up, pick(s ^ (section - 1), p_held)), 3.0,
            scratch=[columns],
        )

    def tied(field, *others):
        return lax.optimization_barrier((tuple(field), others))[0]

    def tied(field, *others):
        return lax.optimization_barrier((tuple(field), others))[0]

    kernels = {}
    half3 = far_half(after(pick(s ^ 3, w_held), *p_parts))
    chips3 = all_chips(half3)
    kernels[3] = both_cores(chips3)
    field3 = spread(
        call(
            functools.partial(first_body, per, sub),
            [jax.ShapeDtypeStruct((rows, width), BF16)] * 4,
            (ids, up, pick(s ^ 3, p_held), inputs), 6.0,
        )
    )
    x_held = [x[half:] for x in field3]
    half2 = far_half(after(pick(s ^ 2, w_held), half3))
    up, g2 = back(3, field3, up)
    field2 = spread([g2] * 4)
    chips2 = all_chips(half2, g2)
    kernels[2] = both_cores(chips2)
    half1 = far_half(after(pick(s ^ 1, w_held), chips3), g2)
    terms3 = terms(tied(field3, g2), pick(s ^ 3, x_held))
    up, g1 = back(2, tied(field2, terms3), up)
    field1 = spread([g1] * 4)
    chips1 = all_chips(half1, g1)
    kernels[1] = both_cores(chips1)
    terms3 = paired(*tied(terms3, g1))
    terms2 = terms(tied(field2, g1), pick(s ^ 2, x_held))
    up, g0 = back(1, tied(field1, terms2, terms3), up)
    field0 = spread([g0] * 4)
    terms3 = reduced(*terms3, g0)
    terms2 = paired(*tied(terms2, g0))
    terms1 = terms(tied(field1, g0), pick(s ^ 1, x_held))
    terms0 = terms(tied(field0, terms1, terms2, terms3), pick(s, x_held))
    terms1 = paired(*terms1)
    terms0 = paired(*terms0)
    sums = [
        summed(*terms3), summed(*reduced(*terms2)), summed(*reduced(*terms1)), summed(*reduced(*terms0))
    ][::-1]
    owned = spread(
        call(sums_body, [array(BF16)] * 4, (ids, *sums[0], *sums[1], *sums[2], *sums[3]), 0.7)
    )
    rate = 1.0 / math.sqrt(n_dp * rows)
    updated = call(
        functools.partial(update_body, per, sub, rate),
        jax.ShapeDtypeStruct((27, per, channels), F32),
        (ids, *owned, by_tap(momentum), by_tap(noise)), 2.0,
    )
    return jnp.swapaxes(updated, 0, 1)[None]


def solution(mesh):
    placed = (
        P("segment", "dp", None, None, None, None),
        P("segment", "dp", None, None, None, None),
        P("dp", None, None, None, None),
        P("segment", "dp", None, None),
        P("segment", "dp", None, None),
        P("segment", "dp", None, None),
    )

    def shards(activations, preacts, out_grad, weights, momentum, noise):
        channels = weights.shape[-1]
        n_dp = mesh.shape["dp"]
        fits = (
            mesh.shape["segment"] == 4
            and channels % (32 * n_dp) == 0
            and n_dp == 8
            and out_grad.shape[3] == 8
        )
        plan = quartered_shards if fits else general_shards
        return plan(activations, preacts, out_grad, weights, momentum, noise)

    return jax.shard_map(
        shards,
        mesh=mesh,
        in_specs=placed,
        out_specs=P("segment", "dp", None, None),
        check_vma=False,
    )
```

time: 172 us -> 123 us (0.72)
  starting transfers between devices: 78.4 us -> 46.8 us
  waiting for transfers between devices: 60.8 us -> 42.8 us
  Pallas kernels: 26.8 us -> 30.4 us
  local copies, waits for them, and re-layouts: 4.39 us -> 1.19 us
    ppermute x49 -> x42, starting transfers between devices: 78.4 us -> 46.8 us  [swapped(): lax.ppermute(x, axis, [(i, i ^ mask) for i in range(lax.axis_size(axis))])]
    ppermute x49 -> x42, waiting for transfers between devices: 60.8 us -> 42.8 us  [swapped(): lax.ppermute(x, axis, [(i, i ^ mask) for i in range(lax.axis_size(axis))])]
    pallas_call x15 -> x20, Pallas kernels: 26.8 us -> 30.4 us  [call(): pl.pallas_call(body, out_shape=out_shape, in_specs=[pl.BlockSpec(memory_s...]
  transfers between devices with their start and end apart: 49 -> 42, of which waited for: 22 -> 18; matrix products, arithmetic and copies ran while one was open for 1% -> 0% of each run, Pallas kernels for 13% -> 19%
where the time goes in v2:
time: 123 us; the launch traced here: 122 us
  starting transfers between devices  46.8 us (38%)
  waiting for transfers between devices  42.8 us (35%)
  Pallas kernels  30.4 us (25%)
    ppermute x42, starting transfers between devices, swapped(): lax.ppermute(x, axis, [(i, i ^ mask) for i in range(lax.axis_size(axis))])  46.8 us
    ppermute x42, waiting for transfers between devices, swapped(): lax.ppermute(x, axis, [(i, i ^ mask) for i in range(lax.axis_size(axis))])  42.8 us
    pallas_call x20, Pallas kernels, call(): pl.pallas_call(body, out_shape=out_shape, in_specs=[pl.BlockSpec(memory_s...  30.4 us
  transfers between devices with their start and end apart: 42, of which 18 were waited for; matrix products, arithmetic and copies ran while one was open for 0% of the time, Pallas kernels for 19%

profile of v2, /device:TPU:0, one launch (start us, length us, event | category | flops | bytes accessed | tf_op | source)
XLA Modules:
  0.0 122.4 jit_solution(15420428668761161302)
XLA Ops:
  2.1 3.0 %collective-permute-start.6 = (bf16[24,2304]{1,0:T(8,128)(2,1)S(1)}, bf16[24,2304]{1,0:T(8,128)(2,1)S(1)}, u32[]{:S(2)}, u32[]{:S(2)}) collective-permute-start(bf16[24,2304]{1,0:T(8,128)(2,1)S(1)} %get-tuple-element.96), channel_id=1, source_target_pairs={{0,8},{8,0},{16,24},{24,16},{1,9},{9,1},{17,25},{25,17},{2,10},{10... | collective-permute-start | bytes 331784 | tf_op jit(solution)/shard_map/ppermute | solution.py:24
  7.8 2.0 %collective-permute-start = (bf16[512,128]{1,0:T(8,128)(2,1)S(1)}, bf16[512,128]{1,0:T(8,128)(2,1)S(1)}, u32[]{:S(2)}, u32[]{:S(2)}) collective-permute-start(bf16[512,128]{1,0:T(8,128)(2,1)S(1)} %get-tuple-element.88), channel_id=1, source_target_pairs={{0,8},{8,0},{16,24},{24,16},{1,9},{9,1},{17,25},{25,17},{2,10},{10... | collective-permute-start | bytes 393224 | tf_op jit(solution)/shard_map/ppermute | solution.py:24
  13.5 2.7 %collective-permute-start.9 = (bf16[24,2304]{1,0:T(8,128)(2,1)S(1)}, bf16[24,2304]{1,0:T(8,128)(2,1)S(1)}, u32[]{:S(2)}, u32[]{:S(2)}) collective-permute-start(bf16[24,2304]{1,0:T(8,128)(2,1)S(1)} %get-tuple-element.99), channel_id=1, source_target_pairs={{0,4},{1,5},{2,6},{3,7},{4,0},{5,1},{6,2},{7,3},{8,12},{9,13},{10,... | collective-permute-start | bytes 331784 | tf_op jit(solution)/shard_map/ppermute | solution.py:24
  18.0 2.5 %collective-permute-done.9 = bf16[24,2304]{1,0:T(8,128)(2,1)S(1)} collective-permute-done((bf16[24,2304]{1,0:T(8,128)(2,1)S(1)}, bf16[24,2304]{1,0:T(8,128)(2,1)S(1)}, u32[]{:S(2)}, u32[]{:S(2)}) %collective-permute-start.9) | collective-permute-done | bytes 110624 | tf_op jit(solution)/shard_map/ppermute | solution.py:24
  21.2 3.6 %collective-permute-start.15 = (bf16[24,2304]{1,0:T(8,128)(2,1)S(1)}, bf16[24,2304]{1,0:T(8,128)(2,1)S(1)}, u32[]{:S(2)}, u32[]{:S(2)}) collective-permute-start(bf16[24,2304]{1,0:T(8,128)(2,1)S(1)} %get-tuple-element.111), channel_id=1, source_target_pairs={{0,4},{1,5},{2,6},{3,7},{4,0},{5,1},{6,2},{7,3},{8,12},{9,13},{10,... | collective-permute-start | bytes 331784 | tf_op jit(solution)/shard_map/ppermute | solution.py:24
  27.1 2.3 %collective-permute-start.5 = (bf16[1024,128]{1,0:T(8,128)(2,1)S(1)}, bf16[1024,128]{1,0:T(8,128)(2,1)S(1)}, u32[]{:S(2)}, u32[]{:S(2)}) collective-permute-start(bf16[1024,128]{1,0:T(8,128)(2,1)S(1)} %get-tuple-element.94), channel_id=1, source_target_pairs={{0,24},{8,16},{16,8},{24,0},{1,25},{9,17},{17,9},{25,1},{2,26},{10... | collective-permute-start | bytes 786440 | tf_op jit(solution)/shard_map/ppermute | solution.py:24
  30.1 2.5 %collective-permute-done.3.g1 = bf16[1024,128]{1,0:T(8,128)(2,1)S(1)} collective-permute-done((bf16[1024,128]{1,0:T(8,128)(2,1)S(1)}, bf16[1024,128]{1,0:T(8,128)(2,1)S(1)}, u32[]{:S(2)}, u32[]{:S(2)}) %collective-permute-start.3) | collective-permute-done | bytes 262176 | tf_op jit(solution)/shard_map/ppermute | solution.py:24
  32.6 4.2 %collective-permute-done.4.g2 = bf16[1024,128]{1,0:T(8,128)(2,1)S(1)} collective-permute-done((bf16[1024,128]{1,0:T(8,128)(2,1)S(1)}, bf16[1024,128]{1,0:T(8,128)(2,1)S(1)}, u32[]{:S(2)}, u32[]{:S(2)}) %collective-permute-start.4) | collective-permute-done | bytes 262176 | tf_op jit(solution)/shard_map/ppermute | solution.py:24
  37.3 2.9 %shard_map.67 = (bf16[512,128]{1,0:T(8,128)(2,1)S(1)}, bf16[512,128]{1,0:T(8,128)(2,1)S(1)}) custom-call(s32[2]{0:T(128)S(1)} %pad_add_fusion.ids, bf16[1024,128]{1,0:T(8,128)(2,1)S(1)} %get-tuple-element.101.g0, bf16[1024,128]{1,0:T(8,128)(2,1)S(1)} %collective-permute-done.3.g1, bf16[1024,128]{1,0:T(8,128)(2,1)S(1)} %collective-permute-done.4.g2, ...), custom_call_target="tpu_custom_call" | custom-call | flops 3460499968 | tf_op jit(solution)/shard_map/pallas_call | solution.py:104
  45.0 2.6 %shard_map.68 = (f32[4,24,2304]{2,1,0:T(8,128)S(1)}, bf16[4,24,2304]{2,1,0:T(8,128)(2,1)S(1)}) custom-call(s32[2]{0:T(128)S(1)} %pad_add_fusion.ids, bf16[1024,128]{1,0:T(8,128)(2,1)S(1)} %get-tuple-element.101.g0, bf16[1024,128]{1,0:T(8,128)(2,1)S(1)} %collective-permute-done.3.g1, bf16[1024,128]{1,0:T(8,128)(2,1)S(1)} %collective-permute-done.4.g2, ...), custom_call_target="tpu_custom_call" | custom-call | flops 2999099904 | tf_op jit(solution)/shard_map/pallas_call | solution.py:104
  47.8 2.9 %shard_map.69 = (bf16[512,128]{1,0:T(8,128)(2,1)S(1)}, bf16[512,128]{1,0:T(8,128)(2,1)S(1)}) custom-call(s32[2]{0:T(128)S(1)} %pad_add_fusion.ids, bf16[512,128]{1,0:T(8,128)(2,1)S(1)} %get-tuple-element.115.g0, bf16[512,128]{1,0:T(8,128)(2,1)S(1)} %collective-permute-done.12.g1, bf16[512,128]{1,0:T(8,128)(2,1)S(1)} %collective-permute-done.13.g2, ...), custom_call_target="tpu_custom_call" | custom-call | flops 3460499968 | tf_op jit(solution)/shard_map/pallas_call | solution.py:104
  56.1 2.6 %shard_map.70 = (f32[4,24,2304]{2,1,0:T(8,128)S(1)}, bf16[4,24,2304]{2,1,0:T(8,128)(2,1)S(1)}) custom-call(s32[2]{0:T(128)S(1)} %pad_add_fusion.ids, bf16[512,128]{1,0:T(8,128)(2,1)S(1)} %get-tuple-element.115.g0, bf16[512,128]{1,0:T(8,128)(2,1)S(1)} %collective-permute-done.12.g1, bf16[512,128]{1,0:T(8,128)(2,1)S(1)} %collective-permute-done.13.g2, ...), custom_call_target="tpu_custom_call" | custom-call | flops 2999099904 | tf_op jit(solution)/shard_map/pallas_call | solution.py:104
  62.1 3.6 %shard_map.72 = (bf16[512,128]{1,0:T(8,128)(2,1)}, bf16[512,128]{1,0:T(8,128)(2,1)S(1)}) custom-call(s32[2]{0:T(128)S(1)} %pad_add_fusion.ids, bf16[512,128]{1,0:T(8,128)(2,1)S(1)} %get-tuple-element.134.g0, bf16[512,128]{1,0:T(8,128)(2,1)S(1)} %collective-permute-done.18.g1, bf16[512,128]{1,0:T(8,128)(2,1)S(1)} %collective-permute-done.19.g2, ...), custom_call_target="tpu_custom_call" | custom-call | flops 3460499968 | tf_op jit(solution)/shard_map/pallas_call | solution.py:104
  70.0 2.6 %shard_map.73 = (f32[4,24,2304]{2,1,0:T(8,128)S(1)}, bf16[4,24,2304]{2,1,0:T(8,128)(2,1)S(1)}) custom-call(s32[2]{0:T(128)S(1)} %pad_add_fusion.ids, bf16[512,128]{1,0:T(8,128)(2,1)S(1)} %get-tuple-element.134.g0, bf16[512,128]{1,0:T(8,128)(2,1)S(1)} %collective-permute-done.18.g1, bf16[512,128]{1,0:T(8,128)(2,1)S(1)} %collective-permute-done.19.g2, ...), custom_call_target="tpu_custom_call" | custom-call | flops 2999099904 | tf_op jit(solution)/shard_map/pallas_call | solution.py:104
  75.8 2.6 %shard_map.76 = (f32[4,24,2304]{2,1,0:T(8,128)S(1)}, bf16[4,24,2304]{2,1,0:T(8,128)(2,1)S(1)}) custom-call(s32[2]{0:T(128)S(1)} %pad_add_fusion.ids, bf16[512,128]{1,0:T(8,128)(2,1)S(1)} %get-tuple-element.147.g0, bf16[512,128]{1,0:T(8,128)(2,1)S(1)} %collective-permute-done.25.g1, bf16[512,128]{1,0:T(8,128)(2,1)S(1)} %collective-permute-done.26.g2, ...), custom_call_target="tpu_custom_call" | custom-call | flops 2999099904 | tf_op jit(solution)/shard_map/pallas_call | solution.py:104
  83.3 2.6 %collective-permute-start.38 = (bf16[24,2304]{1,0:T(8,128)(2,1)S(1)}, bf16[24,2304]{1,0:T(8,128)(2,1)S(1)}, u32[]{:S(2)}, u32[]{:S(2)}) collective-permute-start(bf16[24,2304]{1,0:T(8,128)(2,1)S(1)} %get-tuple-element.146), channel_id=1, source_target_pairs={{0,4},{1,5},{2,6},{3,7},{4,0},{5,1},{6,2},{7,3},{8,12},{9,13},{10,... | collective-permute-start | bytes 331784 | tf_op jit(solution)/shard_map/ppermute | solution.py:24
  85.9 3.3 %collective-permute-done.36.other = bf16[2,24,2304]{2,1,0:T(8,128)(2,1)S(1)} collective-permute-done((bf16[2,24,2304]{2,1,0:T(8,128)(2,1)S(1)}, bf16[2,24,2304]{2,1,0:T(8,128)(2,1)S(1)}, u32[]{:S(2)}, u32[]{:S(2)}) %collective-permute-start.36) | collective-permute-done | bytes 221216 | tf_op jit(solution)/shard_map/ppermute | solution.py:24
  91.2 5.1 %collective-permute-done.34.other = bf16[2,24,2304]{2,1,0:T(8,128)(2,1)S(1)} collective-permute-done((bf16[2,24,2304]{2,1,0:T(8,128)(2,1)S(1)}, bf16[2,24,2304]{2,1,0:T(8,128)(2,1)S(1)}, u32[]{:S(2)}, u32[]{:S(2)}) %collective-permute-start.34) | collective-permute-done | bytes 221216 | tf_op jit(solution)/shard_map/ppermute | solution.py:24
  98.2 2.5 %collective-permute-done.31.other = bf16[2,24,2304]{2,1,0:T(8,128)(2,1)S(1)} collective-permute-done((bf16[2,24,2304]{2,1,0:T(8,128)(2,1)S(1)}, bf16[2,24,2304]{2,1,0:T(8,128)(2,1)S(1)}, u32[]{:S(2)}, u32[]{:S(2)}) %collective-permute-start.31) | collective-permute-done | bytes 221216 | tf_op jit(solution)/shard_map/ppermute | solution.py:24
  102.7 6.7 %collective-permute-done.35.refs_3_ = bf16[24,2304]{1,0:T(8,128)(2,1)S(1)} collective-permute-done((bf16[24,2304]{1,0:T(8,128)(2,1)S(1)}, bf16[24,2304]{1,0:T(8,128)(2,1)S(1)}, u32[]{:S(2)}, u32[]{:S(2)}) %collective-permute-start.35) | collective-permute-done | bytes 110624 | tf_op jit(solution)/shard_map/ppermute | solution.py:24
  109.4 2.3 %collective-permute-done.32.refs_1_ = bf16[24,2304]{1,0:T(8,128)(2,1)S(1)} collective-permute-done((bf16[24,2304]{1,0:T(8,128)(2,1)S(1)}, bf16[24,2304]{1,0:T(8,128)(2,1)S(1)}, u32[]{:S(2)}, u32[]{:S(2)}) %collective-permute-start.32) | collective-permute-done | bytes 110624 | tf_op jit(solution)/shard_map/ppermute | solution.py:24
  116.0 2.1 %collective-permute-done.39.f1 = bf16[24,2304]{1,0:T(8,128)(2,1)S(1)} collective-permute-done((bf16[24,2304]{1,0:T(8,128)(2,1)S(1)}, bf16[24,2304]{1,0:T(8,128)(2,1)S(1)}, u32[]{:S(2)}, u32[]{:S(2)}) %collective-permute-start.39) | collective-permute-done | bytes 110624 | tf_op jit(solution)/shard_map/ppermute | solution.py:24
  118.1 2.4 %collective-permute-done.40.f2 = bf16[24,2304]{1,0:T(8,128)(2,1)S(1)} collective-permute-done((bf16[24,2304]{1,0:T(8,128)(2,1)S(1)}, bf16[24,2304]{1,0:T(8,128)(2,1)S(1)}, u32[]{:S(2)}, u32[]{:S(2)}) %collective-permute-start.40) | collective-permute-done | bytes 110624 | tf_op jit(solution)/shard_map/ppermute | solution.py:24
  120.4 1.9 %shard_map.83 = f32[27,32,256]{2,1,0:T(8,128)} custom-call(s32[2]{0:T(128)S(1)} %pad_add_fusion.ids, bf16[24,2304]{1,0:T(8,128)(2,1)S(1)} %get-tuple-element.163.f0, bf16[24,2304]{1,0:T(8,128)(2,1)S(1)} %collective-permute-done.39.f1, bf16[24,2304]{1,0:T(8,128)(2,1)S(1)} %collective-permute-done.40.f2, bf16[24,2304]{1,0:T(8,128)(2,1)S(1)} %collective-permute-done.41.f3, ...), custom_call_target="tpu_custom_call" | custom-call | flops 2307000064 | tf_op jit(solution)/shard_map/pallas_call | solution.py:104
  (106 shorter events, 50.6 us)
Async XLA Ops:
  2.1 9.2 %collective-permute-start.6 = (bf16[24,2304]{1,0:T(8,128)(2,1)S(1)}, bf16[24,2304]{1,0:T(8,128)(2,1)S(1)}, u32[]{:S(2)}, u32[]{:S(2)}) collective-permute-start(bf16[24,2304]{1,0:T(8,128)(2,1)S(1)} %get-tuple-element.96), channel_id=1, source_target_pairs={{0,8},{8,0},{16,24},{24,16},{1,9},{9,1},{17,25},{25,17},{2,10},{10... | collective-permute-start | bytes 331784 | tf_op jit(solution)/shard_map/ppermute | solution.py:24
  7.8 8.4 %collective-permute-start = (bf16[512,128]{1,0:T(8,128)(2,1)S(1)}, bf16[512,128]{1,0:T(8,128)(2,1)S(1)}, u32[]{:S(2)}, u32[]{:S(2)}) collective-permute-start(bf16[512,128]{1,0:T(8,128)(2,1)S(1)} %get-tuple-element.88), channel_id=1, source_target_pairs={{0,8},{8,0},{16,24},{24,16},{1,9},{9,1},{17,25},{25,17},{2,10},{10... | collective-permute-start | bytes 393224 | tf_op jit(solution)/shard_map/ppermute | solution.py:24
  9.8 8.1 %collective-permute-start.1 = (bf16[512,128]{1,0:T(8,128)(2,1)S(1)}, bf16[512,128]{1,0:T(8,128)(2,1)S(1)}, u32[]{:S(2)}, u32[]{:S(2)}) collective-permute-start(bf16[512,128]{1,0:T(8,128)(2,1)S(1)} %get-tuple-element.89), channel_id=1, source_target_pairs={{0,16},{8,24},{16,0},{24,8},{1,17},{9,25},{17,1},{25,9},{2,18},{10... | collective-permute-start | bytes 393224 | tf_op jit(solution)/shard_map/ppermute | solution.py:24
  20.6 8.9 %collective-permute-start.10 = (bf16[2,24,2304]{2,1,0:T(8,128)(2,1)S(1)}, bf16[2,24,2304]{2,1,0:T(8,128)(2,1)S(1)}, u32[]{:S(2)}, u32[]{:S(2)}) collective-permute-start(bf16[2,24,2304]{2,1,0:T(8,128)(2,1)S(1)} %pad_maximum_fusion.6), channel_id=1, source_target_pairs={{0,2},{1,3},{2,0},{3,1},{4,6},{5,7},{6,4},{7,5},{8,10},{9,11},{10,... | collective-permute-start | bytes 663560 | tf_op jit(solution)/shard_map/ppermute | solution.py:24
  21.2 8.2 %collective-permute-start.15 = (bf16[24,2304]{1,0:T(8,128)(2,1)S(1)}, bf16[24,2304]{1,0:T(8,128)(2,1)S(1)}, u32[]{:S(2)}, u32[]{:S(2)}) collective-permute-start(bf16[24,2304]{1,0:T(8,128)(2,1)S(1)} %get-tuple-element.111), channel_id=1, source_target_pairs={{0,4},{1,5},{2,6},{3,7},{4,0},{5,1},{6,2},{7,3},{8,12},{9,13},{10,... | collective-permute-start | bytes 331784 | tf_op jit(solution)/shard_map/ppermute | solution.py:24
  26.3 10.5 %collective-permute-start.4 = (bf16[1024,128]{1,0:T(8,128)(2,1)S(1)}, bf16[1024,128]{1,0:T(8,128)(2,1)S(1)}, u32[]{:S(2)}, u32[]{:S(2)}) collective-permute-start(bf16[1024,128]{1,0:T(8,128)(2,1)S(1)} %get-tuple-element.93), channel_id=1, source_target_pairs={{0,16},{8,24},{16,0},{24,8},{1,17},{9,25},{17,1},{25,9},{2,18},{10... | collective-permute-start | bytes 786440 | tf_op jit(solution)/shard_map/ppermute | solution.py:24
  27.1 9.7 %collective-permute-start.5 = (bf16[1024,128]{1,0:T(8,128)(2,1)S(1)}, bf16[1024,128]{1,0:T(8,128)(2,1)S(1)}, u32[]{:S(2)}, u32[]{:S(2)}) collective-permute-start(bf16[1024,128]{1,0:T(8,128)(2,1)S(1)} %get-tuple-element.94), channel_id=1, source_target_pairs={{0,24},{8,16},{16,8},{24,0},{1,25},{9,17},{17,9},{25,1},{2,26},{10... | collective-permute-start | bytes 786440 | tf_op jit(solution)/shard_map/ppermute | solution.py:24
  29.5 7.7 %collective-permute-start.11 = (bf16[4,24,2304]{2,1,0:T(8,128)(2,1)S(1)}, bf16[4,24,2304]{2,1,0:T(8,128)(2,1)S(1)}, u32[]{:S(2)}, u32[]{:S(2)}) collective-permute-start(bf16[4,24,2304]{2,1,0:T(8,128)(2,1)S(1)} %pad_maximum_fusion.3), channel_id=1, source_target_pairs={{0,1},{1,0},{2,3},{3,2},{4,5},{5,4},{6,7},{7,6},{8,9},{9,8},{10,11... | collective-permute-start | bytes 1327112 | tf_op jit(solution)/shard_map/ppermute | solution.py:24
  29.6 14.2 %collective-permute-start.16 = (bf16[2,24,2304]{2,1,0:T(8,128)(2,1)S(1)}, bf16[2,24,2304]{2,1,0:T(8,128)(2,1)S(1)}, u32[]{:S(2)}, u32[]{:S(2)}) collective-permute-start(bf16[2,24,2304]{2,1,0:T(8,128)(2,1)S(1)} %pad_maximum_fusion.7), channel_id=1, source_target_pairs={{0,2},{1,3},{2,0},{3,1},{4,6},{5,7},{6,4},{7,5},{8,10},{9,11},{10,... | collective-permute-start | bytes 663560 | tf_op jit(solution)/shard_map/ppermute | solution.py:24
  44.0 7.9 %collective-permute-start.23 = (bf16[2,24,2304]{2,1,0:T(8,128)(2,1)S(1)}, bf16[2,24,2304]{2,1,0:T(8,128)(2,1)S(1)}, u32[]{:S(2)}, u32[]{:S(2)}) collective-permute-start(bf16[2,24,2304]{2,1,0:T(8,128)(2,1)S(1)} %pad_maximum_fusion.8), channel_id=1, source_target_pairs={{0,2},{1,3},{2,0},{3,1},{4,6},{5,7},{6,4},{7,5},{8,10},{9,11},{10,... | collective-permute-start | bytes 663560 | tf_op jit(solution)/shard_map/ppermute | solution.py:24
  51.9 9.9 %collective-permute-start.24 = (bf16[4,24,2304]{2,1,0:T(8,128)(2,1)S(1)}, bf16[4,24,2304]{2,1,0:T(8,128)(2,1)S(1)}, u32[]{:S(2)}, u32[]{:S(2)}) collective-permute-start(bf16[4,24,2304]{2,1,0:T(8,128)(2,1)S(1)} %pad_maximum_fusion.5), channel_id=1, source_target_pairs={{0,1},{1,0},{2,3},{3,2},{4,5},{5,4},{6,7},{7,6},{8,9},{9,8},{10,11... | collective-permute-start | bytes 1327112 | tf_op jit(solution)/shard_map/ppermute | solution.py:24
  52.6 7.3 %collective-permute-start.20 = (bf16[512,128]{1,0:T(8,128)(2,1)S(1)}, bf16[512,128]{1,0:T(8,128)(2,1)S(1)}, u32[]{:S(2)}, u32[]{:S(2)}) collective-permute-start(bf16[512,128]{1,0:T(8,128)(2,1)S(1)} %get-tuple-element.134.g0), channel_id=1, source_target_pairs={{0,24},{8,16},{16,8},{24,0},{1,25},{9,17},{17,9},{25,1},{2,26},{10... | collective-permute-start | bytes 393224 | tf_op jit(solution)/shard_map/ppermute | solution.py:24
  54.0 7.8 %collective-permute-start.19 = (bf16[512,128]{1,0:T(8,128)(2,1)S(1)}, bf16[512,128]{1,0:T(8,128)(2,1)S(1)}, u32[]{:S(2)}, u32[]{:S(2)}) collective-permute-start(bf16[512,128]{1,0:T(8,128)(2,1)S(1)} %get-tuple-element.134.g0), channel_id=1, source_target_pairs={{0,16},{8,24},{16,0},{24,8},{1,17},{9,25},{17,1},{25,9},{2,18},{10... | collective-permute-start | bytes 393224 | tf_op jit(solution)/shard_map/ppermute | solution.py:24
  65.7 8.4 %collective-permute-start.28 = (bf16[4,24,2304]{2,1,0:T(8,128)(2,1)S(1)}, bf16[4,24,2304]{2,1,0:T(8,128)(2,1)S(1)}, u32[]{:S(2)}, u32[]{:S(2)}) collective-permute-start(bf16[4,24,2304]{2,1,0:T(8,128)(2,1)S(1)} %get-tuple-element.141), channel_id=1, source_target_pairs={{0,1},{1,0},{2,3},{3,2},{4,5},{5,4},{6,7},{7,6},{8,9},{9,8},{10,11... | collective-permute-start | bytes 1327112 | tf_op jit(solution)/shard_map/ppermute | solution.py:24
  65.7 7.8 %collective-permute-start.29 = (bf16[2,24,2304]{2,1,0:T(8,128)(2,1)S(1)}, bf16[2,24,2304]{2,1,0:T(8,128)(2,1)S(1)}, u32[]{:S(2)}, u32[]{:S(2)}) collective-permute-start(bf16[2,24,2304]{2,1,0:T(8,128)(2,1)S(1)} %get-tuple-element.124), channel_id=1, source_target_pairs={{0,2},{1,3},{2,0},{3,1},{4,6},{5,7},{6,4},{7,5},{8,10},{9,11},{10,... | collective-permute-start | bytes 663560 | tf_op jit(solution)/shard_map/ppermute | solution.py:24
  66.5 8.3 %collective-permute-start.27 = (bf16[512,128]{1,0:T(8,128)(2,1)S(1)}, bf16[512,128]{1,0:T(8,128)(2,1)S(1)}, u32[]{:S(2)}, u32[]{:S(2)}) collective-permute-start(bf16[512,128]{1,0:T(8,128)(2,1)S(1)} %get-tuple-element.147.g0), channel_id=1, source_target_pairs={{0,24},{8,16},{16,8},{24,0},{1,25},{9,17},{17,9},{25,1},{2,26},{10... | collective-permute-start | bytes 393224 | tf_op jit(solution)/shard_map/ppermute | solution.py:24
  67.7 8.1 %collective-permute-start.26 = (bf16[512,128]{1,0:T(8,128)(2,1)S(1)}, bf16[512,128]{1,0:T(8,128)(2,1)S(1)}, u32[]{:S(2)}, u32[]{:S(2)}) collective-permute-start(bf16[512,128]{1,0:T(8,128)(2,1)S(1)} %get-tuple-element.147.g0), channel_id=1, source_target_pairs={{0,16},{8,24},{16,0},{24,8},{1,17},{9,25},{17,1},{25,9},{2,18},{10... | collective-permute-start | bytes 393224 | tf_op jit(solution)/shard_map/ppermute | solution.py:24
  78.5 10.7 %collective-permute-start.36 = (bf16[2,24,2304]{2,1,0:T(8,128)(2,1)S(1)}, bf16[2,24,2304]{2,1,0:T(8,128)(2,1)S(1)}, u32[]{:S(2)}, u32[]{:S(2)}) collective-permute-start(bf16[2,24,2304]{2,1,0:T(8,128)(2,1)S(1)} %get-tuple-element.143), channel_id=1, source_target_pairs={{0,2},{1,3},{2,0},{3,1},{4,6},{5,7},{6,4},{7,5},{8,10},{9,11},{10,... | collective-permute-start | bytes 663560 | tf_op jit(solution)/shard_map/ppermute | solution.py:24
  80.5 15.8 %collective-permute-start.34 = (bf16[2,24,2304]{2,1,0:T(8,128)(2,1)S(1)}, bf16[2,24,2304]{2,1,0:T(8,128)(2,1)S(1)}, u32[]{:S(2)}, u32[]{:S(2)}) collective-permute-start(bf16[2,24,2304]{2,1,0:T(8,128)(2,1)S(1)} %get-tuple-element.158), channel_id=1, source_target_pairs={{0,2},{1,3},{2,0},{3,1},{4,6},{5,7},{6,4},{7,5},{8,10},{9,11},{10,... | collective-permute-start | bytes 663560 | tf_op jit(solution)/shard_map/ppermute | solution.py:24
  82.0 18.7 %collective-permute-start.31 = (bf16[2,24,2304]{2,1,0:T(8,128)(2,1)S(1)}, bf16[2,24,2304]{2,1,0:T(8,128)(2,1)S(1)}, u32[]{:S(2)}, u32[]{:S(2)}) collective-permute-start(bf16[2,24,2304]{2,1,0:T(8,128)(2,1)S(1)} %get-tuple-element.154), channel_id=1, source_target_pairs={{0,2},{1,3},{2,0},{3,1},{4,6},{5,7},{6,4},{7,5},{8,10},{9,11},{10,... | collective-permute-start | bytes 663560 | tf_op jit(solution)/shard_map/ppermute | solution.py:24
  83.3 19.5 %collective-permute-start.38 = (bf16[24,2304]{1,0:T(8,128)(2,1)S(1)}, bf16[24,2304]{1,0:T(8,128)(2,1)S(1)}, u32[]{:S(2)}, u32[]{:S(2)}) collective-permute-start(bf16[24,2304]{1,0:T(8,128)(2,1)S(1)} %get-tuple-element.146), channel_id=1, source_target_pairs={{0,4},{1,5},{2,6},{3,7},{4,0},{5,1},{6,2},{7,3},{8,12},{9,13},{10,... | collective-permute-start | bytes 331784 | tf_op jit(solution)/shard_map/ppermute | solution.py:24
  89.8 13.0 %collective-permute-start.37 = (bf16[24,2304]{1,0:T(8,128)(2,1)S(1)}, bf16[24,2304]{1,0:T(8,128)(2,1)S(1)}, u32[]{:S(2)}, u32[]{:S(2)}) collective-permute-start(bf16[24,2304]{1,0:T(8,128)(2,1)S(1)} %get-tuple-element.162), channel_id=1, source_target_pairs={{0,4},{1,5},{2,6},{3,7},{4,0},{5,1},{6,2},{7,3},{8,12},{9,13},{10,... | collective-permute-start | bytes 331784 | tf_op jit(solution)/shard_map/ppermute | solution.py:24
  96.9 12.5 %collective-permute-start.35 = (bf16[24,2304]{1,0:T(8,128)(2,1)S(1)}, bf16[24,2304]{1,0:T(8,128)(2,1)S(1)}, u32[]{:S(2)}, u32[]{:S(2)}) collective-permute-start(bf16[24,2304]{1,0:T(8,128)(2,1)S(1)} %get-tuple-element.160), channel_id=1, source_target_pairs={{0,4},{1,5},{2,6},{3,7},{4,0},{5,1},{6,2},{7,3},{8,12},{9,13},{10,... | collective-permute-start | bytes 331784 | tf_op jit(solution)/shard_map/ppermute | solution.py:24
  101.3 10.4 %collective-permute-start.32 = (bf16[24,2304]{1,0:T(8,128)(2,1)S(1)}, bf16[24,2304]{1,0:T(8,128)(2,1)S(1)}, u32[]{:S(2)}, u32[]{:S(2)}) collective-permute-start(bf16[24,2304]{1,0:T(8,128)(2,1)S(1)} %get-tuple-element.156), channel_id=1, source_target_pairs={{0,4},{1,5},{2,6},{3,7},{4,0},{5,1},{6,2},{7,3},{8,12},{9,13},{10,... | collective-permute-start | bytes 331784 | tf_op jit(solution)/shard_map/ppermute | solution.py:24
  (24 other events, 152.1 us)

commit v3 on v2

--- a/solution.py
+++ b/solution.py
@@ -12,6 +12,7 @@
 F32 = jnp.float32
 VMEM_BYTES = 48 * 1024 * 1024
 PEAK_PER_US = 1.1535e9
+WEIGHT = 10
 
 
 def shifted(x, axis, by):
@@ -110,7 +111,7 @@
         scratch_shapes=list(scratch),
         compiler_params=pltpu.CompilerParams(vmem_limit_bytes=VMEM_BYTES),
         cost_estimate=pl.CostEstimate(
-            flops=int(us * PEAK_PER_US), bytes_accessed=0, transcendentals=0
+            flops=int(us * WEIGHT * PEAK_PER_US), bytes_accessed=0, transcendentals=0
         ),
     )(*args)
 
@@ -459,9 +460,10 @@
     terms0 = terms(tied(field0, terms1, terms2, terms3), pick(s, x_held))
     terms1 = paired(*terms1)
     terms0 = paired(*terms0)
-    sums = [
-        summed(*terms3), summed(*reduced(*terms2)), summed(*reduced(*terms1)), summed(*reduced(*terms0))
-    ][::-1]
+    sum3 = summed(*terms3)
+    sum2 = summed(*reduced(*terms2, terms0))
+    sum1 = summed(*reduced(*terms1, terms0))
+    sums = [summed(*reduced(*terms0)), sum1, sum2, sum3]
     owned = spread(
         call(sums_body, [array(BF16)] * 4, (ids, *sums[0], *sums[1], *sums[2], *sums[3]), 0.7)
     )

time: 123 us -> 116 us (0.943)
  waiting for transfers between devices: 42.8 us -> 33.4 us
  starting transfers between devices: 46.8 us -> 49.3 us
    ppermute x42, waiting for transfers between devices: 42.8 us -> 33.4 us  [swapped(): lax.ppermute(x, axis, [(i, i ^ mask) for i in range(lax.axis_size(axis))])]
    ppermute x42, starting transfers between devices: 46.8 us -> 49.3 us  [swapped(): lax.ppermute(x, axis, [(i, i ^ mask) for i in range(lax.axis_size(axis))])]
  transfers between devices with their start and end apart: 42 -> 42, of which waited for: 18 -> 16; matrix products, arithmetic and copies ran while one was open for 0% -> 1% of each run, Pallas kernels for 19% -> 23%
where the time goes in v3:
time: 116 us; the launch traced here: 115 us
  starting transfers between devices  49.3 us (42%)
  waiting for transfers between devices  33.4 us (29%)
  Pallas kernels  30.4 us (26%)
  local copies, waits for them, and re-layouts  1.19 us (1%)
    ppermute x42, starting transfers between devices, swapped(): lax.ppermute(x, axis, [(i, i ^ mask) for i in range(lax.axis_size(axis))])  49.3 us
    ppermute x42, waiting for transfers between devices, swapped(): lax.ppermute(x, axis, [(i, i ^ mask) for i in range(lax.axis_size(axis))])  33.4 us
    pallas_call x20, Pallas kernels, call(): pl.pallas_call(body, out_shape=out_shape, in_specs=[pl.BlockSpec(memory_s...  30.4 us
  transfers between devices with their start and end apart: 42, of which 16 were waited for; matrix products, arithmetic and copies ran while one was open for 1% of the time, Pallas kernels for 23%

profile of v3, /device:TPU:0, one launch (start us, length us, event | category | flops | bytes accessed | tf_op | source)
XLA Modules:
  0.0 115.4 jit_solution(13996999947363311444)
XLA Ops:
  2.1 3.0 %collective-permute-start.6 = (bf16[24,2304]{1,0:T(8,128)(2,1)S(1)}, bf16[24,2304]{1,0:T(8,128)(2,1)S(1)}, u32[]{:S(2)}, u32[]{:S(2)}) collective-permute-start(bf16[24,2304]{1,0:T(8,128)(2,1)S(1)} %get-tuple-element.98), channel_id=1, source_target_pairs={{0,8},{8,0},{16,24},{24,16},{1,9},{9,1},{17,25},{25,17},{2,10},{10... | collective-permute-start | bytes 331784 | tf_op jit(solution)/shard_map/ppermute | solution.py:25
  7.8 2.0 %collective-permute-start = (bf16[512,128]{1,0:T(8,128)(2,1)S(1)}, bf16[512,128]{1,0:T(8,128)(2,1)S(1)}, u32[]{:S(2)}, u32[]{:S(2)}) collective-permute-start(bf16[512,128]{1,0:T(8,128)(2,1)S(1)} %get-tuple-element.90), channel_id=1, source_target_pairs={{0,8},{8,0},{16,24},{24,16},{1,9},{9,1},{17,25},{25,17},{2,10},{10... | collective-permute-start | bytes 393224 | tf_op jit(solution)/shard_map/ppermute | solution.py:25
  13.5 2.7 %collective-permute-start.9 = (bf16[24,2304]{1,0:T(8,128)(2,1)S(1)}, bf16[24,2304]{1,0:T(8,128)(2,1)S(1)}, u32[]{:S(2)}, u32[]{:S(2)}) collective-permute-start(bf16[24,2304]{1,0:T(8,128)(2,1)S(1)} %get-tuple-element.101), channel_id=1, source_target_pairs={{0,4},{1,5},{2,6},{3,7},{4,0},{5,1},{6,2},{7,3},{8,12},{9,13},{10,... | collective-permute-start | bytes 331784 | tf_op jit(solution)/shard_map/ppermute | solution.py:25
  16.2 1.7 %collective-permute-done.1 = bf16[512,128]{1,0:T(8,128)(2,1)S(1)} collective-permute-done((bf16[512,128]{1,0:T(8,128)(2,1)S(1)}, bf16[512,128]{1,0:T(8,128)(2,1)S(1)}, u32[]{:S(2)}, u32[]{:S(2)}) %collective-permute-start.1) | collective-permute-done | bytes 131104 | tf_op jit(solution)/shard_map/ppermute | solution.py:25
  18.0 2.4 %collective-permute-done.9 = bf16[24,2304]{1,0:T(8,128)(2,1)S(1)} collective-permute-done((bf16[24,2304]{1,0:T(8,128)(2,1)S(1)}, bf16[24,2304]{1,0:T(8,128)(2,1)S(1)}, u32[]{:S(2)}, u32[]{:S(2)}) %collective-permute-start.9) | collective-permute-done | bytes 110624 | tf_op jit(solution)/shard_map/ppermute | solution.py:25
  24.6 2.1 %collective-permute-start.5 = (bf16[1024,128]{1,0:T(8,128)(2,1)S(1)}, bf16[1024,128]{1,0:T(8,128)(2,1)S(1)}, u32[]{:S(2)}, u32[]{:S(2)}) collective-permute-start(bf16[1024,128]{1,0:T(8,128)(2,1)S(1)} %get-tuple-element.96), channel_id=1, source_target_pairs={{0,24},{8,16},{16,8},{24,0},{1,25},{9,17},{17,9},{25,1},{2,26},{10... | collective-permute-start | bytes 786440 | tf_op jit(solution)/shard_map/ppermute | solution.py:25
  26.7 4.3 %collective-permute-start.10 = (bf16[2,24,2304]{2,1,0:T(8,128)(2,1)S(1)}, bf16[2,24,2304]{2,1,0:T(8,128)(2,1)S(1)}, u32[]{:S(2)}, u32[]{:S(2)}) collective-permute-start(bf16[2,24,2304]{2,1,0:T(8,128)(2,1)S(1)} %pad_maximum_fusion.6), channel_id=1, source_target_pairs={{0,2},{1,3},{2,0},{3,1},{4,6},{5,7},{6,4},{7,5},{8,10},{9,11},{10,... | collective-permute-start | bytes 663560 | tf_op jit(solution)/shard_map/ppermute | solution.py:25
  31.1 3.8 %collective-permute-done.10 = bf16[2,24,2304]{2,1,0:T(8,128)(2,1)S(1)} collective-permute-done((bf16[2,24,2304]{2,1,0:T(8,128)(2,1)S(1)}, bf16[2,24,2304]{2,1,0:T(8,128)(2,1)S(1)}, u32[]{:S(2)}, u32[]{:S(2)}) %collective-permute-start.10) | collective-permute-done | bytes 221216 | tf_op jit(solution)/shard_map/ppermute | solution.py:25
  36.9 2.9 %shard_map.67 = (bf16[512,128]{1,0:T(8,128)(2,1)S(1)}, bf16[512,128]{1,0:T(8,128)(2,1)S(1)}) custom-call(s32[2]{0:T(128)S(1)} %pad_add_fusion.ids, bf16[1024,128]{1,0:T(8,128)(2,1)S(1)} %get-tuple-element.103.g0, bf16[1024,128]{1,0:T(8,128)(2,1)S(1)} %collective-permute-done.3.g1, bf16[1024,128]{1,0:T(8,128)(2,1)S(1)} %collective-permute-done.4.g2, ...), custom_call_target="tpu_custom_call" | custom-call | flops 34604998656 | tf_op jit(solution)/shard_map/pallas_call | solution.py:105
  41.6 1.8 %collective-permute-start.12 = (bf16[512,128]{1,0:T(8,128)(2,1)S(1)}, bf16[512,128]{1,0:T(8,128)(2,1)S(1)}, u32[]{:S(2)}, u32[]{:S(2)}) collective-permute-start(bf16[512,128]{1,0:T(8,128)(2,1)S(1)} %get-tuple-element.117.g0), channel_id=1, source_target_pairs={{0,8},{8,0},{16,24},{24,16},{1,9},{9,1},{17,25},{25,17},{2,10},{10... | collective-permute-start | bytes 393224 | tf_op jit(solution)/shard_map/ppermute | solution.py:25
  45.7 2.6 %shard_map.68 = (f32[4,24,2304]{2,1,0:T(8,128)S(1)}, bf16[4,24,2304]{2,1,0:T(8,128)(2,1)S(1)}) custom-call(s32[2]{0:T(128)S(1)} %pad_add_fusion.ids, bf16[1024,128]{1,0:T(8,128)(2,1)S(1)} %get-tuple-element.103.g0, bf16[1024,128]{1,0:T(8,128)(2,1)S(1)} %collective-permute-done.3.g1, bf16[1024,128]{1,0:T(8,128)(2,1)S(1)} %collective-permute-done.4.g2, ...), custom_call_target="tpu_custom_call" | custom-call | flops 29991000064 | tf_op jit(solution)/shard_map/pallas_call | solution.py:105
  48.5 2.9 %shard_map.69 = (bf16[512,128]{1,0:T(8,128)(2,1)S(1)}, bf16[512,128]{1,0:T(8,128)(2,1)S(1)}) custom-call(s32[2]{0:T(128)S(1)} %pad_add_fusion.ids, bf16[512,128]{1,0:T(8,128)(2,1)S(1)} %get-tuple-element.117.g0, bf16[512,128]{1,0:T(8,128)(2,1)S(1)} %collective-permute-done.12.g1, bf16[512,128]{1,0:T(8,128)(2,1)S(1)} %collective-permute-done.13.g2, ...), custom_call_target="tpu_custom_call" | custom-call | flops 34604998656 | tf_op jit(solution)/shard_map/pallas_call | solution.py:105
  55.6 2.6 %shard_map.70 = (f32[4,24,2304]{2,1,0:T(8,128)S(1)}, bf16[4,24,2304]{2,1,0:T(8,128)(2,1)S(1)}) custom-call(s32[2]{0:T(128)S(1)} %pad_add_fusion.ids, bf16[512,128]{1,0:T(8,128)(2,1)S(1)} %get-tuple-element.117.g0, bf16[512,128]{1,0:T(8,128)(2,1)S(1)} %collective-permute-done.12.g1, bf16[512,128]{1,0:T(8,128)(2,1)S(1)} %collective-permute-done.13.g2, ...), custom_call_target="tpu_custom_call" | custom-call | flops 29991000064 | tf_op jit(solution)/shard_map/pallas_call | solution.py:105
  58.9 2.3 %collective-permute-start.29 = (bf16[2,24,2304]{2,1,0:T(8,128)(2,1)S(1)}, bf16[2,24,2304]{2,1,0:T(8,128)(2,1)S(1)}, u32[]{:S(2)}, u32[]{:S(2)}) collective-permute-start(bf16[2,24,2304]{2,1,0:T(8,128)(2,1)S(1)} %get-tuple-element.126), channel_id=1, source_target_pairs={{0,2},{1,3},{2,0},{3,1},{4,6},{5,7},{6,4},{7,5},{8,10},{9,11},{10,... | collective-permute-start | bytes 663560 | tf_op jit(solution)/shard_map/ppermute | solution.py:25
  61.3 3.6 %shard_map.72 = (bf16[512,128]{1,0:T(8,128)(2,1)}, bf16[512,128]{1,0:T(8,128)(2,1)S(1)}) custom-call(s32[2]{0:T(128)S(1)} %pad_add_fusion.ids, bf16[512,128]{1,0:T(8,128)(2,1)S(1)} %get-tuple-element.136.g0, bf16[512,128]{1,0:T(8,128)(2,1)S(1)} %collective-permute-done.18.g1, bf16[512,128]{1,0:T(8,128)(2,1)S(1)} %collective-permute-done.19.g2, ...), custom_call_target="tpu_custom_call" | custom-call | flops 34604998656 | tf_op jit(solution)/shard_map/pallas_call | solution.py:105
  68.3 2.6 %shard_map.73 = (f32[4,24,2304]{2,1,0:T(8,128)S(1)}, bf16[4,24,2304]{2,1,0:T(8,128)(2,1)S(1)}) custom-call(s32[2]{0:T(128)S(1)} %pad_add_fusion.ids, bf16[512,128]{1,0:T(8,128)(2,1)S(1)} %get-tuple-element.136.g0, bf16[512,128]{1,0:T(8,128)(2,1)S(1)} %collective-permute-done.18.g1, bf16[512,128]{1,0:T(8,128)(2,1)S(1)} %collective-permute-done.19.g2, ...), custom_call_target="tpu_custom_call" | custom-call | flops 29991000064 | tf_op jit(solution)/shard_map/pallas_call | solution.py:105
  75.1 2.6 %shard_map.76 = (f32[4,24,2304]{2,1,0:T(8,128)S(1)}, bf16[4,24,2304]{2,1,0:T(8,128)(2,1)S(1)}) custom-call(s32[2]{0:T(128)S(1)} %pad_add_fusion.ids, bf16[512,128]{1,0:T(8,128)(2,1)S(1)} %get-tuple-element.149.g0, bf16[512,128]{1,0:T(8,128)(2,1)S(1)} %collective-permute-done.25.g1, bf16[512,128]{1,0:T(8,128)(2,1)S(1)} %collective-permute-done.26.g2, ...), custom_call_target="tpu_custom_call" | custom-call | flops 29991000064 | tf_op jit(solution)/shard_map/pallas_call | solution.py:105
  81.4 2.9 %collective-permute-done.36.other = bf16[2,24,2304]{2,1,0:T(8,128)(2,1)S(1)} collective-permute-done((bf16[2,24,2304]{2,1,0:T(8,128)(2,1)S(1)}, bf16[2,24,2304]{2,1,0:T(8,128)(2,1)S(1)}, u32[]{:S(2)}, u32[]{:S(2)}) %collective-permute-start.36) | collective-permute-done | bytes 221216 | tf_op jit(solution)/shard_map/ppermute | solution.py:25
  85.0 4.1 %collective-permute-done.34.other = bf16[2,24,2304]{2,1,0:T(8,128)(2,1)S(1)} collective-permute-done((bf16[2,24,2304]{2,1,0:T(8,128)(2,1)S(1)}, bf16[2,24,2304]{2,1,0:T(8,128)(2,1)S(1)}, u32[]{:S(2)}, u32[]{:S(2)}) %collective-permute-start.34) | collective-permute-done | bytes 221216 | tf_op jit(solution)/shard_map/ppermute | solution.py:25
  89.8 2.9 %collective-permute-start.37 = (bf16[24,2304]{1,0:T(8,128)(2,1)S(1)}, bf16[24,2304]{1,0:T(8,128)(2,1)S(1)}, u32[]{:S(2)}, u32[]{:S(2)}) collective-permute-start(bf16[24,2304]{1,0:T(8,128)(2,1)S(1)} %get-tuple-element.166), channel_id=1, source_target_pairs={{0,4},{1,5},{2,6},{3,7},{4,0},{5,1},{6,2},{7,3},{8,12},{9,13},{10,... | collective-permute-start | bytes 331784 | tf_op jit(solution)/shard_map/ppermute | solution.py:25
  92.7 1.8 %collective-permute-done.31.other = bf16[2,24,2304]{2,1,0:T(8,128)(2,1)S(1)} collective-permute-done((bf16[2,24,2304]{2,1,0:T(8,128)(2,1)S(1)}, bf16[2,24,2304]{2,1,0:T(8,128)(2,1)S(1)}, u32[]{:S(2)}, u32[]{:S(2)}) %collective-permute-start.31) | collective-permute-done | bytes 221216 | tf_op jit(solution)/shard_map/ppermute | solution.py:25
  95.2 7.2 %collective-permute-done.35.refs_3_ = bf16[24,2304]{1,0:T(8,128)(2,1)S(1)} collective-permute-done((bf16[24,2304]{1,0:T(8,128)(2,1)S(1)}, bf16[24,2304]{1,0:T(8,128)(2,1)S(1)}, u32[]{:S(2)}, u32[]{:S(2)}) %collective-permute-start.35) | collective-permute-done | bytes 110624 | tf_op jit(solution)/shard_map/ppermute | solution.py:25
  102.4 1.7 %collective-permute-done.37.refs_5_ = bf16[24,2304]{1,0:T(8,128)(2,1)S(1)} collective-permute-done((bf16[24,2304]{1,0:T(8,128)(2,1)S(1)}, bf16[24,2304]{1,0:T(8,128)(2,1)S(1)}, u32[]{:S(2)}, u32[]{:S(2)}) %collective-permute-start.37) | collective-permute-done | bytes 110624 | tf_op jit(solution)/shard_map/ppermute | solution.py:25
  113.5 1.9 %shard_map.83 = f32[27,32,256]{2,1,0:T(8,128)} custom-call(s32[2]{0:T(128)S(1)} %pad_add_fusion.ids, bf16[24,2304]{1,0:T(8,128)(2,1)S(1)} %get-tuple-element.167.f0, bf16[24,2304]{1,0:T(8,128)(2,1)S(1)} %collective-permute-done.39.f1, bf16[24,2304]{1,0:T(8,128)(2,1)S(1)} %collective-permute-done.40.f2, bf16[24,2304]{1,0:T(8,128)(2,1)S(1)} %collective-permute-done.41.f3, ...), custom_call_target="tpu_custom_call" | custom-call | flops 23069999104 | tf_op jit(solution)/shard_map/pallas_call | solution.py:105
  (106 shorter events, 46.4 us)
Async XLA Ops:
  2.1 9.2 %collective-permute-start.6 = (bf16[24,2304]{1,0:T(8,128)(2,1)S(1)}, bf16[24,2304]{1,0:T(8,128)(2,1)S(1)}, u32[]{:S(2)}, u32[]{:S(2)}) collective-permute-start(bf16[24,2304]{1,0:T(8,128)(2,1)S(1)} %get-tuple-element.98), channel_id=1, source_target_pairs={{0,8},{8,0},{16,24},{24,16},{1,9},{9,1},{17,25},{25,17},{2,10},{10... | collective-permute-start | bytes 331784 | tf_op jit(solution)/shard_map/ppermute | solution.py:25
  7.8 8.4 %collective-permute-start = (bf16[512,128]{1,0:T(8,128)(2,1)S(1)}, bf16[512,128]{1,0:T(8,128)(2,1)S(1)}, u32[]{:S(2)}, u32[]{:S(2)}) collective-permute-start(bf16[512,128]{1,0:T(8,128)(2,1)S(1)} %get-tuple-element.90), channel_id=1, source_target_pairs={{0,8},{8,0},{16,24},{24,16},{1,9},{9,1},{17,25},{25,17},{2,10},{10... | collective-permute-start | bytes 393224 | tf_op jit(solution)/shard_map/ppermute | solution.py:25
  9.8 8.1 %collective-permute-start.1 = (bf16[512,128]{1,0:T(8,128)(2,1)S(1)}, bf16[512,128]{1,0:T(8,128)(2,1)S(1)}, u32[]{:S(2)}, u32[]{:S(2)}) collective-permute-start(bf16[512,128]{1,0:T(8,128)(2,1)S(1)} %get-tuple-element.91), channel_id=1, source_target_pairs={{0,16},{8,24},{16,0},{24,8},{1,17},{9,25},{17,1},{25,9},{2,18},{10... | collective-permute-start | bytes 393224 | tf_op jit(solution)/shard_map/ppermute | solution.py:25
  20.5 10.5 %collective-permute-start.15 = (bf16[24,2304]{1,0:T(8,128)(2,1)S(1)}, bf16[24,2304]{1,0:T(8,128)(2,1)S(1)}, u32[]{:S(2)}, u32[]{:S(2)}) collective-permute-start(bf16[24,2304]{1,0:T(8,128)(2,1)S(1)} %get-tuple-element.113), channel_id=1, source_target_pairs={{0,4},{1,5},{2,6},{3,7},{4,0},{5,1},{6,2},{7,3},{8,12},{9,13},{10,... | collective-permute-start | bytes 331784 | tf_op jit(solution)/shard_map/ppermute | solution.py:25
  23.1 11.9 %collective-permute-start.3 = (bf16[1024,128]{1,0:T(8,128)(2,1)S(1)}, bf16[1024,128]{1,0:T(8,128)(2,1)S(1)}, u32[]{:S(2)}, u32[]{:S(2)}) collective-permute-start(bf16[1024,128]{1,0:T(8,128)(2,1)S(1)} %get-tuple-element.94), channel_id=1, source_target_pairs={{0,8},{8,0},{16,24},{24,16},{1,9},{9,1},{17,25},{25,17},{2,10},{10... | collective-permute-start | bytes 786440 | tf_op jit(solution)/shard_map/ppermute | solution.py:25
  23.8 11.3 %collective-permute-start.4 = (bf16[1024,128]{1,0:T(8,128)(2,1)S(1)}, bf16[1024,128]{1,0:T(8,128)(2,1)S(1)}, u32[]{:S(2)}, u32[]{:S(2)}) collective-permute-start(bf16[1024,128]{1,0:T(8,128)(2,1)S(1)} %get-tuple-element.95), channel_id=1, source_target_pairs={{0,16},{8,24},{16,0},{24,8},{1,17},{9,25},{17,1},{25,9},{2,18},{10... | collective-permute-start | bytes 786440 | tf_op jit(solution)/shard_map/ppermute | solution.py:25
  24.6 10.5 %collective-permute-start.5 = (bf16[1024,128]{1,0:T(8,128)(2,1)S(1)}, bf16[1024,128]{1,0:T(8,128)(2,1)S(1)}, u32[]{:S(2)}, u32[]{:S(2)}) collective-permute-start(bf16[1024,128]{1,0:T(8,128)(2,1)S(1)} %get-tuple-element.96), channel_id=1, source_target_pairs={{0,24},{8,16},{16,8},{24,0},{1,25},{9,17},{17,9},{25,1},{2,26},{10... | collective-permute-start | bytes 786440 | tf_op jit(solution)/shard_map/ppermute | solution.py:25
  26.7 8.2 %collective-permute-start.10 = (bf16[2,24,2304]{2,1,0:T(8,128)(2,1)S(1)}, bf16[2,24,2304]{2,1,0:T(8,128)(2,1)S(1)}, u32[]{:S(2)}, u32[]{:S(2)}) collective-permute-start(bf16[2,24,2304]{2,1,0:T(8,128)(2,1)S(1)} %pad_maximum_fusion.6), channel_id=1, source_target_pairs={{0,2},{1,3},{2,0},{3,1},{4,6},{5,7},{6,4},{7,5},{8,10},{9,11},{10,... | collective-permute-start | bytes 663560 | tf_op jit(solution)/shard_map/ppermute | solution.py:25
  31.0 12.9 %collective-permute-start.16 = (bf16[2,24,2304]{2,1,0:T(8,128)(2,1)S(1)}, bf16[2,24,2304]{2,1,0:T(8,128)(2,1)S(1)}, u32[]{:S(2)}, u32[]{:S(2)}) collective-permute-start(bf16[2,24,2304]{2,1,0:T(8,128)(2,1)S(1)} %pad_maximum_fusion.7), channel_id=1, source_target_pairs={{0,2},{1,3},{2,0},{3,1},{4,6},{5,7},{6,4},{7,5},{8,10},{9,11},{10,... | collective-permute-start | bytes 663560 | tf_op jit(solution)/shard_map/ppermute | solution.py:25
  35.2 8.8 %collective-permute-start.22 = (bf16[24,2304]{1,0:T(8,128)(2,1)S(1)}, bf16[24,2304]{1,0:T(8,128)(2,1)S(1)}, u32[]{:S(2)}, u32[]{:S(2)}) collective-permute-start(bf16[24,2304]{1,0:T(8,128)(2,1)S(1)} %get-tuple-element.131), channel_id=1, source_target_pairs={{0,4},{1,5},{2,6},{3,7},{4,0},{5,1},{6,2},{7,3},{8,12},{9,13},{10,... | collective-permute-start | bytes 331784 | tf_op jit(solution)/shard_map/ppermute | solution.py:25
  39.9 8.4 %collective-permute-start.14 = (bf16[512,128]{1,0:T(8,128)(2,1)S(1)}, bf16[512,128]{1,0:T(8,128)(2,1)S(1)}, u32[]{:S(2)}, u32[]{:S(2)}) collective-permute-start(bf16[512,128]{1,0:T(8,128)(2,1)S(1)} %get-tuple-element.117.g0), channel_id=1, source_target_pairs={{0,24},{8,16},{16,8},{24,0},{1,25},{9,17},{17,9},{25,1},{2,26},{10... | collective-permute-start | bytes 393224 | tf_op jit(solution)/shard_map/ppermute | solution.py:25
  44.0 11.0 %collective-permute-start.23 = (bf16[2,24,2304]{2,1,0:T(8,128)(2,1)S(1)}, bf16[2,24,2304]{2,1,0:T(8,128)(2,1)S(1)}, u32[]{:S(2)}, u32[]{:S(2)}) collective-permute-start(bf16[2,24,2304]{2,1,0:T(8,128)(2,1)S(1)} %pad_maximum_fusion.8), channel_id=1, source_target_pairs={{0,2},{1,3},{2,0},{3,1},{4,6},{5,7},{6,4},{7,5},{8,10},{9,11},{10,... | collective-permute-start | bytes 663560 | tf_op jit(solution)/shard_map/ppermute | solution.py:25
  51.4 9.7 %collective-permute-start.20 = (bf16[512,128]{1,0:T(8,128)(2,1)S(1)}, bf16[512,128]{1,0:T(8,128)(2,1)S(1)}, u32[]{:S(2)}, u32[]{:S(2)}) collective-permute-start(bf16[512,128]{1,0:T(8,128)(2,1)S(1)} %get-tuple-element.136.g0), channel_id=1, source_target_pairs={{0,24},{8,16},{16,8},{24,0},{1,25},{9,17},{17,9},{25,1},{2,26},{10... | collective-permute-start | bytes 393224 | tf_op jit(solution)/shard_map/ppermute | solution.py:25
  52.6 8.5 %collective-permute-start.19 = (bf16[512,128]{1,0:T(8,128)(2,1)S(1)}, bf16[512,128]{1,0:T(8,128)(2,1)S(1)}, u32[]{:S(2)}, u32[]{:S(2)}) collective-permute-start(bf16[512,128]{1,0:T(8,128)(2,1)S(1)} %get-tuple-element.136.g0), channel_id=1, source_target_pairs={{0,16},{8,24},{16,0},{24,8},{1,17},{9,25},{17,1},{25,9},{2,18},{10... | collective-permute-start | bytes 393224 | tf_op jit(solution)/shard_map/ppermute | solution.py:25
  58.9 12.1 %collective-permute-start.29 = (bf16[2,24,2304]{2,1,0:T(8,128)(2,1)S(1)}, bf16[2,24,2304]{2,1,0:T(8,128)(2,1)S(1)}, u32[]{:S(2)}, u32[]{:S(2)}) collective-permute-start(bf16[2,24,2304]{2,1,0:T(8,128)(2,1)S(1)} %get-tuple-element.126), channel_id=1, source_target_pairs={{0,2},{1,3},{2,0},{3,1},{4,6},{5,7},{6,4},{7,5},{8,10},{9,11},{10,... | collective-permute-start | bytes 663560 | tf_op jit(solution)/shard_map/ppermute | solution.py:25
  64.8 9.3 %collective-permute-start.27 = (bf16[512,128]{1,0:T(8,128)(2,1)S(1)}, bf16[512,128]{1,0:T(8,128)(2,1)S(1)}, u32[]{:S(2)}, u32[]{:S(2)}) collective-permute-start(bf16[512,128]{1,0:T(8,128)(2,1)S(1)} %get-tuple-element.149.g0), channel_id=1, source_target_pairs={{0,24},{8,16},{16,8},{24,0},{1,25},{9,17},{17,9},{25,1},{2,26},{10... | collective-permute-start | bytes 393224 | tf_op jit(solution)/shard_map/ppermute | solution.py:25
  66.0 9.2 %collective-permute-start.26 = (bf16[512,128]{1,0:T(8,128)(2,1)S(1)}, bf16[512,128]{1,0:T(8,128)(2,1)S(1)}, u32[]{:S(2)}, u32[]{:S(2)}) collective-permute-start(bf16[512,128]{1,0:T(8,128)(2,1)S(1)} %get-tuple-element.149.g0), channel_id=1, source_target_pairs={{0,16},{8,24},{16,0},{24,8},{1,17},{9,25},{17,1},{25,9},{2,18},{10... | collective-permute-start | bytes 393224 | tf_op jit(solution)/shard_map/ppermute | solution.py:25
  72.1 23.0 %collective-permute-start.38 = (bf16[24,2304]{1,0:T(8,128)(2,1)S(1)}, bf16[24,2304]{1,0:T(8,128)(2,1)S(1)}, u32[]{:S(2)}, u32[]{:S(2)}) collective-permute-start(bf16[24,2304]{1,0:T(8,128)(2,1)S(1)} %get-tuple-element.148), channel_id=1, source_target_pairs={{0,4},{1,5},{2,6},{3,7},{4,0},{5,1},{6,2},{7,3},{8,12},{9,13},{10,... | collective-permute-start | bytes 331784 | tf_op jit(solution)/shard_map/ppermute | solution.py:25
  74.2 10.2 %collective-permute-start.36 = (bf16[2,24,2304]{2,1,0:T(8,128)(2,1)S(1)}, bf16[2,24,2304]{2,1,0:T(8,128)(2,1)S(1)}, u32[]{:S(2)}, u32[]{:S(2)}) collective-permute-start(bf16[2,24,2304]{2,1,0:T(8,128)(2,1)S(1)} %get-tuple-element.145), channel_id=1, source_target_pairs={{0,2},{1,3},{2,0},{3,1},{4,6},{5,7},{6,4},{7,5},{8,10},{9,11},{10,... | collective-permute-start | bytes 663560 | tf_op jit(solution)/shard_map/ppermute | solution.py:25
  78.4 10.7 %collective-permute-start.34 = (bf16[2,24,2304]{2,1,0:T(8,128)(2,1)S(1)}, bf16[2,24,2304]{2,1,0:T(8,128)(2,1)S(1)}, u32[]{:S(2)}, u32[]{:S(2)}) collective-permute-start(bf16[2,24,2304]{2,1,0:T(8,128)(2,1)S(1)} %get-tuple-element.160), channel_id=1, source_target_pairs={{0,2},{1,3},{2,0},{3,1},{4,6},{5,7},{6,4},{7,5},{8,10},{9,11},{10,... | collective-permute-start | bytes 663560 | tf_op jit(solution)/shard_map/ppermute | solution.py:25
  80.3 14.2 %collective-permute-start.31 = (bf16[2,24,2304]{2,1,0:T(8,128)(2,1)S(1)}, bf16[2,24,2304]{2,1,0:T(8,128)(2,1)S(1)}, u32[]{:S(2)}, u32[]{:S(2)}) collective-permute-start(bf16[2,24,2304]{2,1,0:T(8,128)(2,1)S(1)} %get-tuple-element.156), channel_id=1, source_target_pairs={{0,2},{1,3},{2,0},{3,1},{4,6},{5,7},{6,4},{7,5},{8,10},{9,11},{10,... | collective-permute-start | bytes 663560 | tf_op jit(solution)/shard_map/ppermute | solution.py:25
  89.7 12.7 %collective-permute-start.35 = (bf16[24,2304]{1,0:T(8,128)(2,1)S(1)}, bf16[24,2304]{1,0:T(8,128)(2,1)S(1)}, u32[]{:S(2)}, u32[]{:S(2)}) collective-permute-start(bf16[24,2304]{1,0:T(8,128)(2,1)S(1)} %get-tuple-element.163), channel_id=1, source_target_pairs={{0,4},{1,5},{2,6},{3,7},{4,0},{5,1},{6,2},{7,3},{8,12},{9,13},{10,... | collective-permute-start | bytes 331784 | tf_op jit(solution)/shard_map/ppermute | solution.py:25
  89.8 14.3 %collective-permute-start.37 = (bf16[24,2304]{1,0:T(8,128)(2,1)S(1)}, bf16[24,2304]{1,0:T(8,128)(2,1)S(1)}, u32[]{:S(2)}, u32[]{:S(2)}) collective-permute-start(bf16[24,2304]{1,0:T(8,128)(2,1)S(1)} %get-tuple-element.166), channel_id=1, source_target_pairs={{0,4},{1,5},{2,6},{3,7},{4,0},{5,1},{6,2},{7,3},{8,12},{9,13},{10,... | collective-permute-start | bytes 331784 | tf_op jit(solution)/shard_map/ppermute | solution.py:25
  95.1 10.2 %collective-permute-start.32 = (bf16[24,2304]{1,0:T(8,128)(2,1)S(1)}, bf16[24,2304]{1,0:T(8,128)(2,1)S(1)}, u32[]{:S(2)}, u32[]{:S(2)}) collective-permute-start(bf16[24,2304]{1,0:T(8,128)(2,1)S(1)} %get-tuple-element.158), channel_id=1, source_target_pairs={{0,4},{1,5},{2,6},{3,7},{4,0},{5,1},{6,2},{7,3},{8,12},{9,13},{10,... | collective-permute-start | bytes 331784 | tf_op jit(solution)/shard_map/ppermute | solution.py:25
  (24 other events, 135.8 us)

commit v4 on v3

--- a/solution.py
+++ b/solution.py
@@ -213,15 +213,13 @@
         cols[:, k * channels : (k + 1) * channels] = part.astype(BF16)
 
 
-def back_body(span, n_dp, ids, g0, g1, g2, g3, w_ref, up_ref, pre_ref, up_out, g_out, cols):
+def find_back(cols, w_ref, up_ref, pre_ref, up_out, g_out, span, n_dp, d):
     span_t, span_x, span_y = span
     half, width = up_ref.shape
     quarter_n = width // 2
     sub = quarter_n // n_dp
     rows = 2 * half
     plane = span_x * span_y
-    d = ids[1]
-    fill_columns(cols, (g0, g1, g2, g3), half, span)
     shape = (3 * quarter_n, 3 * quarter_n)
     dst, src = iota(shape, 0), iota(shape, 1)
     a, place = dst >> log2(quarter_n), dst & (quarter_n - 1)
@@ -251,14 +249,12 @@
     g_out[...] = silu_back(passed.astype(F32), pre_ref[...])
 
 
-def grads_body(span, n_dp, ids, g0, g1, g2, g3, x_ref, keep, give, cols, total):
+def find_terms(cols, x_ref, keep, give, total, span, n_dp, d):
     span_t, span_x, span_y = span
     half, width = x_ref.shape
     quarter_n = width // 2
     sub = quarter_n // n_dp
     plane = span_x * span_y
-    d = ids[1]
-    fill_columns(cols, (g0, g1, g2, g3), half, span)
     shape = (width, 2 * width)
     src, dst = iota(shape, 0), iota(shape, 1)
     twice = jnp.logical_and(
@@ -285,6 +281,24 @@
                 for a in range(3)
             ]
             ref[k] = jnp.concatenate(own, axis=0).astype(ref.dtype)
+
+
+def back_body(span, n_dp, ids, g0, g1, g2, g3, w_ref, up_ref, pre_ref, up_out, g_out, cols):
+    fill_columns(cols, (g0, g1, g2, g3), up_ref.shape[0], span)
+    find_back(cols, w_ref, up_ref, pre_ref, up_out, g_out, span, n_dp, ids[1])
+
+
+def section_body(
+    span, n_dp, ids, g0, g1, g2, g3, w_ref, up_ref, pre_ref, x_ref, up_out, g_out, keep, give, cols, total
+):
+    fill_columns(cols, (g0, g1, g2, g3), up_ref.shape[0], span)
+    find_back(cols, w_ref, up_ref, pre_ref, up_out, g_out, span, n_dp, ids[1])
+    find_terms(cols, x_ref, keep, give, total, span, n_dp, ids[1])
+
+
+def terms_body(span, n_dp, ids, g0, g1, g2, g3, x_ref, keep, give, cols, total):
+    fill_columns(cols, (g0, g1, g2, g3), x_ref.shape[0], span)
+    find_terms(cols, x_ref, keep, give, total, span, n_dp, ids[1])
 
 
 def pair_body(ids, keep, other, stay, send):
@@ -395,7 +409,7 @@
 
     def terms(field, x):
         return call(
-            functools.partial(grads_body, span, n_dp),
+            functools.partial(terms_body, span, n_dp),
             [array(F32, 4), array(BF16, 4)],
             (ids, *field, x), 2.6,
             scratch=[columns, pltpu.VMEM((3 * quarter_n, 9 * channels), F32)],
@@ -421,6 +435,18 @@
             scratch=[columns],
         )
 
+    def back_and_terms(section, field, up):
+        up, g, *terms = call(
+            functools.partial(section_body, span, n_dp),
+            [packed, packed, array(F32, 4), array(BF16, 4)],
+            (
+                ids, *field, kernels[section], up,
+                pick(s ^ (section - 1), p_held), pick(s ^ section, x_held),
+            ), 3.8,
+            scratch=[columns, pltpu.VMEM((3 * quarter_n, 9 * channels), F32)],
+        )
+        return up, g, terms
+
     def tied(field, *others):
         return lax.optimization_barrier((tuple(field), others))[0]
 
@@ -428,18 +454,17 @@
         return lax.optimization_barrier((tuple(field), others))[0]
 
     kernels = {}
+    first = call(
+        functools.partial(first_body, per, sub),
+        [jax.ShapeDtypeStruct((rows, width), BF16)] * 4,
+        (ids, up, pick(s ^ 3, p_held), inputs), 1.1,
+    )
+    field3 = spread(first)
     half3 = far_half(after(pick(s ^ 3, w_held), *p_parts))
-    chips3 = all_chips(half3)
+    chips3 = all_chips(after(half3, first[0]))
     kernels[3] = both_cores(chips3)
-    field3 = spread(
-        call(
-            functools.partial(first_body, per, sub),
-            [jax.ShapeDtypeStruct((rows, width), BF16)] * 4,
-            (ids, up, pick(s ^ 3, p_held), inputs), 6.0,
-        )
-    )
     x_held = [x[half:] for x in field3]
-    half2 = far_half(after(pick(s ^ 2, w_held), half3))
+    half2 = far_half(after(pick(s ^ 2, w_held), half3, first[0]))
     up, g2 = back(3, field3, up)
     field2 = spread([g2] * 4)
     chips2 = all_chips(half2, g2)
@@ -452,18 +477,18 @@
     kernels[1] = both_cores(chips1)
     terms3 = paired(*tied(terms3, g1))
     terms2 = terms(tied(field2, g1), pick(s ^ 2, x_held))
-    up, g0 = back(1, tied(field1, terms2, terms3), up)
+    terms2 = paired(*terms2)
+    up, g0, terms1 = back_and_terms(1, tied(field1, terms2, terms3), up)
     field0 = spread([g0] * 4)
     terms3 = reduced(*terms3, g0)
-    terms2 = paired(*tied(terms2, g0))
-    terms1 = terms(tied(field1, g0), pick(s ^ 1, x_held))
-    terms0 = terms(tied(field0, terms1, terms2, terms3), pick(s, x_held))
     terms1 = paired(*terms1)
+    terms0 = terms(tied(field0, terms1, terms3), pick(s, x_held))
     terms0 = paired(*terms0)
     sum3 = summed(*terms3)
-    sum2 = summed(*reduced(*terms2, terms0))
-    sum1 = summed(*reduced(*terms1, terms0))
-    sums = [summed(*reduced(*terms0)), sum1, sum2, sum3]
+    terms2 = reduced(*terms2)
+    terms1 = reduced(*terms1)
+    terms0 = reduced(*terms0)
+    sums = [summed(*terms0), summed(*terms1), summed(*terms2), sum3]
     owned = spread(
         call(sums_body, [array(BF16)] * 4, (ids, *sums[0], *sums[1], *sums[2], *sums[3]), 0.7)
     )

time: 116 us -> 113 us (0.974)
  starting transfers between devices: 49.3 us -> 45.2 us
  waiting for transfers between devices: 33.4 us -> 36.7 us
  Pallas kernels: 30.4 us -> 28.9 us
    ppermute x42, starting transfers between devices: 49.3 us -> 45.2 us  [swapped(): lax.ppermute(x, axis, [(i, i ^ mask) for i in range(lax.axis_size(axis))])]
    ppermute x42, waiting for transfers between devices: 33.4 us -> 36.7 us  [swapped(): lax.ppermute(x, axis, [(i, i ^ mask) for i in range(lax.axis_size(axis))])]
    pallas_call x20 -> x19, Pallas kernels: 30.4 us -> 28.9 us  [call(): pl.pallas_call(body, out_shape=out_shape, in_specs=[pl.BlockSpec(memory_s...]
  transfers between devices with their start and end apart: 42 -> 42, of which waited for: 16 -> 14; matrix products, arithmetic and copies ran while one was open for 1% -> 1% of each run, Pallas kernels for 23% -> 22%
where the time goes in v4:
time: 113 us
  starting transfers between devices  45.2 us (40%)
  waiting for transfers between devices  36.7 us (32%)
  Pallas kernels  28.9 us (26%)
  local copies, waits for them, and re-layouts  1.19 us (1%)
    ppermute x42, starting transfers between devices, swapped(): lax.ppermute(x, axis, [(i, i ^ mask) for i in range(lax.axis_size(axis))])  45.2 us
    ppermute x42, waiting for transfers between devices, swapped(): lax.ppermute(x, axis, [(i, i ^ mask) for i in range(lax.axis_size(axis))])  36.7 us
    pallas_call x19, Pallas kernels, call(): pl.pallas_call(body, out_shape=out_shape, in_specs=[pl.BlockSpec(memory_s...  28.9 us
  transfers between devices with their start and end apart: 42, of which 14 were waited for; matrix products, arithmetic and copies ran while one was open for 1% of the time, Pallas kernels for 22%

profile of v4, /device:TPU:0, one launch (start us, length us, event | category | flops | bytes accessed | tf_op | source)
XLA Modules:
  0.0 113.1 jit_solution(13599942056446820399)
XLA Ops:
  2.1 3.0 %collective-permute-start.6 = (bf16[24,2304]{1,0:T(8,128)(2,1)S(1)}, bf16[24,2304]{1,0:T(8,128)(2,1)S(1)}, u32[]{:S(2)}, u32[]{:S(2)}) collective-permute-start(bf16[24,2304]{1,0:T(8,128)(2,1)S(1)} %get-tuple-element.91), channel_id=1, source_target_pairs={{0,8},{8,0},{16,24},{24,16},{1,9},{9,1},{17,25},{25,17},{2,10},{10... | collective-permute-start | bytes 331784 | tf_op jit(solution)/shard_map/ppermute | solution.py:25
  7.8 2.0 %collective-permute-start = (bf16[512,128]{1,0:T(8,128)(2,1)S(1)}, bf16[512,128]{1,0:T(8,128)(2,1)S(1)}, u32[]{:S(2)}, u32[]{:S(2)}) collective-permute-start(bf16[512,128]{1,0:T(8,128)(2,1)S(1)} %get-tuple-element.83), channel_id=1, source_target_pairs={{0,8},{8,0},{16,24},{24,16},{1,9},{9,1},{17,25},{25,17},{2,10},{10... | collective-permute-start | bytes 393224 | tf_op jit(solution)/shard_map/ppermute | solution.py:25
  11.8 1.7 %collective-permute-done.8 = bf16[24,2304]{1,0:T(8,128)(2,1)S(1)} collective-permute-done((bf16[24,2304]{1,0:T(8,128)(2,1)S(1)}, bf16[24,2304]{1,0:T(8,128)(2,1)S(1)}, u32[]{:S(2)}, u32[]{:S(2)}) %collective-permute-start.8) | collective-permute-done | bytes 110624 | tf_op jit(solution)/shard_map/ppermute | solution.py:25
  13.5 2.7 %collective-permute-start.9 = (bf16[24,2304]{1,0:T(8,128)(2,1)S(1)}, bf16[24,2304]{1,0:T(8,128)(2,1)S(1)}, u32[]{:S(2)}, u32[]{:S(2)}) collective-permute-start(bf16[24,2304]{1,0:T(8,128)(2,1)S(1)} %get-tuple-element.94), channel_id=1, source_target_pairs={{0,4},{1,5},{2,6},{3,7},{4,0},{5,1},{6,2},{7,3},{8,12},{9,13},{10,... | collective-permute-start | bytes 331784 | tf_op jit(solution)/shard_map/ppermute | solution.py:25
  16.2 1.7 %collective-permute-done.1 = bf16[512,128]{1,0:T(8,128)(2,1)S(1)} collective-permute-done((bf16[512,128]{1,0:T(8,128)(2,1)S(1)}, bf16[512,128]{1,0:T(8,128)(2,1)S(1)}, u32[]{:S(2)}, u32[]{:S(2)}) %collective-permute-start.1) | collective-permute-done | bytes 131104 | tf_op jit(solution)/shard_map/ppermute | solution.py:25
  23.7 1.9 %collective-permute-start.5 = (bf16[1024,128]{1,0:T(8,128)(2,1)S(1)}, bf16[1024,128]{1,0:T(8,128)(2,1)S(1)}, u32[]{:S(2)}, u32[]{:S(2)}) collective-permute-start(bf16[1024,128]{1,0:T(8,128)(2,1)S(1)} %get-tuple-element.89), channel_id=1, source_target_pairs={{0,24},{8,16},{16,8},{24,0},{1,25},{9,17},{17,9},{25,1},{2,26},{10... | collective-permute-start | bytes 786440 | tf_op jit(solution)/shard_map/ppermute | solution.py:25
  25.5 2.5 %collective-permute-start.10 = (bf16[2,24,2304]{2,1,0:T(8,128)(2,1)S(1)}, bf16[2,24,2304]{2,1,0:T(8,128)(2,1)S(1)}, u32[]{:S(2)}, u32[]{:S(2)}) collective-permute-start(bf16[2,24,2304]{2,1,0:T(8,128)(2,1)S(1)} %pad_maximum_fusion.6), channel_id=1, source_target_pairs={{0,2},{1,3},{2,0},{3,1},{4,6},{5,7},{6,4},{7,5},{8,10},{9,11},{10,... | collective-permute-start | bytes 663560 | tf_op jit(solution)/shard_map/ppermute | solution.py:25
  28.6 4.7 %collective-permute-done.10 = bf16[2,24,2304]{2,1,0:T(8,128)(2,1)S(1)} collective-permute-done((bf16[2,24,2304]{2,1,0:T(8,128)(2,1)S(1)}, bf16[2,24,2304]{2,1,0:T(8,128)(2,1)S(1)}, u32[]{:S(2)}, u32[]{:S(2)}) %collective-permute-start.10) | collective-permute-done | bytes 221216 | tf_op jit(solution)/shard_map/ppermute | solution.py:25
  33.4 1.6 %collective-permute-done.4.g2 = bf16[1024,128]{1,0:T(8,128)(2,1)S(1)} collective-permute-done((bf16[1024,128]{1,0:T(8,128)(2,1)S(1)}, bf16[1024,128]{1,0:T(8,128)(2,1)S(1)}, u32[]{:S(2)}, u32[]{:S(2)}) %collective-permute-start.4) | collective-permute-done | bytes 262176 | tf_op jit(solution)/shard_map/ppermute | solution.py:25
  36.3 2.9 %shard_map.67 = (bf16[512,128]{1,0:T(8,128)(2,1)S(1)}, bf16[512,128]{1,0:T(8,128)(2,1)S(1)}) custom-call(s32[2]{0:T(128)S(1)} %pad_add_fusion.ids, bf16[1024,128]{1,0:T(8,128)(2,1)S(1)} %get-tuple-element.97.g0, bf16[1024,128]{1,0:T(8,128)(2,1)S(1)} %collective-permute-done.3.g1, bf16[1024,128]{1,0:T(8,128)(2,1)S(1)} %collective-permute-done.4.g2, ...), custom_call_target="tpu_custom_call" | custom-call | flops 34604998656 | tf_op jit(solution)/shard_map/pallas_call | solution.py:105
  41.2 1.6 %collective-permute-start.12 = (bf16[512,128]{1,0:T(8,128)(2,1)S(1)}, bf16[512,128]{1,0:T(8,128)(2,1)S(1)}, u32[]{:S(2)}, u32[]{:S(2)}) collective-permute-start(bf16[512,128]{1,0:T(8,128)(2,1)S(1)} %get-tuple-element.111.g0), channel_id=1, source_target_pairs={{0,8},{8,0},{16,24},{24,16},{1,9},{9,1},{17,25},{25,17},{2,10},{10... | collective-permute-start | bytes 393224 | tf_op jit(solution)/shard_map/ppermute | solution.py:25
  43.9 2.6 %shard_map.68 = (f32[4,24,2304]{2,1,0:T(8,128)S(1)}, bf16[4,24,2304]{2,1,0:T(8,128)(2,1)S(1)}) custom-call(s32[2]{0:T(128)S(1)} %pad_add_fusion.ids, bf16[1024,128]{1,0:T(8,128)(2,1)S(1)} %get-tuple-element.97.g0, bf16[1024,128]{1,0:T(8,128)(2,1)S(1)} %collective-permute-done.3.g1, bf16[1024,128]{1,0:T(8,128)(2,1)S(1)} %collective-permute-done.4.g2, ...), custom_call_target="tpu_custom_call" | custom-call | flops 29991000064 | tf_op jit(solution)/shard_map/pallas_call | solution.py:105
  47.4 3.0 %shard_map.69 = (bf16[512,128]{1,0:T(8,128)(2,1)S(1)}, bf16[512,128]{1,0:T(8,128)(2,1)S(1)}) custom-call(s32[2]{0:T(128)S(1)} %pad_add_fusion.ids, bf16[512,128]{1,0:T(8,128)(2,1)S(1)} %get-tuple-element.111.g0, bf16[512,128]{1,0:T(8,128)(2,1)S(1)} %collective-permute-done.12.g1, bf16[512,128]{1,0:T(8,128)(2,1)S(1)} %collective-permute-done.13.g2, ...), custom_call_target="tpu_custom_call" | custom-call | flops 34604998656 | tf_op jit(solution)/shard_map/pallas_call | solution.py:105
  54.6 2.6 %shard_map.70 = (f32[4,24,2304]{2,1,0:T(8,128)S(1)}, bf16[4,24,2304]{2,1,0:T(8,128)(2,1)S(1)}) custom-call(s32[2]{0:T(128)S(1)} %pad_add_fusion.ids, bf16[512,128]{1,0:T(8,128)(2,1)S(1)} %get-tuple-element.111.g0, bf16[512,128]{1,0:T(8,128)(2,1)S(1)} %collective-permute-done.12.g1, bf16[512,128]{1,0:T(8,128)(2,1)S(1)} %collective-permute-done.13.g2, ...), custom_call_target="tpu_custom_call" | custom-call | flops 29991000064 | tf_op jit(solution)/shard_map/pallas_call | solution.py:105
  60.8 4.5 %shard_map.73 = (bf16[512,128]{1,0:T(8,128)(2,1)}, bf16[512,128]{1,0:T(8,128)(2,1)S(1)}, f32[4,24,2304]{2,1,0:T(8,128)S(1)}, bf16[4,24,2304]{2,1,0:T(8,128)(2,1)S(1)}) custom-call(s32[2]{0:T(128)S(1)} %pad_add_fusion.ids, bf16[512,128]{1,0:T(8,128)(2,1)S(1)} %get-tuple-element.123.g0, bf16[512,128]{1,0:T(8,128)(2,1)S(1)} %collective-permute-done.18.g1, ...), custom_call_target="tpu_custom_call" | custom-call | flops 43832999936 | tf_op jit(solution)/shard_map/pallas_call | solution.py:105
  65.3 1.7 %collective-permute-start.28 = (bf16[512,128]{1,0:T(8,128)(2,1)S(1)}, bf16[512,128]{1,0:T(8,128)(2,1)S(1)}, u32[]{:S(2)}, u32[]{:S(2)}) collective-permute-start(bf16[512,128]{1,0:T(8,128)(2,1)S(1)} %get-tuple-element.139.g0), channel_id=1, source_target_pairs={{0,24},{8,16},{16,8},{24,0},{1,25},{9,17},{17,9},{25,1},{2,26},{10... | collective-permute-start | bytes 393224 | tf_op jit(solution)/shard_map/ppermute | solution.py:25
  70.4 4.7 %collective-permute-done.36.other = bf16[2,24,2304]{2,1,0:T(8,128)(2,1)S(1)} collective-permute-done((bf16[2,24,2304]{2,1,0:T(8,128)(2,1)S(1)}, bf16[2,24,2304]{2,1,0:T(8,128)(2,1)S(1)}, u32[]{:S(2)}, u32[]{:S(2)}) %collective-permute-start.36) | collective-permute-done | bytes 221216 | tf_op jit(solution)/shard_map/ppermute | solution.py:25
  75.1 1.8 %collective-permute-start.38 = (bf16[24,2304]{1,0:T(8,128)(2,1)S(1)}, bf16[24,2304]{1,0:T(8,128)(2,1)S(1)}, u32[]{:S(2)}, u32[]{:S(2)}) collective-permute-start(bf16[24,2304]{1,0:T(8,128)(2,1)S(1)} %get-tuple-element.138), channel_id=1, source_target_pairs={{0,4},{1,5},{2,6},{3,7},{4,0},{5,1},{6,2},{7,3},{8,12},{9,13},{10,... | collective-permute-start | bytes 331784 | tf_op jit(solution)/shard_map/ppermute | solution.py:25
  78.6 2.6 %shard_map.76 = (f32[4,24,2304]{2,1,0:T(8,128)S(1)}, bf16[4,24,2304]{2,1,0:T(8,128)(2,1)S(1)}) custom-call(s32[2]{0:T(128)S(1)} %pad_add_fusion.ids, bf16[512,128]{1,0:T(8,128)(2,1)S(1)} %get-tuple-element.139.g0, bf16[512,128]{1,0:T(8,128)(2,1)S(1)} %collective-permute-done.26.g1, bf16[512,128]{1,0:T(8,128)(2,1)S(1)} %collective-permute-done.27.g2, ...), custom_call_target="tpu_custom_call" | custom-call | flops 29991000064 | tf_op jit(solution)/shard_map/pallas_call | solution.py:105
  86.2 1.8 %collective-permute-start.35 = (bf16[24,2304]{1,0:T(8,128)(2,1)S(1)}, bf16[24,2304]{1,0:T(8,128)(2,1)S(1)}, u32[]{:S(2)}, u32[]{:S(2)}) collective-permute-start(bf16[24,2304]{1,0:T(8,128)(2,1)S(1)} %get-tuple-element.150), channel_id=1, source_target_pairs={{0,4},{1,5},{2,6},{3,7},{4,0},{5,1},{6,2},{7,3},{8,12},{9,13},{10,... | collective-permute-start | bytes 331784 | tf_op jit(solution)/shard_map/ppermute | solution.py:25
  88.1 7.5 %collective-permute-done.32.other = bf16[2,24,2304]{2,1,0:T(8,128)(2,1)S(1)} collective-permute-done((bf16[2,24,2304]{2,1,0:T(8,128)(2,1)S(1)}, bf16[2,24,2304]{2,1,0:T(8,128)(2,1)S(1)}, u32[]{:S(2)}, u32[]{:S(2)}) %collective-permute-start.32) | collective-permute-done | bytes 221216 | tf_op jit(solution)/shard_map/ppermute | solution.py:25
  96.5 5.9 %collective-permute-done.33.refs_1_ = bf16[24,2304]{1,0:T(8,128)(2,1)S(1)} collective-permute-done((bf16[24,2304]{1,0:T(8,128)(2,1)S(1)}, bf16[24,2304]{1,0:T(8,128)(2,1)S(1)}, u32[]{:S(2)}, u32[]{:S(2)}) %collective-permute-start.33) | collective-permute-done | bytes 110624 | tf_op jit(solution)/shard_map/ppermute | solution.py:25
  109.2 1.9 %collective-permute-done.41.f3 = bf16[24,2304]{1,0:T(8,128)(2,1)S(1)} collective-permute-done((bf16[24,2304]{1,0:T(8,128)(2,1)S(1)}, bf16[24,2304]{1,0:T(8,128)(2,1)S(1)}, u32[]{:S(2)}, u32[]{:S(2)}) %collective-permute-start.41) | collective-permute-done | bytes 110624 | tf_op jit(solution)/shard_map/ppermute | solution.py:25
  111.1 1.9 %shard_map.82 = f32[27,32,256]{2,1,0:T(8,128)} custom-call(s32[2]{0:T(128)S(1)} %pad_add_fusion.ids, bf16[24,2304]{1,0:T(8,128)(2,1)S(1)} %get-tuple-element.153.f0, bf16[24,2304]{1,0:T(8,128)(2,1)S(1)} %collective-permute-done.39.f1, bf16[24,2304]{1,0:T(8,128)(2,1)S(1)} %collective-permute-done.40.f2, bf16[24,2304]{1,0:T(8,128)(2,1)S(1)} %collective-permute-done.41.f3, ...), custom_call_target="tpu_custom_call" | custom-call | flops 23069999104 | tf_op jit(solution)/shard_map/pallas_call | solution.py:105
  (105 shorter events, 44.1 us)
Async XLA Ops:
  2.1 9.2 %collective-permute-start.6 = (bf16[24,2304]{1,0:T(8,128)(2,1)S(1)}, bf16[24,2304]{1,0:T(8,128)(2,1)S(1)}, u32[]{:S(2)}, u32[]{:S(2)}) collective-permute-start(bf16[24,2304]{1,0:T(8,128)(2,1)S(1)} %get-tuple-element.91), channel_id=1, source_target_pairs={{0,8},{8,0},{16,24},{24,16},{1,9},{9,1},{17,25},{25,17},{2,10},{10... | collective-permute-start | bytes 331784 | tf_op jit(solution)/shard_map/ppermute | solution.py:25
  7.8 8.4 %collective-permute-start = (bf16[512,128]{1,0:T(8,128)(2,1)S(1)}, bf16[512,128]{1,0:T(8,128)(2,1)S(1)}, u32[]{:S(2)}, u32[]{:S(2)}) collective-permute-start(bf16[512,128]{1,0:T(8,128)(2,1)S(1)} %get-tuple-element.83), channel_id=1, source_target_pairs={{0,8},{8,0},{16,24},{24,16},{1,9},{9,1},{17,25},{25,17},{2,10},{10... | collective-permute-start | bytes 393224 | tf_op jit(solution)/shard_map/ppermute | solution.py:25
  9.8 8.1 %collective-permute-start.1 = (bf16[512,128]{1,0:T(8,128)(2,1)S(1)}, bf16[512,128]{1,0:T(8,128)(2,1)S(1)}, u32[]{:S(2)}, u32[]{:S(2)}) collective-permute-start(bf16[512,128]{1,0:T(8,128)(2,1)S(1)} %get-tuple-element.84), channel_id=1, source_target_pairs={{0,16},{8,24},{16,0},{24,8},{1,17},{9,25},{17,1},{25,9},{2,18},{10... | collective-permute-start | bytes 393224 | tf_op jit(solution)/shard_map/ppermute | solution.py:25
  20.5 7.6 %collective-permute-start.15 = (bf16[24,2304]{1,0:T(8,128)(2,1)S(1)}, bf16[24,2304]{1,0:T(8,128)(2,1)S(1)}, u32[]{:S(2)}, u32[]{:S(2)}) collective-permute-start(bf16[24,2304]{1,0:T(8,128)(2,1)S(1)} %get-tuple-element.107), channel_id=1, source_target_pairs={{0,4},{1,5},{2,6},{3,7},{4,0},{5,1},{6,2},{7,3},{8,12},{9,13},{10,... | collective-permute-start | bytes 331784 | tf_op jit(solution)/shard_map/ppermute | solution.py:25
  22.0 11.3 %collective-permute-start.3 = (bf16[1024,128]{1,0:T(8,128)(2,1)S(1)}, bf16[1024,128]{1,0:T(8,128)(2,1)S(1)}, u32[]{:S(2)}, u32[]{:S(2)}) collective-permute-start(bf16[1024,128]{1,0:T(8,128)(2,1)S(1)} %get-tuple-element.87), channel_id=1, source_target_pairs={{0,8},{8,0},{16,24},{24,16},{1,9},{9,1},{17,25},{25,17},{2,10},{10... | collective-permute-start | bytes 786440 | tf_op jit(solution)/shard_map/ppermute | solution.py:25
  22.8 12.2 %collective-permute-start.4 = (bf16[1024,128]{1,0:T(8,128)(2,1)S(1)}, bf16[1024,128]{1,0:T(8,128)(2,1)S(1)}, u32[]{:S(2)}, u32[]{:S(2)}) collective-permute-start(bf16[1024,128]{1,0:T(8,128)(2,1)S(1)} %get-tuple-element.88), channel_id=1, source_target_pairs={{0,16},{8,24},{16,0},{24,8},{1,17},{9,25},{17,1},{25,9},{2,18},{10... | collective-permute-start | bytes 786440 | tf_op jit(solution)/shard_map/ppermute | solution.py:25
  23.7 11.3 %collective-permute-start.5 = (bf16[1024,128]{1,0:T(8,128)(2,1)S(1)}, bf16[1024,128]{1,0:T(8,128)(2,1)S(1)}, u32[]{:S(2)}, u32[]{:S(2)}) collective-permute-start(bf16[1024,128]{1,0:T(8,128)(2,1)S(1)} %get-tuple-element.89), channel_id=1, source_target_pairs={{0,24},{8,16},{16,8},{24,0},{1,25},{9,17},{17,9},{25,1},{2,26},{10... | collective-permute-start | bytes 786440 | tf_op jit(solution)/shard_map/ppermute | solution.py:25
  25.5 7.7 %collective-permute-start.10 = (bf16[2,24,2304]{2,1,0:T(8,128)(2,1)S(1)}, bf16[2,24,2304]{2,1,0:T(8,128)(2,1)S(1)}, u32[]{:S(2)}, u32[]{:S(2)}) collective-permute-start(bf16[2,24,2304]{2,1,0:T(8,128)(2,1)S(1)} %pad_maximum_fusion.6), channel_id=1, source_target_pairs={{0,2},{1,3},{2,0},{3,1},{4,6},{5,7},{6,4},{7,5},{8,10},{9,11},{10,... | collective-permute-start | bytes 663560 | tf_op jit(solution)/shard_map/ppermute | solution.py:25
  28.1 14.7 %collective-permute-start.16 = (bf16[2,24,2304]{2,1,0:T(8,128)(2,1)S(1)}, bf16[2,24,2304]{2,1,0:T(8,128)(2,1)S(1)}, u32[]{:S(2)}, u32[]{:S(2)}) collective-permute-start(bf16[2,24,2304]{2,1,0:T(8,128)(2,1)S(1)} %pad_maximum_fusion.7), channel_id=1, source_target_pairs={{0,2},{1,3},{2,0},{3,1},{4,6},{5,7},{6,4},{7,5},{8,10},{9,11},{10,... | collective-permute-start | bytes 663560 | tf_op jit(solution)/shard_map/ppermute | solution.py:25
  35.1 7.7 %collective-permute-start.23 = (bf16[24,2304]{1,0:T(8,128)(2,1)S(1)}, bf16[24,2304]{1,0:T(8,128)(2,1)S(1)}, u32[]{:S(2)}, u32[]{:S(2)}) collective-permute-start(bf16[24,2304]{1,0:T(8,128)(2,1)S(1)} %get-tuple-element.127), channel_id=1, source_target_pairs={{0,4},{1,5},{2,6},{3,7},{4,0},{5,1},{6,2},{7,3},{8,12},{9,13},{10,... | collective-permute-start | bytes 331784 | tf_op jit(solution)/shard_map/ppermute | solution.py:25
  39.2 7.3 %collective-permute-start.14 = (bf16[512,128]{1,0:T(8,128)(2,1)S(1)}, bf16[512,128]{1,0:T(8,128)(2,1)S(1)}, u32[]{:S(2)}, u32[]{:S(2)}) collective-permute-start(bf16[512,128]{1,0:T(8,128)(2,1)S(1)} %get-tuple-element.111.g0), channel_id=1, source_target_pairs={{0,24},{8,16},{16,8},{24,0},{1,25},{9,17},{17,9},{25,1},{2,26},{10... | collective-permute-start | bytes 393224 | tf_op jit(solution)/shard_map/ppermute | solution.py:25
  42.8 11.1 %collective-permute-start.24 = (bf16[2,24,2304]{2,1,0:T(8,128)(2,1)S(1)}, bf16[2,24,2304]{2,1,0:T(8,128)(2,1)S(1)}, u32[]{:S(2)}, u32[]{:S(2)}) collective-permute-start(bf16[2,24,2304]{2,1,0:T(8,128)(2,1)S(1)} %pad_maximum_fusion.8), channel_id=1, source_target_pairs={{0,2},{1,3},{2,0},{3,1},{4,6},{5,7},{6,4},{7,5},{8,10},{9,11},{10,... | collective-permute-start | bytes 663560 | tf_op jit(solution)/shard_map/ppermute | solution.py:25
  50.4 10.3 %collective-permute-start.20 = (bf16[512,128]{1,0:T(8,128)(2,1)S(1)}, bf16[512,128]{1,0:T(8,128)(2,1)S(1)}, u32[]{:S(2)}, u32[]{:S(2)}) collective-permute-start(bf16[512,128]{1,0:T(8,128)(2,1)S(1)} %get-tuple-element.123.g0), channel_id=1, source_target_pairs={{0,24},{8,16},{16,8},{24,0},{1,25},{9,17},{17,9},{25,1},{2,26},{10... | collective-permute-start | bytes 393224 | tf_op jit(solution)/shard_map/ppermute | solution.py:25
  51.7 9.0 %collective-permute-start.19 = (bf16[512,128]{1,0:T(8,128)(2,1)S(1)}, bf16[512,128]{1,0:T(8,128)(2,1)S(1)}, u32[]{:S(2)}, u32[]{:S(2)}) collective-permute-start(bf16[512,128]{1,0:T(8,128)(2,1)S(1)} %get-tuple-element.123.g0), channel_id=1, source_target_pairs={{0,16},{8,24},{16,0},{24,8},{1,17},{9,25},{17,1},{25,9},{2,18},{10... | collective-permute-start | bytes 393224 | tf_op jit(solution)/shard_map/ppermute | solution.py:25
  52.7 8.0 %collective-permute-start.18 = (bf16[512,128]{1,0:T(8,128)(2,1)S(1)}, bf16[512,128]{1,0:T(8,128)(2,1)S(1)}, u32[]{:S(2)}, u32[]{:S(2)}) collective-permute-start(bf16[512,128]{1,0:T(8,128)(2,1)S(1)} %get-tuple-element.123.g0), channel_id=1, source_target_pairs={{0,8},{8,0},{16,24},{24,16},{1,9},{9,1},{17,25},{25,17},{2,10},{10... | collective-permute-start | bytes 393224 | tf_op jit(solution)/shard_map/ppermute | solution.py:25
  59.0 10.8 %collective-permute-start.30 = (bf16[2,24,2304]{2,1,0:T(8,128)(2,1)S(1)}, bf16[2,24,2304]{2,1,0:T(8,128)(2,1)S(1)}, u32[]{:S(2)}, u32[]{:S(2)}) collective-permute-start(bf16[2,24,2304]{2,1,0:T(8,128)(2,1)S(1)} %get-tuple-element.122), channel_id=1, source_target_pairs={{0,2},{1,3},{2,0},{3,1},{4,6},{5,7},{6,4},{7,5},{8,10},{9,11},{10,... | collective-permute-start | bytes 663560 | tf_op jit(solution)/shard_map/ppermute | solution.py:25
  65.3 13.3 %collective-permute-start.28 = (bf16[512,128]{1,0:T(8,128)(2,1)S(1)}, bf16[512,128]{1,0:T(8,128)(2,1)S(1)}, u32[]{:S(2)}, u32[]{:S(2)}) collective-permute-start(bf16[512,128]{1,0:T(8,128)(2,1)S(1)} %get-tuple-element.139.g0), channel_id=1, source_target_pairs={{0,24},{8,16},{16,8},{24,0},{1,25},{9,17},{17,9},{25,1},{2,26},{10... | collective-permute-start | bytes 393224 | tf_op jit(solution)/shard_map/ppermute | solution.py:25
  67.0 11.7 %collective-permute-start.27 = (bf16[512,128]{1,0:T(8,128)(2,1)S(1)}, bf16[512,128]{1,0:T(8,128)(2,1)S(1)}, u32[]{:S(2)}, u32[]{:S(2)}) collective-permute-start(bf16[512,128]{1,0:T(8,128)(2,1)S(1)} %get-tuple-element.139.g0), channel_id=1, source_target_pairs={{0,16},{8,24},{16,0},{24,8},{1,17},{9,25},{17,1},{25,9},{2,18},{10... | collective-permute-start | bytes 393224 | tf_op jit(solution)/shard_map/ppermute | solution.py:25
  67.9 10.8 %collective-permute-start.26 = (bf16[512,128]{1,0:T(8,128)(2,1)S(1)}, bf16[512,128]{1,0:T(8,128)(2,1)S(1)}, u32[]{:S(2)}, u32[]{:S(2)}) collective-permute-start(bf16[512,128]{1,0:T(8,128)(2,1)S(1)} %get-tuple-element.139.g0), channel_id=1, source_target_pairs={{0,8},{8,0},{16,24},{24,16},{1,9},{9,1},{17,25},{25,17},{2,10},{10... | collective-permute-start | bytes 393224 | tf_op jit(solution)/shard_map/ppermute | solution.py:25
  69.8 7.1 %collective-permute-start.29 = (bf16[4,24,2304]{2,1,0:T(8,128)(2,1)S(1)}, bf16[4,24,2304]{2,1,0:T(8,128)(2,1)S(1)}, u32[]{:S(2)}, u32[]{:S(2)}) collective-permute-start(bf16[4,24,2304]{2,1,0:T(8,128)(2,1)S(1)} %get-tuple-element.133), channel_id=1, source_target_pairs={{0,1},{1,0},{2,3},{3,2},{4,5},{5,4},{6,7},{7,6},{8,9},{9,8},{10,11... | collective-permute-start | bytes 1327112 | tf_op jit(solution)/shard_map/ppermute | solution.py:25
  75.1 21.4 %collective-permute-start.38 = (bf16[24,2304]{1,0:T(8,128)(2,1)S(1)}, bf16[24,2304]{1,0:T(8,128)(2,1)S(1)}, u32[]{:S(2)}, u32[]{:S(2)}) collective-permute-start(bf16[24,2304]{1,0:T(8,128)(2,1)S(1)} %get-tuple-element.138), channel_id=1, source_target_pairs={{0,4},{1,5},{2,6},{3,7},{4,0},{5,1},{6,2},{7,3},{8,12},{9,13},{10,... | collective-permute-start | bytes 331784 | tf_op jit(solution)/shard_map/ppermute | solution.py:25
  81.9 14.6 %collective-permute-start.37 = (bf16[24,2304]{1,0:T(8,128)(2,1)S(1)}, bf16[24,2304]{1,0:T(8,128)(2,1)S(1)}, u32[]{:S(2)}, u32[]{:S(2)}) collective-permute-start(bf16[24,2304]{1,0:T(8,128)(2,1)S(1)} %get-tuple-element.152), channel_id=1, source_target_pairs={{0,4},{1,5},{2,6},{3,7},{4,0},{5,1},{6,2},{7,3},{8,12},{9,13},{10,... | collective-permute-start | bytes 331784 | tf_op jit(solution)/shard_map/ppermute | solution.py:25
  85.2 10.3 %collective-permute-start.32 = (bf16[2,24,2304]{2,1,0:T(8,128)(2,1)S(1)}, bf16[2,24,2304]{2,1,0:T(8,128)(2,1)S(1)}, u32[]{:S(2)}, u32[]{:S(2)}) collective-permute-start(bf16[2,24,2304]{2,1,0:T(8,128)(2,1)S(1)} %get-tuple-element.146), channel_id=1, source_target_pairs={{0,2},{1,3},{2,0},{3,1},{4,6},{5,7},{6,4},{7,5},{8,10},{9,11},{10,... | collective-permute-start | bytes 663560 | tf_op jit(solution)/shard_map/ppermute | solution.py:25
  86.2 10.3 %collective-permute-start.35 = (bf16[24,2304]{1,0:T(8,128)(2,1)S(1)}, bf16[24,2304]{1,0:T(8,128)(2,1)S(1)}, u32[]{:S(2)}, u32[]{:S(2)}) collective-permute-start(bf16[24,2304]{1,0:T(8,128)(2,1)S(1)} %get-tuple-element.150), channel_id=1, source_target_pairs={{0,4},{1,5},{2,6},{3,7},{4,0},{5,1},{6,2},{7,3},{8,12},{9,13},{10,... | collective-permute-start | bytes 331784 | tf_op jit(solution)/shard_map/ppermute | solution.py:25
  (24 other events, 130.2 us)

commit v5 on v4

--- a/solution.py
+++ b/solution.py
@@ -480,13 +480,13 @@
     terms2 = paired(*terms2)
     up, g0, terms1 = back_and_terms(1, tied(field1, terms2, terms3), up)
     field0 = spread([g0] * 4)
-    terms3 = reduced(*terms3, g0)
     terms1 = paired(*terms1)
-    terms0 = terms(tied(field0, terms1, terms3), pick(s, x_held))
+    terms0 = terms(tied(field0, terms1), pick(s, x_held))
+    terms3 = reduced(*terms3, terms0[0])
     terms0 = paired(*terms0)
     sum3 = summed(*terms3)
     terms2 = reduced(*terms2)
-    terms1 = reduced(*terms1)
+    terms1 = reduced(*terms1, terms0)
     terms0 = reduced(*terms0)
     sums = [summed(*terms0), summed(*terms1), summed(*terms2), sum3]
     owned = spread(

time: 113 us -> 112 us (level)
  starting transfers between devices: 45.2 us -> 43.8 us
    ppermute x42, starting transfers between devices: 45.2 us -> 43.8 us  [swapped(): lax.ppermute(x, axis, [(i, i ^ mask) for i in range(lax.axis_size(axis))])]
  transfers between devices with their start and end apart: 42 -> 42, of which waited for: 14 -> 14; matrix products, arithmetic and copies ran while one was open for 1% -> 1% of each run, Pallas kernels for 22% -> 23%
where the time goes in v5:
time: 112 us
  starting transfers between devices  43.8 us (39%)
  waiting for transfers between devices  36.8 us (33%)
  Pallas kernels  28.9 us (26%)
  local copies, waits for them, and re-layouts  1.19 us (1%)
    ppermute x42, starting transfers between devices, swapped(): lax.ppermute(x, axis, [(i, i ^ mask) for i in range(lax.axis_size(axis))])  43.8 us
    ppermute x42, waiting for transfers between devices, swapped(): lax.ppermute(x, axis, [(i, i ^ mask) for i in range(lax.axis_size(axis))])  36.8 us
    pallas_call x19, Pallas kernels, call(): pl.pallas_call(body, out_shape=out_shape, in_specs=[pl.BlockSpec(memory_s...  28.9 us
  transfers between devices with their start and end apart: 42, of which 14 were waited for; matrix products, arithmetic and copies ran while one was open for 1% of the time, Pallas kernels for 23%

profile of v5, /device:TPU:0, one launch (start us, length us, event | category | flops | bytes accessed | tf_op | source)
XLA Modules:
  0.0 111.8 jit_solution(8914458199426347858)
XLA Ops:
  2.1 3.0 %collective-permute-start.6 = (bf16[24,2304]{1,0:T(8,128)(2,1)S(1)}, bf16[24,2304]{1,0:T(8,128)(2,1)S(1)}, u32[]{:S(2)}, u32[]{:S(2)}) collective-permute-start(bf16[24,2304]{1,0:T(8,128)(2,1)S(1)} %get-tuple-element.92), channel_id=1, source_target_pairs={{0,8},{8,0},{16,24},{24,16},{1,9},{9,1},{17,25},{25,17},{2,10},{10... | collective-permute-start | bytes 331784 | tf_op jit(solution)/shard_map/ppermute | solution.py:25
  7.8 2.0 %collective-permute-start = (bf16[512,128]{1,0:T(8,128)(2,1)S(1)}, bf16[512,128]{1,0:T(8,128)(2,1)S(1)}, u32[]{:S(2)}, u32[]{:S(2)}) collective-permute-start(bf16[512,128]{1,0:T(8,128)(2,1)S(1)} %get-tuple-element.84), channel_id=1, source_target_pairs={{0,8},{8,0},{16,24},{24,16},{1,9},{9,1},{17,25},{25,17},{2,10},{10... | collective-permute-start | bytes 393224 | tf_op jit(solution)/shard_map/ppermute | solution.py:25
  11.8 1.7 %collective-permute-done.8 = bf16[24,2304]{1,0:T(8,128)(2,1)S(1)} collective-permute-done((bf16[24,2304]{1,0:T(8,128)(2,1)S(1)}, bf16[24,2304]{1,0:T(8,128)(2,1)S(1)}, u32[]{:S(2)}, u32[]{:S(2)}) %collective-permute-start.8) | collective-permute-done | bytes 110624 | tf_op jit(solution)/shard_map/ppermute | solution.py:25
  13.5 2.7 %collective-permute-start.9 = (bf16[24,2304]{1,0:T(8,128)(2,1)S(1)}, bf16[24,2304]{1,0:T(8,128)(2,1)S(1)}, u32[]{:S(2)}, u32[]{:S(2)}) collective-permute-start(bf16[24,2304]{1,0:T(8,128)(2,1)S(1)} %get-tuple-element.95), channel_id=1, source_target_pairs={{0,4},{1,5},{2,6},{3,7},{4,0},{5,1},{6,2},{7,3},{8,12},{9,13},{10,... | collective-permute-start | bytes 331784 | tf_op jit(solution)/shard_map/ppermute | solution.py:25
  16.2 1.7 %collective-permute-done.1 = bf16[512,128]{1,0:T(8,128)(2,1)S(1)} collective-permute-done((bf16[512,128]{1,0:T(8,128)(2,1)S(1)}, bf16[512,128]{1,0:T(8,128)(2,1)S(1)}, u32[]{:S(2)}, u32[]{:S(2)}) %collective-permute-start.1) | collective-permute-done | bytes 131104 | tf_op jit(solution)/shard_map/ppermute | solution.py:25
  20.5 1.6 %collective-permute-start.15 = (bf16[24,2304]{1,0:T(8,128)(2,1)S(1)}, bf16[24,2304]{1,0:T(8,128)(2,1)S(1)}, u32[]{:S(2)}, u32[]{:S(2)}) collective-permute-start(bf16[24,2304]{1,0:T(8,128)(2,1)S(1)} %get-tuple-element.108), channel_id=1, source_target_pairs={{0,4},{1,5},{2,6},{3,7},{4,0},{5,1},{6,2},{7,3},{8,12},{9,13},{10,... | collective-permute-start | bytes 331784 | tf_op jit(solution)/shard_map/ppermute | solution.py:25
  23.7 1.9 %collective-permute-start.5 = (bf16[1024,128]{1,0:T(8,128)(2,1)S(1)}, bf16[1024,128]{1,0:T(8,128)(2,1)S(1)}, u32[]{:S(2)}, u32[]{:S(2)}) collective-permute-start(bf16[1024,128]{1,0:T(8,128)(2,1)S(1)} %get-tuple-element.90), channel_id=1, source_target_pairs={{0,24},{8,16},{16,8},{24,0},{1,25},{9,17},{17,9},{25,1},{2,26},{10... | collective-permute-start | bytes 786440 | tf_op jit(solution)/shard_map/ppermute | solution.py:25
  25.5 2.5 %collective-permute-start.10 = (bf16[2,24,2304]{2,1,0:T(8,128)(2,1)S(1)}, bf16[2,24,2304]{2,1,0:T(8,128)(2,1)S(1)}, u32[]{:S(2)}, u32[]{:S(2)}) collective-permute-start(bf16[2,24,2304]{2,1,0:T(8,128)(2,1)S(1)} %pad_maximum_fusion.6), channel_id=1, source_target_pairs={{0,2},{1,3},{2,0},{3,1},{4,6},{5,7},{6,4},{7,5},{8,10},{9,11},{10,... | collective-permute-start | bytes 663560 | tf_op jit(solution)/shard_map/ppermute | solution.py:25
  28.6 4.7 %collective-permute-done.10 = bf16[2,24,2304]{2,1,0:T(8,128)(2,1)S(1)} collective-permute-done((bf16[2,24,2304]{2,1,0:T(8,128)(2,1)S(1)}, bf16[2,24,2304]{2,1,0:T(8,128)(2,1)S(1)}, u32[]{:S(2)}, u32[]{:S(2)}) %collective-permute-start.10) | collective-permute-done | bytes 221216 | tf_op jit(solution)/shard_map/ppermute | solution.py:25
  33.4 1.6 %collective-permute-done.4.g2 = bf16[1024,128]{1,0:T(8,128)(2,1)S(1)} collective-permute-done((bf16[1024,128]{1,0:T(8,128)(2,1)S(1)}, bf16[1024,128]{1,0:T(8,128)(2,1)S(1)}, u32[]{:S(2)}, u32[]{:S(2)}) %collective-permute-start.4) | collective-permute-done | bytes 262176 | tf_op jit(solution)/shard_map/ppermute | solution.py:25
  36.3 2.9 %shard_map.67 = (bf16[512,128]{1,0:T(8,128)(2,1)S(1)}, bf16[512,128]{1,0:T(8,128)(2,1)S(1)}) custom-call(s32[2]{0:T(128)S(1)} %pad_add_fusion.ids, bf16[1024,128]{1,0:T(8,128)(2,1)S(1)} %get-tuple-element.98.g0, bf16[1024,128]{1,0:T(8,128)(2,1)S(1)} %collective-permute-done.3.g1, bf16[1024,128]{1,0:T(8,128)(2,1)S(1)} %collective-permute-done.4.g2, ...), custom_call_target="tpu_custom_call" | custom-call | flops 34604998656 | tf_op jit(solution)/shard_map/pallas_call | solution.py:105
  41.2 1.6 %collective-permute-start.12 = (bf16[512,128]{1,0:T(8,128)(2,1)S(1)}, bf16[512,128]{1,0:T(8,128)(2,1)S(1)}, u32[]{:S(2)}, u32[]{:S(2)}) collective-permute-start(bf16[512,128]{1,0:T(8,128)(2,1)S(1)} %get-tuple-element.112.g0), channel_id=1, source_target_pairs={{0,8},{8,0},{16,24},{24,16},{1,9},{9,1},{17,25},{25,17},{2,10},{10... | collective-permute-start | bytes 393224 | tf_op jit(solution)/shard_map/ppermute | solution.py:25
  43.9 2.6 %shard_map.68 = (f32[4,24,2304]{2,1,0:T(8,128)S(1)}, bf16[4,24,2304]{2,1,0:T(8,128)(2,1)S(1)}) custom-call(s32[2]{0:T(128)S(1)} %pad_add_fusion.ids, bf16[1024,128]{1,0:T(8,128)(2,1)S(1)} %get-tuple-element.98.g0, bf16[1024,128]{1,0:T(8,128)(2,1)S(1)} %collective-permute-done.3.g1, bf16[1024,128]{1,0:T(8,128)(2,1)S(1)} %collective-permute-done.4.g2, ...), custom_call_target="tpu_custom_call" | custom-call | flops 29991000064 | tf_op jit(solution)/shard_map/pallas_call | solution.py:105
  47.4 2.9 %shard_map.69 = (bf16[512,128]{1,0:T(8,128)(2,1)S(1)}, bf16[512,128]{1,0:T(8,128)(2,1)S(1)}) custom-call(s32[2]{0:T(128)S(1)} %pad_add_fusion.ids, bf16[512,128]{1,0:T(8,128)(2,1)S(1)} %get-tuple-element.112.g0, bf16[512,128]{1,0:T(8,128)(2,1)S(1)} %collective-permute-done.12.g1, bf16[512,128]{1,0:T(8,128)(2,1)S(1)} %collective-permute-done.13.g2, ...), custom_call_target="tpu_custom_call" | custom-call | flops 34604998656 | tf_op jit(solution)/shard_map/pallas_call | solution.py:105
  54.6 2.6 %shard_map.70 = (f32[4,24,2304]{2,1,0:T(8,128)S(1)}, bf16[4,24,2304]{2,1,0:T(8,128)(2,1)S(1)}) custom-call(s32[2]{0:T(128)S(1)} %pad_add_fusion.ids, bf16[512,128]{1,0:T(8,128)(2,1)S(1)} %get-tuple-element.112.g0, bf16[512,128]{1,0:T(8,128)(2,1)S(1)} %collective-permute-done.12.g1, bf16[512,128]{1,0:T(8,128)(2,1)S(1)} %collective-permute-done.13.g2, ...), custom_call_target="tpu_custom_call" | custom-call | flops 29991000064 | tf_op jit(solution)/shard_map/pallas_call | solution.py:105
  61.9 4.5 %shard_map.73 = (bf16[512,128]{1,0:T(8,128)(2,1)}, bf16[512,128]{1,0:T(8,128)(2,1)S(1)}, f32[4,24,2304]{2,1,0:T(8,128)S(1)}, bf16[4,24,2304]{2,1,0:T(8,128)(2,1)S(1)}) custom-call(s32[2]{0:T(128)S(1)} %pad_add_fusion.ids, bf16[512,128]{1,0:T(8,128)(2,1)S(1)} %get-tuple-element.124.g0, bf16[512,128]{1,0:T(8,128)(2,1)S(1)} %collective-permute-done.18.g1, ...), custom_call_target="tpu_custom_call" | custom-call | flops 43832999936 | tf_op jit(solution)/shard_map/pallas_call | solution.py:105
  73.0 1.8 %collective-permute-start.36 = (bf16[24,2304]{1,0:T(8,128)(2,1)S(1)}, bf16[24,2304]{1,0:T(8,128)(2,1)S(1)}, u32[]{:S(2)}, u32[]{:S(2)}) collective-permute-start(bf16[24,2304]{1,0:T(8,128)(2,1)S(1)} %get-tuple-element.151), channel_id=1, source_target_pairs={{0,4},{1,5},{2,6},{3,7},{4,0},{5,1},{6,2},{7,3},{8,12},{9,13},{10,... | collective-permute-start | bytes 331784 | tf_op jit(solution)/shard_map/ppermute | solution.py:25
  76.6 2.6 %shard_map.75 = (f32[4,24,2304]{2,1,0:T(8,128)S(1)}, bf16[4,24,2304]{2,1,0:T(8,128)(2,1)S(1)}) custom-call(s32[2]{0:T(128)S(1)} %pad_add_fusion.ids, bf16[512,128]{1,0:T(8,128)(2,1)S(1)} %get-tuple-element.137.g0, bf16[512,128]{1,0:T(8,128)(2,1)S(1)} %collective-permute-done.26.g1, bf16[512,128]{1,0:T(8,128)(2,1)S(1)} %collective-permute-done.27.g2, ...), custom_call_target="tpu_custom_call" | custom-call | flops 29991000064 | tf_op jit(solution)/shard_map/pallas_call | solution.py:105
  82.8 2.7 %collective-permute-done.33.other = bf16[2,24,2304]{2,1,0:T(8,128)(2,1)S(1)} collective-permute-done((bf16[2,24,2304]{2,1,0:T(8,128)(2,1)S(1)}, bf16[2,24,2304]{2,1,0:T(8,128)(2,1)S(1)}, u32[]{:S(2)}, u32[]{:S(2)}) %collective-permute-start.33) | collective-permute-done | bytes 221216 | tf_op jit(solution)/shard_map/ppermute | solution.py:25
  86.1 7.7 %collective-permute-done.31.other = bf16[2,24,2304]{2,1,0:T(8,128)(2,1)S(1)} collective-permute-done((bf16[2,24,2304]{2,1,0:T(8,128)(2,1)S(1)}, bf16[2,24,2304]{2,1,0:T(8,128)(2,1)S(1)}, u32[]{:S(2)}, u32[]{:S(2)}) %collective-permute-start.31) | collective-permute-done | bytes 221216 | tf_op jit(solution)/shard_map/ppermute | solution.py:25
  94.5 7.1 %collective-permute-done.32.refs_1_ = bf16[24,2304]{1,0:T(8,128)(2,1)S(1)} collective-permute-done((bf16[24,2304]{1,0:T(8,128)(2,1)S(1)}, bf16[24,2304]{1,0:T(8,128)(2,1)S(1)}, u32[]{:S(2)}, u32[]{:S(2)}) %collective-permute-start.32) | collective-permute-done | bytes 110624 | tf_op jit(solution)/shard_map/ppermute | solution.py:25
  103.7 2.3 %collective-permute-start.41 = (bf16[24,2304]{1,0:T(8,128)(2,1)S(1)}, bf16[24,2304]{1,0:T(8,128)(2,1)S(1)}, u32[]{:S(2)}, u32[]{:S(2)}) collective-permute-start(bf16[24,2304]{1,0:T(8,128)(2,1)S(1)} %get-tuple-element.158), channel_id=1, source_target_pairs={{0,24},{8,16},{16,8},{24,0},{1,25},{9,17},{17,9},{25,1},{2,26},{10... | collective-permute-start | bytes 331784 | tf_op jit(solution)/shard_map/ppermute | solution.py:25
  105.9 2.4 %collective-permute-done.39.f1 = bf16[24,2304]{1,0:T(8,128)(2,1)S(1)} collective-permute-done((bf16[24,2304]{1,0:T(8,128)(2,1)S(1)}, bf16[24,2304]{1,0:T(8,128)(2,1)S(1)}, u32[]{:S(2)}, u32[]{:S(2)}) %collective-permute-start.39) | collective-permute-done | bytes 110624 | tf_op jit(solution)/shard_map/ppermute | solution.py:25
  109.9 1.9 %shard_map.82 = f32[27,32,256]{2,1,0:T(8,128)} custom-call(s32[2]{0:T(128)S(1)} %pad_add_fusion.ids, bf16[24,2304]{1,0:T(8,128)(2,1)S(1)} %get-tuple-element.155.f0, bf16[24,2304]{1,0:T(8,128)(2,1)S(1)} %collective-permute-done.39.f1, bf16[24,2304]{1,0:T(8,128)(2,1)S(1)} %collective-permute-done.40.f2, bf16[24,2304]{1,0:T(8,128)(2,1)S(1)} %collective-permute-done.41.f3, ...), custom_call_target="tpu_custom_call" | custom-call | flops 23069999104 | tf_op jit(solution)/shard_map/pallas_call | solution.py:105
  (105 shorter events, 42.5 us)
Async XLA Ops:
  2.1 9.2 %collective-permute-start.6 = (bf16[24,2304]{1,0:T(8,128)(2,1)S(1)}, bf16[24,2304]{1,0:T(8,128)(2,1)S(1)}, u32[]{:S(2)}, u32[]{:S(2)}) collective-permute-start(bf16[24,2304]{1,0:T(8,128)(2,1)S(1)} %get-tuple-element.92), channel_id=1, source_target_pairs={{0,8},{8,0},{16,24},{24,16},{1,9},{9,1},{17,25},{25,17},{2,10},{10... | collective-permute-start | bytes 331784 | tf_op jit(solution)/shard_map/ppermute | solution.py:25
  7.8 8.4 %collective-permute-start = (bf16[512,128]{1,0:T(8,128)(2,1)S(1)}, bf16[512,128]{1,0:T(8,128)(2,1)S(1)}, u32[]{:S(2)}, u32[]{:S(2)}) collective-permute-start(bf16[512,128]{1,0:T(8,128)(2,1)S(1)} %get-tuple-element.84), channel_id=1, source_target_pairs={{0,8},{8,0},{16,24},{24,16},{1,9},{9,1},{17,25},{25,17},{2,10},{10... | collective-permute-start | bytes 393224 | tf_op jit(solution)/shard_map/ppermute | solution.py:25
  9.8 8.1 %collective-permute-start.1 = (bf16[512,128]{1,0:T(8,128)(2,1)S(1)}, bf16[512,128]{1,0:T(8,128)(2,1)S(1)}, u32[]{:S(2)}, u32[]{:S(2)}) collective-permute-start(bf16[512,128]{1,0:T(8,128)(2,1)S(1)} %get-tuple-element.85), channel_id=1, source_target_pairs={{0,16},{8,24},{16,0},{24,8},{1,17},{9,25},{17,1},{25,9},{2,18},{10... | collective-permute-start | bytes 393224 | tf_op jit(solution)/shard_map/ppermute | solution.py:25
  22.0 11.3 %collective-permute-start.3 = (bf16[1024,128]{1,0:T(8,128)(2,1)S(1)}, bf16[1024,128]{1,0:T(8,128)(2,1)S(1)}, u32[]{:S(2)}, u32[]{:S(2)}) collective-permute-start(bf16[1024,128]{1,0:T(8,128)(2,1)S(1)} %get-tuple-element.88), channel_id=1, source_target_pairs={{0,8},{8,0},{16,24},{24,16},{1,9},{9,1},{17,25},{25,17},{2,10},{10... | collective-permute-start | bytes 786440 | tf_op jit(solution)/shard_map/ppermute | solution.py:25
  22.8 12.2 %collective-permute-start.4 = (bf16[1024,128]{1,0:T(8,128)(2,1)S(1)}, bf16[1024,128]{1,0:T(8,128)(2,1)S(1)}, u32[]{:S(2)}, u32[]{:S(2)}) collective-permute-start(bf16[1024,128]{1,0:T(8,128)(2,1)S(1)} %get-tuple-element.89), channel_id=1, source_target_pairs={{0,16},{8,24},{16,0},{24,8},{1,17},{9,25},{17,1},{25,9},{2,18},{10... | collective-permute-start | bytes 786440 | tf_op jit(solution)/shard_map/ppermute | solution.py:25
  23.7 11.3 %collective-permute-start.5 = (bf16[1024,128]{1,0:T(8,128)(2,1)S(1)}, bf16[1024,128]{1,0:T(8,128)(2,1)S(1)}, u32[]{:S(2)}, u32[]{:S(2)}) collective-permute-start(bf16[1024,128]{1,0:T(8,128)(2,1)S(1)} %get-tuple-element.90), channel_id=1, source_target_pairs={{0,24},{8,16},{16,8},{24,0},{1,25},{9,17},{17,9},{25,1},{2,26},{10... | collective-permute-start | bytes 786440 | tf_op jit(solution)/shard_map/ppermute | solution.py:25
  25.5 7.7 %collective-permute-start.10 = (bf16[2,24,2304]{2,1,0:T(8,128)(2,1)S(1)}, bf16[2,24,2304]{2,1,0:T(8,128)(2,1)S(1)}, u32[]{:S(2)}, u32[]{:S(2)}) collective-permute-start(bf16[2,24,2304]{2,1,0:T(8,128)(2,1)S(1)} %pad_maximum_fusion.6), channel_id=1, source_target_pairs={{0,2},{1,3},{2,0},{3,1},{4,6},{5,7},{6,4},{7,5},{8,10},{9,11},{10,... | collective-permute-start | bytes 663560 | tf_op jit(solution)/shard_map/ppermute | solution.py:25
  28.1 14.7 %collective-permute-start.16 = (bf16[2,24,2304]{2,1,0:T(8,128)(2,1)S(1)}, bf16[2,24,2304]{2,1,0:T(8,128)(2,1)S(1)}, u32[]{:S(2)}, u32[]{:S(2)}) collective-permute-start(bf16[2,24,2304]{2,1,0:T(8,128)(2,1)S(1)} %pad_maximum_fusion.7), channel_id=1, source_target_pairs={{0,2},{1,3},{2,0},{3,1},{4,6},{5,7},{6,4},{7,5},{8,10},{9,11},{10,... | collective-permute-start | bytes 663560 | tf_op jit(solution)/shard_map/ppermute | solution.py:25
  35.1 7.7 %collective-permute-start.23 = (bf16[24,2304]{1,0:T(8,128)(2,1)S(1)}, bf16[24,2304]{1,0:T(8,128)(2,1)S(1)}, u32[]{:S(2)}, u32[]{:S(2)}) collective-permute-start(bf16[24,2304]{1,0:T(8,128)(2,1)S(1)} %get-tuple-element.128), channel_id=1, source_target_pairs={{0,4},{1,5},{2,6},{3,7},{4,0},{5,1},{6,2},{7,3},{8,12},{9,13},{10,... | collective-permute-start | bytes 331784 | tf_op jit(solution)/shard_map/ppermute | solution.py:25
  42.8 11.1 %collective-permute-start.24 = (bf16[2,24,2304]{2,1,0:T(8,128)(2,1)S(1)}, bf16[2,24,2304]{2,1,0:T(8,128)(2,1)S(1)}, u32[]{:S(2)}, u32[]{:S(2)}) collective-permute-start(bf16[2,24,2304]{2,1,0:T(8,128)(2,1)S(1)} %pad_maximum_fusion.8), channel_id=1, source_target_pairs={{0,2},{1,3},{2,0},{3,1},{4,6},{5,7},{6,4},{7,5},{8,10},{9,11},{10,... | collective-permute-start | bytes 663560 | tf_op jit(solution)/shard_map/ppermute | solution.py:25
  50.4 10.3 %collective-permute-start.20 = (bf16[512,128]{1,0:T(8,128)(2,1)S(1)}, bf16[512,128]{1,0:T(8,128)(2,1)S(1)}, u32[]{:S(2)}, u32[]{:S(2)}) collective-permute-start(bf16[512,128]{1,0:T(8,128)(2,1)S(1)} %get-tuple-element.124.g0), channel_id=1, source_target_pairs={{0,24},{8,16},{16,8},{24,0},{1,25},{9,17},{17,9},{25,1},{2,26},{10... | collective-permute-start | bytes 393224 | tf_op jit(solution)/shard_map/ppermute | solution.py:25
  51.7 10.0 %collective-permute-start.19 = (bf16[512,128]{1,0:T(8,128)(2,1)S(1)}, bf16[512,128]{1,0:T(8,128)(2,1)S(1)}, u32[]{:S(2)}, u32[]{:S(2)}) collective-permute-start(bf16[512,128]{1,0:T(8,128)(2,1)S(1)} %get-tuple-element.124.g0), channel_id=1, source_target_pairs={{0,16},{8,24},{16,0},{24,8},{1,17},{9,25},{17,1},{25,9},{2,18},{10... | collective-permute-start | bytes 393224 | tf_op jit(solution)/shard_map/ppermute | solution.py:25
  52.7 9.0 %collective-permute-start.18 = (bf16[512,128]{1,0:T(8,128)(2,1)S(1)}, bf16[512,128]{1,0:T(8,128)(2,1)S(1)}, u32[]{:S(2)}, u32[]{:S(2)}) collective-permute-start(bf16[512,128]{1,0:T(8,128)(2,1)S(1)} %get-tuple-element.124.g0), channel_id=1, source_target_pairs={{0,8},{8,0},{16,24},{24,16},{1,9},{9,1},{17,25},{25,17},{2,10},{10... | collective-permute-start | bytes 393224 | tf_op jit(solution)/shard_map/ppermute | solution.py:25
  54.0 7.8 %collective-permute-start.25 = (bf16[4,24,2304]{2,1,0:T(8,128)(2,1)S(1)}, bf16[4,24,2304]{2,1,0:T(8,128)(2,1)S(1)}, u32[]{:S(2)}, u32[]{:S(2)}) collective-permute-start(bf16[4,24,2304]{2,1,0:T(8,128)(2,1)S(1)} %pad_maximum_fusion.5), channel_id=1, source_target_pairs={{0,1},{1,0},{2,3},{3,2},{4,5},{5,4},{6,7},{7,6},{8,9},{9,8},{10,11... | collective-permute-start | bytes 1327112 | tf_op jit(solution)/shard_map/ppermute | solution.py:25
  59.0 20.1 %collective-permute-start.37 = (bf16[2,24,2304]{2,1,0:T(8,128)(2,1)S(1)}, bf16[2,24,2304]{2,1,0:T(8,128)(2,1)S(1)}, u32[]{:S(2)}, u32[]{:S(2)}) collective-permute-start(bf16[2,24,2304]{2,1,0:T(8,128)(2,1)S(1)} %get-tuple-element.123), channel_id=1, source_target_pairs={{0,2},{1,3},{2,0},{3,1},{4,6},{5,7},{6,4},{7,5},{8,10},{9,11},{10,... | collective-permute-start | bytes 663560 | tf_op jit(solution)/shard_map/ppermute | solution.py:25
  60.7 10.5 %collective-permute-start.35 = (bf16[2,24,2304]{2,1,0:T(8,128)(2,1)S(1)}, bf16[2,24,2304]{2,1,0:T(8,128)(2,1)S(1)}, u32[]{:S(2)}, u32[]{:S(2)}) collective-permute-start(bf16[2,24,2304]{2,1,0:T(8,128)(2,1)S(1)} %get-tuple-element.119), channel_id=1, source_target_pairs={{0,2},{1,3},{2,0},{3,1},{4,6},{5,7},{6,4},{7,5},{8,10},{9,11},{10,... | collective-permute-start | bytes 663560 | tf_op jit(solution)/shard_map/ppermute | solution.py:25
  66.3 9.1 %collective-permute-start.28 = (bf16[512,128]{1,0:T(8,128)(2,1)S(1)}, bf16[512,128]{1,0:T(8,128)(2,1)S(1)}, u32[]{:S(2)}, u32[]{:S(2)}) collective-permute-start(bf16[512,128]{1,0:T(8,128)(2,1)S(1)} %get-tuple-element.137.g0), channel_id=1, source_target_pairs={{0,24},{8,16},{16,8},{24,0},{1,25},{9,17},{17,9},{25,1},{2,26},{10... | collective-permute-start | bytes 393224 | tf_op jit(solution)/shard_map/ppermute | solution.py:25
  67.6 9.0 %collective-permute-start.27 = (bf16[512,128]{1,0:T(8,128)(2,1)S(1)}, bf16[512,128]{1,0:T(8,128)(2,1)S(1)}, u32[]{:S(2)}, u32[]{:S(2)}) collective-permute-start(bf16[512,128]{1,0:T(8,128)(2,1)S(1)} %get-tuple-element.137.g0), channel_id=1, source_target_pairs={{0,16},{8,24},{16,0},{24,8},{1,17},{9,25},{17,1},{25,9},{2,18},{10... | collective-permute-start | bytes 393224 | tf_op jit(solution)/shard_map/ppermute | solution.py:25
  68.6 8.0 %collective-permute-start.26 = (bf16[512,128]{1,0:T(8,128)(2,1)S(1)}, bf16[512,128]{1,0:T(8,128)(2,1)S(1)}, u32[]{:S(2)}, u32[]{:S(2)}) collective-permute-start(bf16[512,128]{1,0:T(8,128)(2,1)S(1)} %get-tuple-element.137.g0), channel_id=1, source_target_pairs={{0,8},{8,0},{16,24},{24,16},{1,9},{9,1},{17,25},{25,17},{2,10},{10... | collective-permute-start | bytes 393224 | tf_op jit(solution)/shard_map/ppermute | solution.py:25
  73.0 21.5 %collective-permute-start.36 = (bf16[24,2304]{1,0:T(8,128)(2,1)S(1)}, bf16[24,2304]{1,0:T(8,128)(2,1)S(1)}, u32[]{:S(2)}, u32[]{:S(2)}) collective-permute-start(bf16[24,2304]{1,0:T(8,128)(2,1)S(1)} %get-tuple-element.151), channel_id=1, source_target_pairs={{0,4},{1,5},{2,6},{3,7},{4,0},{5,1},{6,2},{7,3},{8,12},{9,13},{10,... | collective-permute-start | bytes 331784 | tf_op jit(solution)/shard_map/ppermute | solution.py:25
  75.5 10.0 %collective-permute-start.33 = (bf16[2,24,2304]{2,1,0:T(8,128)(2,1)S(1)}, bf16[2,24,2304]{2,1,0:T(8,128)(2,1)S(1)}, u32[]{:S(2)}, u32[]{:S(2)}) collective-permute-start(bf16[2,24,2304]{2,1,0:T(8,128)(2,1)S(1)} %get-tuple-element.136), channel_id=1, source_target_pairs={{0,2},{1,3},{2,0},{3,1},{4,6},{5,7},{6,4},{7,5},{8,10},{9,11},{10,... | collective-permute-start | bytes 663560 | tf_op jit(solution)/shard_map/ppermute | solution.py:25
  79.8 14.7 %collective-permute-start.38 = (bf16[24,2304]{1,0:T(8,128)(2,1)S(1)}, bf16[24,2304]{1,0:T(8,128)(2,1)S(1)}, u32[]{:S(2)}, u32[]{:S(2)}) collective-permute-start(bf16[24,2304]{1,0:T(8,128)(2,1)S(1)} %get-tuple-element.154), channel_id=1, source_target_pairs={{0,4},{1,5},{2,6},{3,7},{4,0},{5,1},{6,2},{7,3},{8,12},{9,13},{10,... | collective-permute-start | bytes 331784 | tf_op jit(solution)/shard_map/ppermute | solution.py:25
  81.7 12.1 %collective-permute-start.31 = (bf16[2,24,2304]{2,1,0:T(8,128)(2,1)S(1)}, bf16[2,24,2304]{2,1,0:T(8,128)(2,1)S(1)}, u32[]{:S(2)}, u32[]{:S(2)}) collective-permute-start(bf16[2,24,2304]{2,1,0:T(8,128)(2,1)S(1)} %get-tuple-element.144), channel_id=1, source_target_pairs={{0,2},{1,3},{2,0},{3,1},{4,6},{5,7},{6,4},{7,5},{8,10},{9,11},{10,... | collective-permute-start | bytes 663560 | tf_op jit(solution)/shard_map/ppermute | solution.py:25
  86.0 8.5 %collective-permute-start.34 = (bf16[24,2304]{1,0:T(8,128)(2,1)S(1)}, bf16[24,2304]{1,0:T(8,128)(2,1)S(1)}, u32[]{:S(2)}, u32[]{:S(2)}) collective-permute-start(bf16[24,2304]{1,0:T(8,128)(2,1)S(1)} %get-tuple-element.149), channel_id=1, source_target_pairs={{0,4},{1,5},{2,6},{3,7},{4,0},{5,1},{6,2},{7,3},{8,12},{9,13},{10,... | collective-permute-start | bytes 331784 | tf_op jit(solution)/shard_map/ppermute | solution.py:25
  (24 other events, 129.3 us)

commit v6 on v5

--- a/solution.py
+++ b/solution.py
@@ -471,12 +471,11 @@
     kernels[2] = both_cores(chips2)
     half1 = far_half(after(pick(s ^ 1, w_held), chips3), g2)
     terms3 = terms(tied(field3, g2), pick(s ^ 3, x_held))
-    up, g1 = back(2, tied(field2, terms3), up)
+    up, g1, terms2 = back_and_terms(2, tied(field2, terms3), up)
     field1 = spread([g1] * 4)
     chips1 = all_chips(half1, g1)
     kernels[1] = both_cores(chips1)
     terms3 = paired(*tied(terms3, g1))
-    terms2 = terms(tied(field2, g1), pick(s ^ 2, x_held))
     terms2 = paired(*terms2)
     up, g0, terms1 = back_and_terms(1, tied(field1, terms2, terms3), up)
     field0 = spread([g0] * 4)

time: 112 us -> 111 us (level)
  Pallas kernels: 28.9 us -> 27.1 us
    pallas_call x19 -> x18, Pallas kernels: 28.9 us -> 27.1 us  [call(): pl.pallas_call(body, out_shape=out_shape, in_specs=[pl.BlockSpec(memory_s...]
  transfers between devices with their start and end apart: 42 -> 42, of which waited for: 14 -> 16; matrix products, arithmetic and copies ran while one was open for 1% -> 1% of each run, Pallas kernels for 23% -> 21%
where the time goes in v6:
time: 111 us
  starting transfers between devices  44.6 us (40%)
  waiting for transfers between devices  36.9 us (33%)
  Pallas kernels  27.1 us (24%)
  local copies, waits for them, and re-layouts  1.19 us (1%)
    ppermute x42, starting transfers between devices, swapped(): lax.ppermute(x, axis, [(i, i ^ mask) for i in range(lax.axis_size(axis))])  44.6 us
    ppermute x42, waiting for transfers between devices, swapped(): lax.ppermute(x, axis, [(i, i ^ mask) for i in range(lax.axis_size(axis))])  36.9 us
    pallas_call x18, Pallas kernels, call(): pl.pallas_call(body, out_shape=out_shape, in_specs=[pl.BlockSpec(memory_s...  27.1 us
  transfers between devices with their start and end apart: 42, of which 16 were waited for; matrix products, arithmetic and copies ran while one was open for 1% of the time, Pallas kernels for 21%

profile of v6, /device:TPU:0, one launch (start us, length us, event | category | flops | bytes accessed | tf_op | source)
XLA Modules:
  0.0 110.9 jit_solution(10528559186583784237)
XLA Ops:
  2.1 3.0 %collective-permute-start.6 = (bf16[24,2304]{1,0:T(8,128)(2,1)S(1)}, bf16[24,2304]{1,0:T(8,128)(2,1)S(1)}, u32[]{:S(2)}, u32[]{:S(2)}) collective-permute-start(bf16[24,2304]{1,0:T(8,128)(2,1)S(1)} %get-tuple-element.88), channel_id=1, source_target_pairs={{0,8},{8,0},{16,24},{24,16},{1,9},{9,1},{17,25},{25,17},{2,10},{10... | collective-permute-start | bytes 331784 | tf_op jit(solution)/shard_map/ppermute | solution.py:25
  7.8 2.0 %collective-permute-start = (bf16[512,128]{1,0:T(8,128)(2,1)S(1)}, bf16[512,128]{1,0:T(8,128)(2,1)S(1)}, u32[]{:S(2)}, u32[]{:S(2)}) collective-permute-start(bf16[512,128]{1,0:T(8,128)(2,1)S(1)} %get-tuple-element.80), channel_id=1, source_target_pairs={{0,8},{8,0},{16,24},{24,16},{1,9},{9,1},{17,25},{25,17},{2,10},{10... | collective-permute-start | bytes 393224 | tf_op jit(solution)/shard_map/ppermute | solution.py:25
  11.8 1.7 %collective-permute-done.8 = bf16[24,2304]{1,0:T(8,128)(2,1)S(1)} collective-permute-done((bf16[24,2304]{1,0:T(8,128)(2,1)S(1)}, bf16[24,2304]{1,0:T(8,128)(2,1)S(1)}, u32[]{:S(2)}, u32[]{:S(2)}) %collective-permute-start.8) | collective-permute-done | bytes 110624 | tf_op jit(solution)/shard_map/ppermute | solution.py:25
  13.5 2.7 %collective-permute-start.9 = (bf16[24,2304]{1,0:T(8,128)(2,1)S(1)}, bf16[24,2304]{1,0:T(8,128)(2,1)S(1)}, u32[]{:S(2)}, u32[]{:S(2)}) collective-permute-start(bf16[24,2304]{1,0:T(8,128)(2,1)S(1)} %get-tuple-element.91), channel_id=1, source_target_pairs={{0,4},{1,5},{2,6},{3,7},{4,0},{5,1},{6,2},{7,3},{8,12},{9,13},{10,... | collective-permute-start | bytes 331784 | tf_op jit(solution)/shard_map/ppermute | solution.py:25
  16.2 1.7 %collective-permute-done.1 = bf16[512,128]{1,0:T(8,128)(2,1)S(1)} collective-permute-done((bf16[512,128]{1,0:T(8,128)(2,1)S(1)}, bf16[512,128]{1,0:T(8,128)(2,1)S(1)}, u32[]{:S(2)}, u32[]{:S(2)}) %collective-permute-start.1) | collective-permute-done | bytes 131104 | tf_op jit(solution)/shard_map/ppermute | solution.py:25
  20.5 1.6 %collective-permute-start.15 = (bf16[24,2304]{1,0:T(8,128)(2,1)S(1)}, bf16[24,2304]{1,0:T(8,128)(2,1)S(1)}, u32[]{:S(2)}, u32[]{:S(2)}) collective-permute-start(bf16[24,2304]{1,0:T(8,128)(2,1)S(1)} %get-tuple-element.104), channel_id=1, source_target_pairs={{0,4},{1,5},{2,6},{3,7},{4,0},{5,1},{6,2},{7,3},{8,12},{9,13},{10,... | collective-permute-start | bytes 331784 | tf_op jit(solution)/shard_map/ppermute | solution.py:25
  23.7 1.9 %collective-permute-start.5 = (bf16[1024,128]{1,0:T(8,128)(2,1)S(1)}, bf16[1024,128]{1,0:T(8,128)(2,1)S(1)}, u32[]{:S(2)}, u32[]{:S(2)}) collective-permute-start(bf16[1024,128]{1,0:T(8,128)(2,1)S(1)} %get-tuple-element.86), channel_id=1, source_target_pairs={{0,24},{8,16},{16,8},{24,0},{1,25},{9,17},{17,9},{25,1},{2,26},{10... | collective-permute-start | bytes 786440 | tf_op jit(solution)/shard_map/ppermute | solution.py:25
  25.5 2.5 %collective-permute-start.10 = (bf16[2,24,2304]{2,1,0:T(8,128)(2,1)S(1)}, bf16[2,24,2304]{2,1,0:T(8,128)(2,1)S(1)}, u32[]{:S(2)}, u32[]{:S(2)}) collective-permute-start(bf16[2,24,2304]{2,1,0:T(8,128)(2,1)S(1)} %pad_maximum_fusion.6), channel_id=1, source_target_pairs={{0,2},{1,3},{2,0},{3,1},{4,6},{5,7},{6,4},{7,5},{8,10},{9,11},{10,... | collective-permute-start | bytes 663560 | tf_op jit(solution)/shard_map/ppermute | solution.py:25
  28.6 4.7 %collective-permute-done.10 = bf16[2,24,2304]{2,1,0:T(8,128)(2,1)S(1)} collective-permute-done((bf16[2,24,2304]{2,1,0:T(8,128)(2,1)S(1)}, bf16[2,24,2304]{2,1,0:T(8,128)(2,1)S(1)}, u32[]{:S(2)}, u32[]{:S(2)}) %collective-permute-start.10) | collective-permute-done | bytes 221216 | tf_op jit(solution)/shard_map/ppermute | solution.py:25
  33.4 1.6 %collective-permute-done.4.g2 = bf16[1024,128]{1,0:T(8,128)(2,1)S(1)} collective-permute-done((bf16[1024,128]{1,0:T(8,128)(2,1)S(1)}, bf16[1024,128]{1,0:T(8,128)(2,1)S(1)}, u32[]{:S(2)}, u32[]{:S(2)}) %collective-permute-start.4) | collective-permute-done | bytes 262176 | tf_op jit(solution)/shard_map/ppermute | solution.py:25
  36.3 2.9 %shard_map.67 = (bf16[512,128]{1,0:T(8,128)(2,1)S(1)}, bf16[512,128]{1,0:T(8,128)(2,1)S(1)}) custom-call(s32[2]{0:T(128)S(1)} %pad_add_fusion.ids, bf16[1024,128]{1,0:T(8,128)(2,1)S(1)} %get-tuple-element.94.g0, bf16[1024,128]{1,0:T(8,128)(2,1)S(1)} %collective-permute-done.3.g1, bf16[1024,128]{1,0:T(8,128)(2,1)S(1)} %collective-permute-done.4.g2, ...), custom_call_target="tpu_custom_call" | custom-call | flops 34604998656 | tf_op jit(solution)/shard_map/pallas_call | solution.py:105
  41.2 1.6 %collective-permute-start.12 = (bf16[512,128]{1,0:T(8,128)(2,1)S(1)}, bf16[512,128]{1,0:T(8,128)(2,1)S(1)}, u32[]{:S(2)}, u32[]{:S(2)}) collective-permute-start(bf16[512,128]{1,0:T(8,128)(2,1)S(1)} %get-tuple-element.100.g0), channel_id=1, source_target_pairs={{0,8},{8,0},{16,24},{24,16},{1,9},{9,1},{17,25},{25,17},{2,10},{10... | collective-permute-start | bytes 393224 | tf_op jit(solution)/shard_map/ppermute | solution.py:25
  43.9 2.6 %shard_map.68 = (f32[4,24,2304]{2,1,0:T(8,128)S(1)}, bf16[4,24,2304]{2,1,0:T(8,128)(2,1)S(1)}) custom-call(s32[2]{0:T(128)S(1)} %pad_add_fusion.ids, bf16[1024,128]{1,0:T(8,128)(2,1)S(1)} %get-tuple-element.94.g0, bf16[1024,128]{1,0:T(8,128)(2,1)S(1)} %collective-permute-done.3.g1, bf16[1024,128]{1,0:T(8,128)(2,1)S(1)} %collective-permute-done.4.g2, ...), custom_call_target="tpu_custom_call" | custom-call | flops 29991000064 | tf_op jit(solution)/shard_map/pallas_call | solution.py:105
  47.4 3.8 %shard_map.69 = (bf16[512,128]{1,0:T(8,128)(2,1)S(1)}, bf16[512,128]{1,0:T(8,128)(2,1)S(1)}, f32[4,24,2304]{2,1,0:T(8,128)S(1)}, bf16[4,24,2304]{2,1,0:T(8,128)(2,1)S(1)}) custom-call(s32[2]{0:T(128)S(1)} %pad_add_fusion.ids, bf16[512,128]{1,0:T(8,128)(2,1)S(1)} %get-tuple-element.100.g0, bf16[512,128]{1,0:T(8,128)(2,1)S(1)} %collective-permute-done.12.g1, ...), custom_call_target="tpu_custom_call" | custom-call | flops 43832999936 | tf_op jit(solution)/shard_map/pallas_call | solution.py:105
  61.0 4.7 %shard_map.72 = (bf16[512,128]{1,0:T(8,128)(2,1)}, bf16[512,128]{1,0:T(8,128)(2,1)S(1)}, f32[4,24,2304]{2,1,0:T(8,128)S(1)}, bf16[4,24,2304]{2,1,0:T(8,128)(2,1)S(1)}) custom-call(s32[2]{0:T(128)S(1)} %pad_add_fusion.ids, bf16[512,128]{1,0:T(8,128)(2,1)S(1)} %get-tuple-element.116.g0, bf16[512,128]{1,0:T(8,128)(2,1)S(1)} %collective-permute-done.18.g1, ...), custom_call_target="tpu_custom_call" | custom-call | flops 43832999936 | tf_op jit(solution)/shard_map/pallas_call | solution.py:105
  71.4 2.2 %collective-permute-start.36 = (bf16[24,2304]{1,0:T(8,128)(2,1)S(1)}, bf16[24,2304]{1,0:T(8,128)(2,1)S(1)}, u32[]{:S(2)}, u32[]{:S(2)}) collective-permute-start(bf16[24,2304]{1,0:T(8,128)(2,1)S(1)} %get-tuple-element.143), channel_id=1, source_target_pairs={{0,4},{1,5},{2,6},{3,7},{4,0},{5,1},{6,2},{7,3},{8,12},{9,13},{10,... | collective-permute-start | bytes 331784 | tf_op jit(solution)/shard_map/ppermute | solution.py:25
  74.9 2.6 %shard_map.74 = (f32[4,24,2304]{2,1,0:T(8,128)S(1)}, bf16[4,24,2304]{2,1,0:T(8,128)(2,1)S(1)}) custom-call(s32[2]{0:T(128)S(1)} %pad_add_fusion.ids, bf16[512,128]{1,0:T(8,128)(2,1)S(1)} %get-tuple-element.129.g0, bf16[512,128]{1,0:T(8,128)(2,1)S(1)} %collective-permute-done.26.g1, bf16[512,128]{1,0:T(8,128)(2,1)S(1)} %collective-permute-done.27.g2, ...), custom_call_target="tpu_custom_call" | custom-call | flops 29991000064 | tf_op jit(solution)/shard_map/pallas_call | solution.py:105
  78.2 1.8 %collective-permute-start.38 = (bf16[24,2304]{1,0:T(8,128)(2,1)S(1)}, bf16[24,2304]{1,0:T(8,128)(2,1)S(1)}, u32[]{:S(2)}, u32[]{:S(2)}) collective-permute-start(bf16[24,2304]{1,0:T(8,128)(2,1)S(1)} %get-tuple-element.146), channel_id=1, source_target_pairs={{0,4},{1,5},{2,6},{3,7},{4,0},{5,1},{6,2},{7,3},{8,12},{9,13},{10,... | collective-permute-start | bytes 331784 | tf_op jit(solution)/shard_map/ppermute | solution.py:25
  81.7 3.2 %collective-permute-done.33.other = bf16[2,24,2304]{2,1,0:T(8,128)(2,1)S(1)} collective-permute-done((bf16[2,24,2304]{2,1,0:T(8,128)(2,1)S(1)}, bf16[2,24,2304]{2,1,0:T(8,128)(2,1)S(1)}, u32[]{:S(2)}, u32[]{:S(2)}) %collective-permute-start.33) | collective-permute-done | bytes 221216 | tf_op jit(solution)/shard_map/ppermute | solution.py:25
  85.6 6.4 %collective-permute-done.31.other = bf16[2,24,2304]{2,1,0:T(8,128)(2,1)S(1)} collective-permute-done((bf16[2,24,2304]{2,1,0:T(8,128)(2,1)S(1)}, bf16[2,24,2304]{2,1,0:T(8,128)(2,1)S(1)}, u32[]{:S(2)}, u32[]{:S(2)}) %collective-permute-start.31) | collective-permute-done | bytes 221216 | tf_op jit(solution)/shard_map/ppermute | solution.py:25
  93.5 6.5 %collective-permute-done.32.refs_1_ = bf16[24,2304]{1,0:T(8,128)(2,1)S(1)} collective-permute-done((bf16[24,2304]{1,0:T(8,128)(2,1)S(1)}, bf16[24,2304]{1,0:T(8,128)(2,1)S(1)}, u32[]{:S(2)}, u32[]{:S(2)}) %collective-permute-start.32) | collective-permute-done | bytes 110624 | tf_op jit(solution)/shard_map/ppermute | solution.py:25
  104.3 1.9 %collective-permute-done.39.f1 = bf16[24,2304]{1,0:T(8,128)(2,1)S(1)} collective-permute-done((bf16[24,2304]{1,0:T(8,128)(2,1)S(1)}, bf16[24,2304]{1,0:T(8,128)(2,1)S(1)}, u32[]{:S(2)}, u32[]{:S(2)}) %collective-permute-start.39) | collective-permute-done | bytes 110624 | tf_op jit(solution)/shard_map/ppermute | solution.py:25
  106.1 2.8 %collective-permute-done.40.f2 = bf16[24,2304]{1,0:T(8,128)(2,1)S(1)} collective-permute-done((bf16[24,2304]{1,0:T(8,128)(2,1)S(1)}, bf16[24,2304]{1,0:T(8,128)(2,1)S(1)}, u32[]{:S(2)}, u32[]{:S(2)}) %collective-permute-start.40) | collective-permute-done | bytes 110624 | tf_op jit(solution)/shard_map/ppermute | solution.py:25
  109.0 1.9 %shard_map.81 = f32[27,32,256]{2,1,0:T(8,128)} custom-call(s32[2]{0:T(128)S(1)} %pad_add_fusion.ids, bf16[24,2304]{1,0:T(8,128)(2,1)S(1)} %get-tuple-element.147.f0, bf16[24,2304]{1,0:T(8,128)(2,1)S(1)} %collective-permute-done.39.f1, bf16[24,2304]{1,0:T(8,128)(2,1)S(1)} %collective-permute-done.40.f2, bf16[24,2304]{1,0:T(8,128)(2,1)S(1)} %collective-permute-done.41.f3, ...), custom_call_target="tpu_custom_call" | custom-call | flops 23069999104 | tf_op jit(solution)/shard_map/pallas_call | solution.py:105
  (104 shorter events, 42.3 us)
Async XLA Ops:
  2.1 9.2 %collective-permute-start.6 = (bf16[24,2304]{1,0:T(8,128)(2,1)S(1)}, bf16[24,2304]{1,0:T(8,128)(2,1)S(1)}, u32[]{:S(2)}, u32[]{:S(2)}) collective-permute-start(bf16[24,2304]{1,0:T(8,128)(2,1)S(1)} %get-tuple-element.88), channel_id=1, source_target_pairs={{0,8},{8,0},{16,24},{24,16},{1,9},{9,1},{17,25},{25,17},{2,10},{10... | collective-permute-start | bytes 331784 | tf_op jit(solution)/shard_map/ppermute | solution.py:25
  7.8 8.4 %collective-permute-start = (bf16[512,128]{1,0:T(8,128)(2,1)S(1)}, bf16[512,128]{1,0:T(8,128)(2,1)S(1)}, u32[]{:S(2)}, u32[]{:S(2)}) collective-permute-start(bf16[512,128]{1,0:T(8,128)(2,1)S(1)} %get-tuple-element.80), channel_id=1, source_target_pairs={{0,8},{8,0},{16,24},{24,16},{1,9},{9,1},{17,25},{25,17},{2,10},{10... | collective-permute-start | bytes 393224 | tf_op jit(solution)/shard_map/ppermute | solution.py:25
  9.8 8.1 %collective-permute-start.1 = (bf16[512,128]{1,0:T(8,128)(2,1)S(1)}, bf16[512,128]{1,0:T(8,128)(2,1)S(1)}, u32[]{:S(2)}, u32[]{:S(2)}) collective-permute-start(bf16[512,128]{1,0:T(8,128)(2,1)S(1)} %get-tuple-element.81), channel_id=1, source_target_pairs={{0,16},{8,24},{16,0},{24,8},{1,17},{9,25},{17,1},{25,9},{2,18},{10... | collective-permute-start | bytes 393224 | tf_op jit(solution)/shard_map/ppermute | solution.py:25
  20.5 7.6 %collective-permute-start.15 = (bf16[24,2304]{1,0:T(8,128)(2,1)S(1)}, bf16[24,2304]{1,0:T(8,128)(2,1)S(1)}, u32[]{:S(2)}, u32[]{:S(2)}) collective-permute-start(bf16[24,2304]{1,0:T(8,128)(2,1)S(1)} %get-tuple-element.104), channel_id=1, source_target_pairs={{0,4},{1,5},{2,6},{3,7},{4,0},{5,1},{6,2},{7,3},{8,12},{9,13},{10,... | collective-permute-start | bytes 331784 | tf_op jit(solution)/shard_map/ppermute | solution.py:25
  22.0 11.3 %collective-permute-start.3 = (bf16[1024,128]{1,0:T(8,128)(2,1)S(1)}, bf16[1024,128]{1,0:T(8,128)(2,1)S(1)}, u32[]{:S(2)}, u32[]{:S(2)}) collective-permute-start(bf16[1024,128]{1,0:T(8,128)(2,1)S(1)} %get-tuple-element.84), channel_id=1, source_target_pairs={{0,8},{8,0},{16,24},{24,16},{1,9},{9,1},{17,25},{25,17},{2,10},{10... | collective-permute-start | bytes 786440 | tf_op jit(solution)/shard_map/ppermute | solution.py:25
  22.8 12.2 %collective-permute-start.4 = (bf16[1024,128]{1,0:T(8,128)(2,1)S(1)}, bf16[1024,128]{1,0:T(8,128)(2,1)S(1)}, u32[]{:S(2)}, u32[]{:S(2)}) collective-permute-start(bf16[1024,128]{1,0:T(8,128)(2,1)S(1)} %get-tuple-element.85), channel_id=1, source_target_pairs={{0,16},{8,24},{16,0},{24,8},{1,17},{9,25},{17,1},{25,9},{2,18},{10... | collective-permute-start | bytes 786440 | tf_op jit(solution)/shard_map/ppermute | solution.py:25
  23.7 11.3 %collective-permute-start.5 = (bf16[1024,128]{1,0:T(8,128)(2,1)S(1)}, bf16[1024,128]{1,0:T(8,128)(2,1)S(1)}, u32[]{:S(2)}, u32[]{:S(2)}) collective-permute-start(bf16[1024,128]{1,0:T(8,128)(2,1)S(1)} %get-tuple-element.86), channel_id=1, source_target_pairs={{0,24},{8,16},{16,8},{24,0},{1,25},{9,17},{17,9},{25,1},{2,26},{10... | collective-permute-start | bytes 786440 | tf_op jit(solution)/shard_map/ppermute | solution.py:25
  25.5 7.7 %collective-permute-start.10 = (bf16[2,24,2304]{2,1,0:T(8,128)(2,1)S(1)}, bf16[2,24,2304]{2,1,0:T(8,128)(2,1)S(1)}, u32[]{:S(2)}, u32[]{:S(2)}) collective-permute-start(bf16[2,24,2304]{2,1,0:T(8,128)(2,1)S(1)} %pad_maximum_fusion.6), channel_id=1, source_target_pairs={{0,2},{1,3},{2,0},{3,1},{4,6},{5,7},{6,4},{7,5},{8,10},{9,11},{10,... | collective-permute-start | bytes 663560 | tf_op jit(solution)/shard_map/ppermute | solution.py:25
  28.1 14.7 %collective-permute-start.16 = (bf16[2,24,2304]{2,1,0:T(8,128)(2,1)S(1)}, bf16[2,24,2304]{2,1,0:T(8,128)(2,1)S(1)}, u32[]{:S(2)}, u32[]{:S(2)}) collective-permute-start(bf16[2,24,2304]{2,1,0:T(8,128)(2,1)S(1)} %pad_maximum_fusion.7), channel_id=1, source_target_pairs={{0,2},{1,3},{2,0},{3,1},{4,6},{5,7},{6,4},{7,5},{8,10},{9,11},{10,... | collective-permute-start | bytes 663560 | tf_op jit(solution)/shard_map/ppermute | solution.py:25
  35.1 7.7 %collective-permute-start.23 = (bf16[24,2304]{1,0:T(8,128)(2,1)S(1)}, bf16[24,2304]{1,0:T(8,128)(2,1)S(1)}, u32[]{:S(2)}, u32[]{:S(2)}) collective-permute-start(bf16[24,2304]{1,0:T(8,128)(2,1)S(1)} %get-tuple-element.120), channel_id=1, source_target_pairs={{0,4},{1,5},{2,6},{3,7},{4,0},{5,1},{6,2},{7,3},{8,12},{9,13},{10,... | collective-permute-start | bytes 331784 | tf_op jit(solution)/shard_map/ppermute | solution.py:25
  42.8 12.1 %collective-permute-start.24 = (bf16[2,24,2304]{2,1,0:T(8,128)(2,1)S(1)}, bf16[2,24,2304]{2,1,0:T(8,128)(2,1)S(1)}, u32[]{:S(2)}, u32[]{:S(2)}) collective-permute-start(bf16[2,24,2304]{2,1,0:T(8,128)(2,1)S(1)} %pad_maximum_fusion.8), channel_id=1, source_target_pairs={{0,2},{1,3},{2,0},{3,1},{4,6},{5,7},{6,4},{7,5},{8,10},{9,11},{10,... | collective-permute-start | bytes 663560 | tf_op jit(solution)/shard_map/ppermute | solution.py:25
  51.3 7.7 %collective-permute-start.20 = (bf16[512,128]{1,0:T(8,128)(2,1)S(1)}, bf16[512,128]{1,0:T(8,128)(2,1)S(1)}, u32[]{:S(2)}, u32[]{:S(2)}) collective-permute-start(bf16[512,128]{1,0:T(8,128)(2,1)S(1)} %get-tuple-element.116.g0), channel_id=1, source_target_pairs={{0,24},{8,16},{16,8},{24,0},{1,25},{9,17},{17,9},{25,1},{2,26},{10... | collective-permute-start | bytes 393224 | tf_op jit(solution)/shard_map/ppermute | solution.py:25
  52.7 8.3 %collective-permute-start.19 = (bf16[512,128]{1,0:T(8,128)(2,1)S(1)}, bf16[512,128]{1,0:T(8,128)(2,1)S(1)}, u32[]{:S(2)}, u32[]{:S(2)}) collective-permute-start(bf16[512,128]{1,0:T(8,128)(2,1)S(1)} %get-tuple-element.116.g0), channel_id=1, source_target_pairs={{0,16},{8,24},{16,0},{24,8},{1,17},{9,25},{17,1},{25,9},{2,18},{10... | collective-permute-start | bytes 393224 | tf_op jit(solution)/shard_map/ppermute | solution.py:25
  53.7 7.3 %collective-permute-start.18 = (bf16[512,128]{1,0:T(8,128)(2,1)S(1)}, bf16[512,128]{1,0:T(8,128)(2,1)S(1)}, u32[]{:S(2)}, u32[]{:S(2)}) collective-permute-start(bf16[512,128]{1,0:T(8,128)(2,1)S(1)} %get-tuple-element.116.g0), channel_id=1, source_target_pairs={{0,8},{8,0},{16,24},{24,16},{1,9},{9,1},{17,25},{25,17},{2,10},{10... | collective-permute-start | bytes 393224 | tf_op jit(solution)/shard_map/ppermute | solution.py:25
  57.4 20.1 %collective-permute-start.37 = (bf16[2,24,2304]{2,1,0:T(8,128)(2,1)S(1)}, bf16[2,24,2304]{2,1,0:T(8,128)(2,1)S(1)}, u32[]{:S(2)}, u32[]{:S(2)}) collective-permute-start(bf16[2,24,2304]{2,1,0:T(8,128)(2,1)S(1)} %get-tuple-element.115), channel_id=1, source_target_pairs={{0,2},{1,3},{2,0},{3,1},{4,6},{5,7},{6,4},{7,5},{8,10},{9,11},{10,... | collective-permute-start | bytes 663560 | tf_op jit(solution)/shard_map/ppermute | solution.py:25
  59.1 10.6 %collective-permute-start.35 = (bf16[2,24,2304]{2,1,0:T(8,128)(2,1)S(1)}, bf16[2,24,2304]{2,1,0:T(8,128)(2,1)S(1)}, u32[]{:S(2)}, u32[]{:S(2)}) collective-permute-start(bf16[2,24,2304]{2,1,0:T(8,128)(2,1)S(1)} %get-tuple-element.111), channel_id=1, source_target_pairs={{0,2},{1,3},{2,0},{3,1},{4,6},{5,7},{6,4},{7,5},{8,10},{9,11},{10,... | collective-permute-start | bytes 663560 | tf_op jit(solution)/shard_map/ppermute | solution.py:25
  65.7 8.5 %collective-permute-start.28 = (bf16[512,128]{1,0:T(8,128)(2,1)S(1)}, bf16[512,128]{1,0:T(8,128)(2,1)S(1)}, u32[]{:S(2)}, u32[]{:S(2)}) collective-permute-start(bf16[512,128]{1,0:T(8,128)(2,1)S(1)} %get-tuple-element.129.g0), channel_id=1, source_target_pairs={{0,24},{8,16},{16,8},{24,0},{1,25},{9,17},{17,9},{25,1},{2,26},{10... | collective-permute-start | bytes 393224 | tf_op jit(solution)/shard_map/ppermute | solution.py:25
  67.0 7.9 %collective-permute-start.27 = (bf16[512,128]{1,0:T(8,128)(2,1)S(1)}, bf16[512,128]{1,0:T(8,128)(2,1)S(1)}, u32[]{:S(2)}, u32[]{:S(2)}) collective-permute-start(bf16[512,128]{1,0:T(8,128)(2,1)S(1)} %get-tuple-element.129.g0), channel_id=1, source_target_pairs={{0,16},{8,24},{16,0},{24,8},{1,17},{9,25},{17,1},{25,9},{2,18},{10... | collective-permute-start | bytes 393224 | tf_op jit(solution)/shard_map/ppermute | solution.py:25
  71.4 21.5 %collective-permute-start.36 = (bf16[24,2304]{1,0:T(8,128)(2,1)S(1)}, bf16[24,2304]{1,0:T(8,128)(2,1)S(1)}, u32[]{:S(2)}, u32[]{:S(2)}) collective-permute-start(bf16[24,2304]{1,0:T(8,128)(2,1)S(1)} %get-tuple-element.143), channel_id=1, source_target_pairs={{0,4},{1,5},{2,6},{3,7},{4,0},{5,1},{6,2},{7,3},{8,12},{9,13},{10,... | collective-permute-start | bytes 331784 | tf_op jit(solution)/shard_map/ppermute | solution.py:25
  74.2 10.7 %collective-permute-start.33 = (bf16[2,24,2304]{2,1,0:T(8,128)(2,1)S(1)}, bf16[2,24,2304]{2,1,0:T(8,128)(2,1)S(1)}, u32[]{:S(2)}, u32[]{:S(2)}) collective-permute-start(bf16[2,24,2304]{2,1,0:T(8,128)(2,1)S(1)} %get-tuple-element.128), channel_id=1, source_target_pairs={{0,2},{1,3},{2,0},{3,1},{4,6},{5,7},{6,4},{7,5},{8,10},{9,11},{10,... | collective-permute-start | bytes 663560 | tf_op jit(solution)/shard_map/ppermute | solution.py:25
  78.2 14.7 %collective-permute-start.38 = (bf16[24,2304]{1,0:T(8,128)(2,1)S(1)}, bf16[24,2304]{1,0:T(8,128)(2,1)S(1)}, u32[]{:S(2)}, u32[]{:S(2)}) collective-permute-start(bf16[24,2304]{1,0:T(8,128)(2,1)S(1)} %get-tuple-element.146), channel_id=1, source_target_pairs={{0,4},{1,5},{2,6},{3,7},{4,0},{5,1},{6,2},{7,3},{8,12},{9,13},{10,... | collective-permute-start | bytes 331784 | tf_op jit(solution)/shard_map/ppermute | solution.py:25
  80.6 11.4 %collective-permute-start.31 = (bf16[2,24,2304]{2,1,0:T(8,128)(2,1)S(1)}, bf16[2,24,2304]{2,1,0:T(8,128)(2,1)S(1)}, u32[]{:S(2)}, u32[]{:S(2)}) collective-permute-start(bf16[2,24,2304]{2,1,0:T(8,128)(2,1)S(1)} %get-tuple-element.136), channel_id=1, source_target_pairs={{0,2},{1,3},{2,0},{3,1},{4,6},{5,7},{6,4},{7,5},{8,10},{9,11},{10,... | collective-permute-start | bytes 663560 | tf_op jit(solution)/shard_map/ppermute | solution.py:25
  85.5 8.0 %collective-permute-start.34 = (bf16[24,2304]{1,0:T(8,128)(2,1)S(1)}, bf16[24,2304]{1,0:T(8,128)(2,1)S(1)}, u32[]{:S(2)}, u32[]{:S(2)}) collective-permute-start(bf16[24,2304]{1,0:T(8,128)(2,1)S(1)} %get-tuple-element.141), channel_id=1, source_target_pairs={{0,4},{1,5},{2,6},{3,7},{4,0},{5,1},{6,2},{7,3},{8,12},{9,13},{10,... | collective-permute-start | bytes 331784 | tf_op jit(solution)/shard_map/ppermute | solution.py:25
  92.6 7.4 %collective-permute-start.32 = (bf16[24,2304]{1,0:T(8,128)(2,1)S(1)}, bf16[24,2304]{1,0:T(8,128)(2,1)S(1)}, u32[]{:S(2)}, u32[]{:S(2)}) collective-permute-start(bf16[24,2304]{1,0:T(8,128)(2,1)S(1)} %get-tuple-element.138), channel_id=1, source_target_pairs={{0,4},{1,5},{2,6},{3,7},{4,0},{5,1},{6,2},{7,3},{8,12},{9,13},{10,... | collective-permute-start | bytes 331784 | tf_op jit(solution)/shard_map/ppermute | solution.py:25
  (24 other events, 130.2 us)
